TPU v7x, 128 devices: a whole 4x4x4 slice. The times are simulated.
128 devices in a mesh: grp: 8 (over z, core), dev: 16 (over y, x).
Axes of the slice: x: 4, y: 4, z: 4, core: 2. Of those that a mesh axis runs over, the one named last changes fastest.
Arguments:
- coarse_state: float32 [9, 128, 128, 128], P(None, 'grp', 'dev'), may hold values from -6 to 6
- coef_index: int32 [128, 128, 128], P('grp', 'dev'), may hold values from 0 to 7
- coef_table: float32 [8, 9], replicated, may hold values from 0.05 to 1
- patch_root: int32 [128, 3], replicated, may hold values from 0 to 112, as said below
- fine_index: int32 [128, 32, 1024], P(('grp', 'dev')), may hold values from 0 to 7
Outputs:
- coarse_new: float32 [9, 128, 128, 128], P(None, 'grp', 'dev')
- fine_state: float32 [128, 9, 32, 1024], P(('grp', 'dev'))
Inputs may be any that keep to these rules, and one draw needn't show every extreme that they name: `patch_root`: row i is patch number k = i % 1 of device (i % 16) // 1 of group i // 16. Its first coordinate lies from (i // 16) * 16 to (i // 16) * 16 + 16 - 16; with q = 128, its second lies from k * q + 1 to k * q + q - 17; its third from 1 to 111. Patches may intersect; their corrections add.
All inputs are finite; a program needn't handle non-finite values.
Results may differ from a plain program's by a relative error of at most 0.0003.
Values sent between devices are 32-bit elements; how exact they have to be, the bound alone decides.
No kernel may reach another device: no remote copies, remote signals or barrier semaphores. Data moves between devices by JAX's collectives and lax.ppermute only.
A program may use at most 192 MiB of HBM per device.

v0:
```python
import jax
import jax.numpy as jnp
from jax import lax
from jax.sharding import PartitionSpec as P

NSUB = 2


lam_coarse = 0.08
lam_fine = 0.16


def padded(cells, sides, width):
    for axis, dim in sides:
        count = lax.axis_size(axis)
        ends = count - 1
        head = lax.slice_in_dim(cells, 0, width, axis=dim)
        tail = lax.slice_in_dim(cells, cells.shape[dim] - width, cells.shape[dim], axis=dim)
        cells = jnp.concatenate(
            [
                lax.ppermute(tail, axis, [(i, (i + 1) % count) for i in range(ends)]),
                cells,
                lax.ppermute(head, axis, [((i + 1) % count, i) for i in range(ends)]),
            ],
            axis=dim,
        )
    return cells


def passed_along(array, axis, by):
    length = lax.axis_size(axis)
    pairs = [(i, i + by) for i in range(length) if 0 <= i + by < length]
    return lax.ppermute(array, axis, pairs)


def lookup(index_field, table):
    result = jnp.zeros((table.shape[1],) + index_field.shape, jnp.float32)
    ones_shape = (-1,) + (1,) * index_field.ndim
    for category in range(table.shape[0]):
        result = result + jnp.where(
            index_field[None] == category, table[category].reshape(ones_shape), jnp.float32(0.0)
        )
    return result


def coarse_step(field, diff):
    center = field[:, 1:-1, 1:-1, 1:-1]
    dcenter = diff[:, 1:-1, 1:-1, 1:-1]

    def term(nbr_u, nbr_d):
        return 0.5 * (dcenter + nbr_d) * (nbr_u - center)

    total = term(field[:, :-2, 1:-1, 1:-1], diff[:, :-2, 1:-1, 1:-1])
    total = total + term(field[:, 2:, 1:-1, 1:-1], diff[:, 2:, 1:-1, 1:-1])
    total = total + term(field[:, 1:-1, :-2, 1:-1], diff[:, 1:-1, :-2, 1:-1])
    total = total + term(field[:, 1:-1, 2:, 1:-1], diff[:, 1:-1, 2:, 1:-1])
    total = total + term(field[:, 1:-1, 1:-1, :-2], diff[:, 1:-1, 1:-1, :-2])
    total = total + term(field[:, 1:-1, 1:-1, 2:], diff[:, 1:-1, 1:-1, 2:])
    return center + lam_coarse * total


def upsample(block):
    return jnp.repeat(jnp.repeat(jnp.repeat(block, 2, 1), 2, 2), 2, 3)


def ghost_fill(coarse):
    return upsample(coarse)[:, 1:-1, 1:-1, 1:-1]


def prolong(coarse):
    side = coarse.shape[1] - 2
    inner = slice(1, side + 1)
    core = coarse[:, inner, inner, inner]
    slope_x = (coarse[:, 2:, inner, inner] - coarse[:, :-2, inner, inner]) * 0.125
    slope_y = (coarse[:, inner, 2:, inner] - coarse[:, inner, :-2, inner]) * 0.125
    slope_z = (coarse[:, inner, inner, 2:] - coarse[:, inner, inner, :-2]) * 0.125
    signs = jnp.tile(jnp.array([-1.0, 1.0], jnp.float32), side)
    interior = upsample(core) + signs.reshape((1, -1, 1, 1)) * upsample(slope_x)
    interior = interior + signs.reshape((1, 1, -1, 1)) * upsample(slope_y)
    interior = interior + signs.reshape((1, 1, 1, -1)) * upsample(slope_z)
    return ghost_fill(coarse).at[:, 1:-1, 1:-1, 1:-1].set(interior)


def coarsen_face(register):
    species, fine_n, _ = register.shape
    return register.reshape((species, fine_n // 2, 2, fine_n // 2, 2)).sum(axis=(2, 4))


def pad_inner(block):
    return jnp.pad(block, ((0, 0), (1, 1), (1, 1), (1, 1)))


def patch_work(foot_u, foot_d, fine_flat, table):
    side = foot_u.shape[1] - 2
    fine_n = 2 * side
    species = foot_u.shape[0]
    field = prolong(foot_u)
    shell = field - pad_inner(field[:, 1:-1, 1:-1, 1:-1])
    inner_d = lookup(fine_flat, table).reshape((species, fine_n, fine_n, fine_n))
    dext = ghost_fill(foot_d).at[:, 1:-1, 1:-1, 1:-1].set(inner_d)
    face_x = 0.5 * (dext[:, 1:, 1:-1, 1:-1] + dext[:, :-1, 1:-1, 1:-1])
    face_y = 0.5 * (dext[:, 1:-1, 1:, 1:-1] + dext[:, 1:-1, :-1, 1:-1])
    face_z = 0.5 * (dext[:, 1:-1, 1:-1, 1:] + dext[:, 1:-1, 1:-1, :-1])
    zero_face = jnp.zeros((species, fine_n, fine_n), jnp.float32)
    regs = [zero_face] * 6
    for substep in range(NSUB):
        core = field[:, 1:-1, 1:-1, 1:-1]
        flux_x = face_x * (field[:, 1:, 1:-1, 1:-1] - field[:, :-1, 1:-1, 1:-1])
        flux_y = face_y * (field[:, 1:-1, 1:, 1:-1] - field[:, 1:-1, :-1, 1:-1])
        flux_z = face_z * (field[:, 1:-1, 1:-1, 1:] - field[:, 1:-1, 1:-1, :-1])
        change = flux_x[:, 1:] - flux_x[:, :-1] + (flux_y[:, :, 1:] - flux_y[:, :, :-1])
        change = change + (flux_z[:, :, :, 1:] - flux_z[:, :, :, :-1])
        field = shell + pad_inner(core + lam_fine * change)
        regs = [
            regs[0] + flux_x[:, 0],
            regs[1] - flux_x[:, fine_n],
            regs[2] + flux_y[:, :, 0],
            regs[3] - flux_y[:, :, fine_n],
            regs[4] + flux_z[:, :, :, 0],
            regs[5] - flux_z[:, :, :, fine_n],
        ]
    inner = slice(1, side + 1)
    last = side + 1

    def face_flux(cycle_u, cycle_d, edge_u, edge_d):
        return lam_coarse * (0.5 * (cycle_d + edge_d)) * (edge_u - cycle_u)

    coarse_faces = [
        face_flux(
            foot_u[:, 0, inner, inner],
            foot_d[:, 0, inner, inner],
            foot_u[:, 1, inner, inner],
            foot_d[:, 1, inner, inner],
        ),
        face_flux(
            foot_u[:, last, inner, inner],
            foot_d[:, last, inner, inner],
            foot_u[:, side, inner, inner],
            foot_d[:, side, inner, inner],
        ),
        face_flux(
            foot_u[:, inner, 0, inner],
            foot_d[:, inner, 0, inner],
            foot_u[:, inner, 1, inner],
            foot_d[:, inner, 1, inner],
        ),
        face_flux(
            foot_u[:, inner, last, inner],
            foot_d[:, inner, last, inner],
            foot_u[:, inner, side, inner],
            foot_d[:, inner, side, inner],
        ),
        face_flux(
            foot_u[:, inner, inner, 0],
            foot_d[:, inner, inner, 0],
            foot_u[:, inner, inner, 1],
            foot_d[:, inner, inner, 1],
        ),
        face_flux(
            foot_u[:, inner, inner, last],
            foot_d[:, inner, inner, last],
            foot_u[:, inner, inner, side],
            foot_d[:, inner, inner, side],
        ),
    ]
    corrections = [
        lam_fine * 0.125 * coarsen_face(regs[number]) - coarse_faces[number] for number in range(6)
    ]
    interior = field[:, 1:-1, 1:-1, 1:-1]
    means = interior.reshape((species, side, 2, side, 2, side, 2)).sum(axis=(2, 4, 6)) * 0.125
    delta = jnp.zeros(foot_u.shape, jnp.float32)
    delta = delta.at[:, inner, inner, inner].set(means - coarse_step(foot_u, foot_d))
    delta = delta.at[:, 0, inner, inner].set(corrections[0])
    delta = delta.at[:, last, inner, inner].set(corrections[1])
    delta = delta.at[:, inner, 0, inner].set(corrections[2])
    delta = delta.at[:, inner, last, inner].set(corrections[3])
    delta = delta.at[:, inner, inner, 0].set(corrections[4])
    delta = delta.at[:, inner, inner, last].set(corrections[5])
    return (interior.reshape((species, fine_n, fine_n * fine_n)), delta)


def stripe_selector(roots, stripe_devs, height, width):
    patches = roots.shape[0]
    wanted = roots[:, 1][:, None] - 1 + jnp.arange(width, dtype=jnp.int32)[None, :]
    first_dev = jnp.arange(patches, dtype=jnp.int32) * stripe_devs
    rows_held = (
        first_dev[:, None, None] + jnp.arange(stripe_devs, dtype=jnp.int32)[None, :, None]
    ) * height
    rows_held = rows_held + jnp.arange(height, dtype=jnp.int32)[None, None, :]
    return (wanted[:, :, None, None] == rows_held[:, None]).astype(jnp.float32)


def place_windows(totals, windows, starts_x, starts_z):
    window_shape = windows.shape[1:]

    def put_one(number, acc):
        anchor = (jnp.int32(0), starts_x[number], jnp.int32(0), starts_z[number])
        current = lax.dynamic_slice(acc, anchor, window_shape)
        return lax.dynamic_update_slice(acc, current + windows[number], anchor)

    return lax.fori_loop(0, windows.shape[0], put_one, totals)


def body(coarse_state, coef_index, coef_table, patch_root, fine_index):
    species, cells_x, cells_y, cells_z = coarse_state.shape
    per_device = fine_index.shape[0]
    fine_n = fine_index.shape[1]
    side = fine_n // 2
    width = side + 2
    devices = lax.axis_size("dev")
    group = lax.axis_index("grp")
    member = lax.axis_index("dev")
    group_count = per_device * devices
    stripe_devs = devices // per_device
    classes = (coef_index + 1).astype(jnp.float32)
    stacked = jnp.concatenate([coarse_state, classes[None]], axis=0)
    rimmed = padded(stacked, (("grp", 1), ("dev", 2)), 1)
    rim_diff = lookup(rimmed[species] - 1.0, coef_table)
    padded_u = jnp.pad(rimmed[:species], ((0, 0), (0, 0), (0, 0), (1, 1)))
    padded_d = jnp.pad(rim_diff, ((0, 0), (0, 0), (0, 0), (1, 1)))
    coarse_one = coarse_step(padded_u, padded_d)
    group_rows = lax.dynamic_slice_in_dim(patch_root, group * group_count, group_count, 0)
    own_rows = lax.dynamic_slice_in_dim(group_rows, member * per_device, per_device, 0)
    my_stripe = member // stripe_devs
    targets = lax.dynamic_index_in_dim(
        group_rows.reshape((devices, per_device, 3)), my_stripe, 1, keepdims=False
    )
    low_row = member * cells_y
    touching = jnp.logical_and(
        targets[:, 1] - 1 <= low_row + cells_y - 1, targets[:, 1] + side >= low_row
    )
    touching = touching.astype(jnp.float32).reshape((devices, 1, 1, 1, 1))
    selector = stripe_selector(own_rows, stripe_devs, cells_y, width)
    slab_u = rimmed[:species, :, 1:-1, :]
    slab = jnp.concatenate([slab_u, rim_diff[:, :, 1:-1, :]], axis=0)
    channels = slab.shape[0]

    def cut_one(root):
        anchor = (jnp.int32(0), root[0] - group * cells_x, jnp.int32(0), root[2] - 1)
        return lax.dynamic_slice(slab, anchor, (channels, width, cells_y, width))

    windows = jax.vmap(cut_one)(targets) * touching
    received = lax.all_to_all(windows, "dev", split_axis=0, concat_axis=0, tiled=True)
    parts = received.reshape((per_device, stripe_devs) + received.shape[1:])
    footprints = jnp.einsum("krtc,ktaxcz->kaxrz", selector, parts, precision=lax.Precision.HIGHEST)
    foot_u = footprints[:, :species]
    foot_d = footprints[:, species:]
    interiors, deltas = jax.vmap(
        lambda one_u, one_d, idx: patch_work(one_u, one_d, idx, coef_table)
    )(foot_u, foot_d, fine_index)
    outgoing = jnp.einsum("krtc,ksxrz->ktsxcz", selector, deltas, precision=lax.Precision.HIGHEST)
    outgoing = outgoing.reshape((devices,) + outgoing.shape[2:])
    arrived = lax.all_to_all(outgoing, "dev", split_axis=0, concat_axis=0, tiled=True)
    totals = jnp.zeros((species, cells_x + 2, cells_y, cells_z), jnp.float32)
    totals = place_windows(totals, arrived, targets[:, 0] - group * cells_x, targets[:, 2] - 1)
    from_above = passed_along(totals[:, 0], "grp", -1)
    from_below = passed_along(totals[:, cells_x + 1], "grp", 1)
    totals = totals.at[:, cells_x].add(from_above)
    totals = totals.at[:, 1].add(from_below)
    coarse_new = coarse_one + totals[:, 1 : cells_x + 1]
    return (coarse_new, interiors)


def solution(mesh):
    return jax.shard_map(
        body,
        mesh=mesh,
        in_specs=(
            P(None, "grp", "dev", None),
            P("grp", "dev", None),
            P(),
            P(),
            P(("grp", "dev"), None, None),
        ),
        out_specs=(P(None, "grp", "dev", None), P(("grp", "dev"), None, None, None)),
        check_vma=False,
    )
```

profile of v0, /device:TPU:32, one launch (start us, length us, event | category | flops | bytes accessed | tf_op | source)
XLA Modules:
  0.0 1588.4 jit_solution(5632275114454045922)
XLA Ops:
  25.2 11.6 copy.1088
  36.9 20.8 %gather_fusion = f32[16,18,18,8,18]{2,1,3,4,0:T(8,128)} fusion(f32[18,18,8,128]{1,0,2,3:T(8,128)} %copy.1088, s32[16]{0:T(128)S(1)} %get-tuple-element.333), kind=kCustom, calls=%fused_computation | custom fusion | bytes 5972224 | tf_op jit(solution)/shard_map/vmap()/gather | solution.py:240
  57.7 27.0 %copy.1089 = f32[16,18,18,8,18]{4,3,2,1,0:T(8,128)} copy(f32[16,18,18,8,18]{2,1,3,4,0:T(8,128)} %gather_fusion) | data formatting | bytes 5971968 | tf_op jit(solution)/shard_map/vmap()/gather | solution.py:240
  84.6 15.3 broadcast_multiply_fusion
  99.9 22.4 %reshape.1410 = f32[16,1,46656]{2,1,0:T(1,128)} reshape(f32[16,18,18,8,18]{4,3,2,1,0:T(8,128)} %broadcast_multiply_fusion) | data formatting | bytes 5971968
  122.4 9.2 all-to-all-start
  146.6 23.8 %all-to-all-done = f32[16,1,46656]{2,1,0:T(1,128)S(1)} async-done(((f32[16,1,46656]{2,1,0:T(1,128)}), f32[16,1,46656]{2,1,0:T(1,128)S(1)}, u32[]{:S(2)}, u32[]{:S(2)}) %all-to-all-start) | async-done | bytes 2986016 | tf_op jit(solution)/shard_map/all_to_all | solution.py:243
  170.8 10.3 reduce.35
  181.1 35.6 %reshape.1411 = f32[16,18,18,8,18]{4,3,2,1,0:T(8,128)} reshape(f32[16,46656]{1,0:T(8,128)} %reduce.35) | data formatting | bytes 5971968
  216.7 20.1 %fusion = f32[18,18,18,18,1]{3,2,0,1,4:T(8,128)S(1)} fusion(f32[16,18,18,8,18]{4,3,2,1,0:T(8,128)} %reshape.1411, pred[18,16,8,1,1]{0,1,2,4,3:T(8,128)(4,1)S(1)} %compare_bitcast_fusion), kind=kOutput, calls=%fused_computation.2 | convolution fusion | flops 161243136 | bytes 3408192 | tf_op jit(solution)/shard_map/krtc,ktaxcz->kaxrz/dot_general | solution.py:245
  255.1 6.6 copy.1101
  274.1 6.6 copy.1102
  293.1 6.5 copy.1106
  310.0 6.9 copy.1110
  347.7 8.4 copy.1184
  387.1 8.4 copy.1185
  395.5 11.1 multiply_add_fusion
  406.6 110.5 %scatter.30 = f32[1,9,34,34,34]{4,3,2,1,0:T(8,128)} dynamic-update-slice(f32[1,9,34,34,34]{4,3,2,1,0:T(8,128)} %copy.1184, f32[1,9,32,32,32]{4,3,2,1,0:T(8,128)} %multiply_add_fusion, s32[]{:T(128)} %constant.468.clone.1, s32[]{:T(128)} %constant.468.clone.1, s32[]{:T(128)} %constant.456.clone.1, s32[]{:T(128)} %constant.456.clone.1, s32[]{:T(128)} %constant.456.clone.1) | dynamic-update-slice | bytes 2359300 | tf_op jit(solution)/shard_map/vmap()/scatter | solution.py:81
  517.1 110.7 %scatter.31 = f32[1,9,34,34,34]{4,3,2,1,0:T(8,128)} dynamic-update-slice(f32[1,9,34,34,34]{4,3,2,1,0:T(8,128)} %copy.1185, f32[1,9,32,32,32]{4,3,2,1,0:T(8,128)} %select_add_fusion, s32[]{:T(128)} %constant.468.clone.1, s32[]{:T(128)} %constant.468.clone.1, s32[]{:T(128)} %constant.456.clone.1, s32[]{:T(128)} %constant.456.clone.1, s32[]{:T(128)} %constant.456.clone.1) | dynamic-update-slice | bytes 2359300 | tf_op jit(solution)/shard_map/vmap()/scatter | solution.py:100
  627.8 15.4 fusion.6
  643.2 12.6 fusion.3
  655.8 6.1 fusion.16
  664.1 8.8 fusion.15
  672.9 13.1 pad_add_fusion
  686.0 11.5 fusion.11
  697.5 11.0 fusion.2
  708.5 15.2 fusion.5
  723.6 10.7 slice_subtract_fusion.4
  734.3 7.8 copy.1141
  746.6 8.0 copy.1146
  757.2 15.2 fusion.10
  785.0 7.6 pad_add_fusion.1
  792.7 11.5 copy.1115
  804.2 12.8 reduce_sum.63
  818.9 11.1 fusion.33
  840.9 7.9 scatter.39
  848.8 29.3 %scatter.40 = f32[9,18,18,18]{2,3,1,0:T(8,128)S(1)} dynamic-update-slice(f32[9,18,18,18]{2,3,1,0:T(8,128)S(1)} %scatter.39, f32[9,16,1,16]{2,3,1,0:T(8,128)S(1)} %get-tuple-element.281, s32[]{:T(128)} %constant.468.clone.1, s32[]{:T(128)} %constant.456.clone.1, s32[]{:T(128)} %constant.491.clone.1, s32[]{:T(128)} %constant.456.clone.1) | dynamic-update-slice | bytes 18436 | tf_op jit(solution)/shard_map/vmap()/scatter | solution.py:176
  878.1 25.4 %scatter.41 = f32[9,18,18,18]{2,3,1,0:T(8,128)S(1)} dynamic-update-slice(f32[9,18,18,18]{2,3,1,0:T(8,128)S(1)} %scatter.40, f32[9,16,16,1]{2,3,1,0:T(1,128)S(1)} %get-tuple-element.280, s32[]{:T(128)} %constant.468.clone.1, s32[]{:T(128)} %constant.456.clone.1, s32[]{:T(128)} %constant.456.clone.1, s32[]{:T(128)} %constant.468.clone.1) | dynamic-update-slice | bytes 18436 | tf_op jit(solution)/shard_map/vmap()/scatter | solution.py:177
  903.5 25.6 %scatter.44 = f32[9,18,18,18]{2,3,1,0:T(8,128)S(1)} dynamic-update-slice(f32[9,18,18,18]{2,3,1,0:T(8,128)S(1)} %scatter.41, f32[9,16,16,1]{2,3,1,0:T(1,128)S(1)} %copy-done.21, s32[]{:T(128)} %constant.468.clone.1, s32[]{:T(128)} %constant.456.clone.1, s32[]{:T(128)} %constant.456.clone.1, s32[]{:T(128)} %constant.491.clone.1) | dynamic-update-slice | bytes 18436 | tf_op jit(solution)/shard_map/vmap()/scatter | solution.py:178
  934.4 7.3 copy.1151
  941.7 11.3 reshape.1412
  957.9 21.5 %all-to-all-done.1 = f32[16,1,23328]{2,1,0:T(1,128)S(1)} async-done(((f32[16,1,23328]{2,1,0:T(1,128)}), f32[16,1,23328]{2,1,0:T(1,128)S(1)}, u32[]{:S(2)}, u32[]{:S(2)}) %all-to-all-start.1) | async-done | bytes 1493024 | tf_op jit(solution)/shard_map/all_to_all | solution.py:253
  979.5 5.9 reduce.36
  985.4 13.4 reshape.1413
  998.8 556.7 %while.24 = (s32[]{:T(128)}, f32[9,18,8,128]{3,2,1,0:T(8,128)S(1)}, s32[16]{0:T(128)S(1)}, f32[16,9,18,8,18]{4,3,2,1,0:T(8,128)}, s32[]{:T(128)}, /*index=5*/s32[]{:T(128)}, s32[]{:T(128)}) while((s32[]{:T(128)}, f32[9,18,8,128]{3,2,1,0:T(8,128)S(1)}, s32[16]{0:T(128)S(1)}, f32[16,9,18,8,18]{4,3,2,1,0:T(8,128)}, s32[]{:T(128)}, ...), condition=%wide.region_8.9_spmd, body=%wide.region_7.8_spmd.sunk | while | flops 23333 | bytes 466695 | solution.py:201
  1002.6 31.0 %dynamic_update_slice.9 = f32[9,18,8,128]{3,2,1,0:T(8,128)S(1)} dynamic-update-slice(f32[9,18,8,128]{3,2,1,0:T(8,128)S(1)} %get-tuple-element.376, f32[9,18,8,18]{3,2,1,0:T(8,128)S(1)} %bitcast_add_fusion.3, s32[]{:T(128)} %constant.468.clone.1..sunk, s32[]{:T(128)} %constant.468.clone.1..sunk, s32[]{:T(128)} %constant.468.clone.1..sunk, s32[]{:T(128)S(6)} %select_n.219) | dynamic-update-slice | bytes 186628 | tf_op jit(solution)/shard_map/while/body/eval_jaxpr/dynamic_update_slice | solution.py:199
  1037.4 31.0 %dynamic_update_slice.9 = f32[9,18,8,128]{3,2,1,0:T(8,128)S(1)} dynamic-update-slice(f32[9,18,8,128]{3,2,1,0:T(8,128)S(1)} %get-tuple-element.376, f32[9,18,8,18]{3,2,1,0:T(8,128)S(1)} %bitcast_add_fusion.3, s32[]{:T(128)} %constant.468.clone.1..sunk, s32[]{:T(128)} %constant.468.clone.1..sunk, s32[]{:T(128)} %constant.468.clone.1..sunk, s32[]{:T(128)S(6)} %select_n.219) | dynamic-update-slice | bytes 186628 | tf_op jit(solution)/shard_map/while/body/eval_jaxpr/dynamic_update_slice | solution.py:199
  1072.2 31.0 %dynamic_update_slice.9 = f32[9,18,8,128]{3,2,1,0:T(8,128)S(1)} dynamic-update-slice(f32[9,18,8,128]{3,2,1,0:T(8,128)S(1)} %get-tuple-element.376, f32[9,18,8,18]{3,2,1,0:T(8,128)S(1)} %bitcast_add_fusion.3, s32[]{:T(128)} %constant.468.clone.1..sunk, s32[]{:T(128)} %constant.468.clone.1..sunk, s32[]{:T(128)} %constant.468.clone.1..sunk, s32[]{:T(128)S(6)} %select_n.219) | dynamic-update-slice | bytes 186628 | tf_op jit(solution)/shard_map/while/body/eval_jaxpr/dynamic_update_slice | solution.py:199
  1107.0 31.0 %dynamic_update_slice.9 = f32[9,18,8,128]{3,2,1,0:T(8,128)S(1)} dynamic-update-slice(f32[9,18,8,128]{3,2,1,0:T(8,128)S(1)} %get-tuple-element.376, f32[9,18,8,18]{3,2,1,0:T(8,128)S(1)} %bitcast_add_fusion.3, s32[]{:T(128)} %constant.468.clone.1..sunk, s32[]{:T(128)} %constant.468.clone.1..sunk, s32[]{:T(128)} %constant.468.clone.1..sunk, s32[]{:T(128)S(6)} %select_n.219) | dynamic-update-slice | bytes 186628 | tf_op jit(solution)/shard_map/while/body/eval_jaxpr/dynamic_update_slice | solution.py:199
  1141.8 31.0 %dynamic_update_slice.9 = f32[9,18,8,128]{3,2,1,0:T(8,128)S(1)} dynamic-update-slice(f32[9,18,8,128]{3,2,1,0:T(8,128)S(1)} %get-tuple-element.376, f32[9,18,8,18]{3,2,1,0:T(8,128)S(1)} %bitcast_add_fusion.3, s32[]{:T(128)} %constant.468.clone.1..sunk, s32[]{:T(128)} %constant.468.clone.1..sunk, s32[]{:T(128)} %constant.468.clone.1..sunk, s32[]{:T(128)S(6)} %select_n.219) | dynamic-update-slice | bytes 186628 | tf_op jit(solution)/shard_map/while/body/eval_jaxpr/dynamic_update_slice | solution.py:199
  1176.6 31.0 %dynamic_update_slice.9 = f32[9,18,8,128]{3,2,1,0:T(8,128)S(1)} dynamic-update-slice(f32[9,18,8,128]{3,2,1,0:T(8,128)S(1)} %get-tuple-element.376, f32[9,18,8,18]{3,2,1,0:T(8,128)S(1)} %bitcast_add_fusion.3, s32[]{:T(128)} %constant.468.clone.1..sunk, s32[]{:T(128)} %constant.468.clone.1..sunk, s32[]{:T(128)} %constant.468.clone.1..sunk, s32[]{:T(128)S(6)} %select_n.219) | dynamic-update-slice | bytes 186628 | tf_op jit(solution)/shard_map/while/body/eval_jaxpr/dynamic_update_slice | solution.py:199
  1211.4 31.0 %dynamic_update_slice.9 = f32[9,18,8,128]{3,2,1,0:T(8,128)S(1)} dynamic-update-slice(f32[9,18,8,128]{3,2,1,0:T(8,128)S(1)} %get-tuple-element.376, f32[9,18,8,18]{3,2,1,0:T(8,128)S(1)} %bitcast_add_fusion.3, s32[]{:T(128)} %constant.468.clone.1..sunk, s32[]{:T(128)} %constant.468.clone.1..sunk, s32[]{:T(128)} %constant.468.clone.1..sunk, s32[]{:T(128)S(6)} %select_n.219) | dynamic-update-slice | bytes 186628 | tf_op jit(solution)/shard_map/while/body/eval_jaxpr/dynamic_update_slice | solution.py:199
  1246.2 31.0 %dynamic_update_slice.9 = f32[9,18,8,128]{3,2,1,0:T(8,128)S(1)} dynamic-update-slice(f32[9,18,8,128]{3,2,1,0:T(8,128)S(1)} %get-tuple-element.376, f32[9,18,8,18]{3,2,1,0:T(8,128)S(1)} %bitcast_add_fusion.3, s32[]{:T(128)} %constant.468.clone.1..sunk, s32[]{:T(128)} %constant.468.clone.1..sunk, s32[]{:T(128)} %constant.468.clone.1..sunk, s32[]{:T(128)S(6)} %select_n.219) | dynamic-update-slice | bytes 186628 | tf_op jit(solution)/shard_map/while/body/eval_jaxpr/dynamic_update_slice | solution.py:199
  1281.0 31.0 %dynamic_update_slice.9 = f32[9,18,8,128]{3,2,1,0:T(8,128)S(1)} dynamic-update-slice(f32[9,18,8,128]{3,2,1,0:T(8,128)S(1)} %get-tuple-element.376, f32[9,18,8,18]{3,2,1,0:T(8,128)S(1)} %bitcast_add_fusion.3, s32[]{:T(128)} %constant.468.clone.1..sunk, s32[]{:T(128)} %constant.468.clone.1..sunk, s32[]{:T(128)} %constant.468.clone.1..sunk, s32[]{:T(128)S(6)} %select_n.219) | dynamic-update-slice | bytes 186628 | tf_op jit(solution)/shard_map/while/body/eval_jaxpr/dynamic_update_slice | solution.py:199
  1315.8 31.0 %dynamic_update_slice.9 = f32[9,18,8,128]{3,2,1,0:T(8,128)S(1)} dynamic-update-slice(f32[9,18,8,128]{3,2,1,0:T(8,128)S(1)} %get-tuple-element.376, f32[9,18,8,18]{3,2,1,0:T(8,128)S(1)} %bitcast_add_fusion.3, s32[]{:T(128)} %constant.468.clone.1..sunk, s32[]{:T(128)} %constant.468.clone.1..sunk, s32[]{:T(128)} %constant.468.clone.1..sunk, s32[]{:T(128)S(6)} %select_n.219) | dynamic-update-slice | bytes 186628 | tf_op jit(solution)/shard_map/while/body/eval_jaxpr/dynamic_update_slice | solution.py:199
  1350.6 31.0 %dynamic_update_slice.9 = f32[9,18,8,128]{3,2,1,0:T(8,128)S(1)} dynamic-update-slice(f32[9,18,8,128]{3,2,1,0:T(8,128)S(1)} %get-tuple-element.376, f32[9,18,8,18]{3,2,1,0:T(8,128)S(1)} %bitcast_add_fusion.3, s32[]{:T(128)} %constant.468.clone.1..sunk, s32[]{:T(128)} %constant.468.clone.1..sunk, s32[]{:T(128)} %constant.468.clone.1..sunk, s32[]{:T(128)S(6)} %select_n.219) | dynamic-update-slice | bytes 186628 | tf_op jit(solution)/shard_map/while/body/eval_jaxpr/dynamic_update_slice | solution.py:199
  1385.4 31.0 %dynamic_update_slice.9 = f32[9,18,8,128]{3,2,1,0:T(8,128)S(1)} dynamic-update-slice(f32[9,18,8,128]{3,2,1,0:T(8,128)S(1)} %get-tuple-element.376, f32[9,18,8,18]{3,2,1,0:T(8,128)S(1)} %bitcast_add_fusion.3, s32[]{:T(128)} %constant.468.clone.1..sunk, s32[]{:T(128)} %constant.468.clone.1..sunk, s32[]{:T(128)} %constant.468.clone.1..sunk, s32[]{:T(128)S(6)} %select_n.219) | dynamic-update-slice | bytes 186628 | tf_op jit(solution)/shard_map/while/body/eval_jaxpr/dynamic_update_slice | solution.py:199
  1420.2 31.0 %dynamic_update_slice.9 = f32[9,18,8,128]{3,2,1,0:T(8,128)S(1)} dynamic-update-slice(f32[9,18,8,128]{3,2,1,0:T(8,128)S(1)} %get-tuple-element.376, f32[9,18,8,18]{3,2,1,0:T(8,128)S(1)} %bitcast_add_fusion.3, s32[]{:T(128)} %constant.468.clone.1..sunk, s32[]{:T(128)} %constant.468.clone.1..sunk, s32[]{:T(128)} %constant.468.clone.1..sunk, s32[]{:T(128)S(6)} %select_n.219) | dynamic-update-slice | bytes 186628 | tf_op jit(solution)/shard_map/while/body/eval_jaxpr/dynamic_update_slice | solution.py:199
  1455.0 31.0 %dynamic_update_slice.9 = f32[9,18,8,128]{3,2,1,0:T(8,128)S(1)} dynamic-update-slice(f32[9,18,8,128]{3,2,1,0:T(8,128)S(1)} %get-tuple-element.376, f32[9,18,8,18]{3,2,1,0:T(8,128)S(1)} %bitcast_add_fusion.3, s32[]{:T(128)} %constant.468.clone.1..sunk, s32[]{:T(128)} %constant.468.clone.1..sunk, s32[]{:T(128)} %constant.468.clone.1..sunk, s32[]{:T(128)S(6)} %select_n.219) | dynamic-update-slice | bytes 186628 | tf_op jit(solution)/shard_map/while/body/eval_jaxpr/dynamic_update_slice | solution.py:199
  1489.8 31.0 %dynamic_update_slice.9 = f32[9,18,8,128]{3,2,1,0:T(8,128)S(1)} dynamic-update-slice(f32[9,18,8,128]{3,2,1,0:T(8,128)S(1)} %get-tuple-element.376, f32[9,18,8,18]{3,2,1,0:T(8,128)S(1)} %bitcast_add_fusion.3, s32[]{:T(128)} %constant.468.clone.1..sunk, s32[]{:T(128)} %constant.468.clone.1..sunk, s32[]{:T(128)} %constant.468.clone.1..sunk, s32[]{:T(128)S(6)} %select_n.219) | dynamic-update-slice | bytes 186628 | tf_op jit(solution)/shard_map/while/body/eval_jaxpr/dynamic_update_slice | solution.py:199
  1524.6 31.0 %dynamic_update_slice.9 = f32[9,18,8,128]{3,2,1,0:T(8,128)S(1)} dynamic-update-slice(f32[9,18,8,128]{3,2,1,0:T(8,128)S(1)} %get-tuple-element.376, f32[9,18,8,18]{3,2,1,0:T(8,128)S(1)} %bitcast_add_fusion.3, s32[]{:T(128)} %constant.468.clone.1..sunk, s32[]{:T(128)} %constant.468.clone.1..sunk, s32[]{:T(128)} %constant.468.clone.1..sunk, s32[]{:T(128)S(6)} %select_n.219) | dynamic-update-slice | bytes 186628 | tf_op jit(solution)/shard_map/while/body/eval_jaxpr/dynamic_update_slice | solution.py:199
  1555.6 9.9 collective-permute-start.4
  1567.7 5.4 reshape.1398
  1578.7 8.4 fusion.48
  (261 shorter events, 238.3 us)
Async XLA Ops:
  0.6 8.3 copy-start
  1.5 21.4 %copy-start.17 = (f32[1,16,8,128]{3,2,1,0:T(8,128)}, f32[1,16,8,128]{3,2,1,0:T(8,128)S(1)}, u32[]{:S(2)}) copy-start(f32[1,16,8,128]{3,2,1,0:T(8,128)S(1)} %convert_bitcast_fusion) | copy-start | bytes 196612
  2.3 7.3 collective-permute-start
  4.2 5.4 collective-permute-start.1
  8.9 14.2 copy-start.29
  8.9 14.2 copy-start.30
  8.9 14.2 copy-start.31
  8.9 14.2 copy-start.32
  8.9 14.2 copy-start.33
  8.9 14.2 copy-start.34
  8.9 14.2 copy-start.35
  8.9 14.2 copy-start.36
  9.6 13.3 copy-start.22
  9.6 13.3 copy-start.24
  10.9 5.5 collective-permute-start.2
  14.4 6.8 collective-permute-start.3
  21.9 1.3 copy-start.16
  24.0 1.1 copy-start.7
  122.4 9.8 copy-start.40
  122.4 9.9 copy-start.26
  122.4 47.9 %all-to-all-start = ((f32[16,1,46656]{2,1,0:T(1,128)}), f32[16,1,46656]{2,1,0:T(1,128)S(1)}, u32[]{:S(2)}, u32[]{:S(2)}) async-start(f32[16,1,46656]{2,1,0:T(1,128)} %reshape.1410), calls=%async_computation | async-start | bytes 5980160 | tf_op jit(solution)/shard_map/all_to_all | solution.py:243
  141.1 40.0 %copy-start.37 = (s32[18]{0:T(128)}, s32[18]{0:T(128)S(1)}, u32[]{:S(2)}) copy-start(s32[18]{0:T(128)S(1)} %iota_add_fusion.1) | copy-start | bytes 220
  141.1 40.0 %copy-start.27 = (s32[16,8]{0,1:T(8,128)}, s32[16,8]{0,1:T(8,128)S(1)}, u32[]{:S(2)}) copy-start(s32[16,8]{0,1:T(8,128)S(1)} %iota_add_fusion) | copy-start | bytes 1540
  237.1 3.3 copy-start.2
  255.1 6.6 copy-start.14
  274.1 6.6 copy-start.13
  627.8 28.0 %slice-start = ((s8[6266880]{0:T(1024)(128)(4,1)}), s8[2072576]{0:T(1024)(128)(4,1)S(1)}, s32[]{:S(2)}) async-start(s8[6266880]{0:T(1024)(128)(4,1)} %bitcast.210), calls=%async_computation.2 | async-start | bytes 4145152
  643.2 12.6 slice-start.1
  655.8 8.3 copy-start.6
  661.9 2.2 copy-start.5
  686.0 11.5 copy-start.4
  818.9 11.7 copy-start.3
  830.0 1.3 copy-start.11
  830.0 1.6 copy-start.12
  834.5 69.0 %copy-start.21 = (f32[9,16,16,1]{2,3,1,0:T(1,128)S(1)}, f32[9,16,16,1]{2,3,1,0:T(1,128)}, u32[]{:S(2)}) copy-start(f32[9,16,16,1]{2,3,1,0:T(1,128)} %copy.1149) | copy-start | bytes 27652
  834.5 94.6 %copy-start.28 = (s32[16,8]{0,1:T(8,128)S(1)}, s32[16,8]{0,1:T(8,128)}, u32[]{:S(2)}) copy-start(s32[16,8]{0,1:T(8,128)} %copy-done.27) | copy-start | bytes 1540
  834.5 94.6 %copy-start.38 = (s32[18]{0:T(128)S(1)}, s32[18]{0:T(128)}, u32[]{:S(2)}) copy-start(s32[18]{0:T(128)} %copy-done.37) | copy-start | bytes 220
  941.7 15.1 copy-start.9
  941.7 15.1 copy-start.18
  941.7 15.1 copy-start.23
  941.7 15.1 copy-start.25
  953.0 26.5 %all-to-all-start.1 = ((f32[16,1,23328]{2,1,0:T(1,128)}), f32[16,1,23328]{2,1,0:T(1,128)S(1)}, u32[]{:S(2)}, u32[]{:S(2)}) async-start(f32[16,1,23328]{2,1,0:T(1,128)} %reshape.1412), calls=%async_computation.1 | async-start | bytes 2998272 | tf_op jit(solution)/shard_map/all_to_all | solution.py:253
  985.4 13.4 copy-start.39
  998.8 566.7 %copy-start.8 = (f32[9,18,10,128]{3,2,1,0:T(8,128)S(1)}, f32[9,18,10,128]{3,2,1,0:T(8,128)}, u32[]{:S(2)}) copy-start(f32[9,18,10,128]{3,2,1,0:T(8,128)} %copy-done.7) | copy-start | bytes 2488324
  1555.6 19.7 %collective-permute-start.4 = (f32[9,8,128]{2,1,0:T(8,128)S(1)}, f32[9,8,128]{2,1,0:T(8,128)S(1)}, u32[]{:S(2)}, u32[]{:S(2)}) collective-permute-start(f32[9,8,128]{2,1,0:T(8,128)S(1)} %get-tuple-element.308), channel_id=1, source_target_pairs={{16,0},{32,16},{48,32},{64,48},{80,64},{96,80},{112,96},{17,1},{33... | collective-permute-start | bytes 110600 | tf_op jit(solution)/shard_map/ppermute | solution.py:33
  1567.7 11.0 copy-start.10
  1567.7 11.0 copy-start.15
  1567.7 11.0 copy-start.19
  1567.7 11.1 copy-start.20
  1573.4 5.3 collective-permute-start.5
  1578.7 9.4 copy-start.1
where the time goes:
time: 1600 us; the launch traced here: 1590 us
  local copies, waits for them, and re-layouts  1190 us (74%)
  other arithmetic  257 us (16%)
  waiting for transfers between devices  52.2 us (3%)
  starting transfers between devices  35 us (2%)
  loops' own time  30.6 us (2%)
  matrix products  25.3 us (2%)
    dynamic_update_slice x16, local copies, waits for them, and re-layouts, put_one(): return lax.dynamic_update_slice(acc, current + windows[number], anchor)  495 us
    broadcast_in_dim x38, local copies, waits for them, and re-layouts, upsample(): return jnp.repeat(jnp.repeat(jnp.repeat(block, 2, 1), 2, 2), 2, 3)  115 us
    scatter x1, local copies, waits for them, and re-layouts, patch_work(): dext = ghost_fill(foot_d).at[:, 1:-1, 1:-1, 1:-1].set(inner_d)  111 us
    scatter x1, local copies, waits for them, and re-layouts, prolong(): return ghost_fill(coarse).at[:, 1:-1, 1:-1, 1:-1].set(interior)  110 us
    unnamed x93, local copies, waits for them, and re-layouts  105 us
    gather x2, local copies, waits for them, and re-layouts, cut_one(): return lax.dynamic_slice(slab, anchor, (channels, width, cells_y, width))  47.8 us
    add x4, other arithmetic, patch_work(): field = shell + pad_inner(core + lam_fine * change)  44.8 us
  transfers between devices with their start and end apart: 8, of which 5 were waited for; matrix products, arithmetic and copies ran while one was open for 2% of the time, Pallas kernels for 0%

commit v1 on v0

v1 whole, which is shorter than its diff:
```python
import jax
import jax.numpy as jnp
import ml_dtypes
import numpy as np
from jax import lax
from jax.experimental import pallas as pl
from jax.experimental.pallas import tpu as pltpu
from jax.sharding import PartitionSpec as P

F32 = jnp.float32
S = 9
CH = 10
CX = 16
CY = 8
DEV = 16
W = 18
PITCH = 24
FRAME = W * W
BLK = CY * W
SLAB_ROWS = CH * CX + 2 * CH
GF = 23
NF = GF + 3
TR = GF * 8
GB = 21
NB = GB + 3
CLS = 9
VMEM = pl.BlockSpec(memory_space=pltpu.VMEM)
SMEM = pl.BlockSpec(memory_space=pltpu.SMEM)


def weights():
    wf = np.zeros((128, 384), np.float32)
    rb = np.zeros((2, 128, 128), np.float32)
    for lane in range(128):
        q, fz = divmod(lane, 32)
        k, z = 1 + q // 2, fz // 2 + 1
        sy, sz = (0.125 if q % 2 else -0.125), (0.125 if fz % 2 else -0.125)
        wf[k * W + z, lane] += 1.0
        wf[(k + 1) * W + z, lane] += sy
        wf[(k - 1) * W + z, lane] -= sy
        wf[k * W + z + 1, lane] += sz
        wf[k * W + z - 1, lane] -= sz
        wf[k * W + z, 256 + lane] = 1.0
        rb[0, lane, (q // 2) * W + z] = 0.125
        if fz == 0:
            wf[k * W, 128 + lane] = 1.0
            rb[1, lane, (q // 2) * W] = 0.125
        if fz == 31:
            wf[k * W + W - 1, 128 + lane] = 1.0
            rb[1, lane, (q // 2) * W + W - 1] = 0.125
    wy = np.zeros((128, 128), np.float32)
    ry = np.zeros((128, 128), np.float32)
    for fz in range(32):
        z = fz // 2 + 1
        wy[z, fz] = 1.0
        wy[W + z, 96 + fz] = 1.0
        ry[fz, z] = 0.125
        ry[96 + fz, 50 + z] = 0.125
    twice = lambda m: np.concatenate([m, m], 0).astype(ml_dtypes.bfloat16)
    return twice(wf), twice(wy), np.concatenate([twice(rb[0]), twice(rb[1])], 0), twice(ry)


def lanes(shape):
    return lax.broadcasted_iota(jnp.int32, shape, 1)


def mod128(x):
    return lax.bitwise_and(x, 127)


def halves(x):
    hi = x.astype(jnp.bfloat16)
    return hi, (x - hi.astype(F32)).astype(jnp.bfloat16)


def pick(tab, index):
    rows = index.shape[0]
    parts = [
        jnp.take_along_axis(tab, index[r : r + 8], axis=1, mode="promise_in_bounds") for r in range(0, rows, 8)
    ]
    return parts[0] if len(parts) == 1 else jnp.concatenate(parts, 0)


def where_is(roots, row):
    first = roots[row, 1] - 1
    owner = lax.shift_right_logical(first, 3)
    return owner, first - 8 * owner, roots[row, 2] - 1


def pack_kernel(roots, u, idx, lo, hi, out, slab):
    grp, me = lax.axis_index("grp"), lax.axis_index("dev")
    for x in range(CX):
        for s in range(S):
            slab[pl.ds(s * CX + x, 8, stride=TR), :] = u[s, x]
        slab[pl.ds(S * CX + x, 8, stride=TR), :] = (idx[x] + 1).astype(F32)
    for c in range(CH):
        slab[pl.ds(CH * CX + c, 8, stride=TR), :] = lo[c]
        slab[pl.ds(CH * CX + CH + c, 8, stride=TR), :] = hi[c]
    for r in range(SLAB_ROWS, TR):
        slab[pl.ds(r, 8, stride=TR), :] = jnp.zeros((8, 128), F32)
    lane = lanes((8, 128))

    def one(p, carry):
        owner, y0, z0 = where_is(roots, grp * DEV + p)

        @pl.when(jnp.logical_and(me >= owner, 8 * (me - owner) - y0 < W))
        def _():
            rest = None
            for g in range(GF):
                main = None
                for y in range(8):
                    rows = slab[y * TR + 8 * g : y * TR + 8 * g + 8, :]
                    moved = pltpu.roll(rows, mod128(W * y + 128 - z0), 1)
                    main = moved if y == 0 else jnp.where(lane >= W * y, moved, main)
                out[p, g] = main
                slot = 16 * (g % 8)
                moved = pltpu.roll(rows, mod128(126 + slot + 128 - z0), 1)
                rest = moved if slot == 0 else jnp.where(lane >= slot, moved, rest)
                if slot == 112 or g == GF - 1:
                    out[p, GF + g // 8] = rest

        return carry

    lax.fori_loop(0, DEV, one, 0)


def coarse_kernel(u, idx, lo, hi, ylo, yhi, ptab, out, cls, px, pyl, pyh, pzl, pzh):
    lane = lanes((8, 128))
    sub = lax.broadcasted_iota(jnp.int32, (8, 128), 0)
    cls[0] = lo[S].astype(jnp.int32)
    cls[CX + 1] = hi[S].astype(jnp.int32)
    for x in range(CX):
        cls[x + 1] = idx[x] + 1

    def below_y(a, row):
        return jnp.where(sub == 0, jnp.broadcast_to(row, (8, 128)), pltpu.roll(a, 1, 0))

    def above_y(a, row):
        return jnp.where(sub == 7, jnp.broadcast_to(row, (8, 128)), pltpu.roll(a, 7, 0))

    def below_z(a):
        return jnp.where(lane == 0, jnp.zeros_like(a), pltpu.roll(a, 1, 1))

    def above_z(a):
        return jnp.where(lane == 127, jnp.zeros_like(a), pltpu.roll(a, 127, 1))

    for x in range(CX + 1):
        px[x] = cls[x + 1] * CLS + cls[x]
    for x in range(CX):
        c = cls[x + 1]
        pyl[x] = c * CLS + below_y(c, ylo[S, x : x + 1, :].astype(jnp.int32))
        pyh[x] = c * CLS + above_y(c, yhi[S, x : x + 1, :].astype(jnp.int32))
        pzl[x] = c * CLS + below_z(c)
        pzh[x] = c * CLS + above_z(c)

    def species(s, carry):
        tab = jnp.broadcast_to(0.5 * ptab[pl.ds(s, 1), :], (8, 128))
        center = u[s, 0]
        flux = pick(tab, px[0]) * (center - lo[s])
        for x in range(CX):
            after = u[s, x + 1] if x + 1 < CX else hi[s]
            next_flux = pick(tab, px[x + 1]) * (after - center)
            total = next_flux - flux
            total = total + pick(tab, pyl[x]) * (below_y(center, ylo[s, x : x + 1, :]) - center)
            total = total + pick(tab, pyh[x]) * (above_y(center, yhi[s, x : x + 1, :]) - center)
            total = total + pick(tab, pzl[x]) * (below_z(center) - center)
            total = total + pick(tab, pzh[x]) * (above_z(center) - center)
            out[s, x] = center + total
            center, flux = after, next_flux
        return carry

    lax.fori_loop(0, S, species, 0)


def patch_kernel(
    roots, recv, fidx, ptab, wf, wy, rb, ry,
    fine, back,
    fr, up, upy, ei, ipx, ipy, ipz, ipb, ua, ub, uy, zg, fx, fy, fz, fb, zr, yr, b1, b2, by, dl, hb,
):
    grp, me = lax.axis_index("grp"), lax.axis_index("dev")
    owner, y0, _ = where_is(roots, grp * DEV + me)
    lane = lanes((8, 128))
    lane_all = lanes((CH * PITCH, 128))
    start = [BLK * k - W * y0 for k in range(4)]
    source = [jnp.minimum(owner + k, DEV - 1) for k in range(4)]
    zero8 = jnp.zeros((8, 128), F32)

    for c in range(CH):
        for t in range(3):
            fr[t, c, 16:24] = zero8
    for g in range(GF):
        slot = 16 * (g % 8)
        main = [pltpu.roll(recv[source[k], g], mod128(start[k] + 256), 1) for k in range(4)]
        rest = [pltpu.roll(recv[source[k], GF + g // 8], mod128(start[k] + 384 - slot), 1) for k in range(3)]

        def over(t, piece, at, below):
            return jnp.where(lane >= at - 128 * t, piece, below)

        tile0 = over(0, main[1], start[1], over(0, rest[0], start[0] + 128, main[0]))
        tile1 = over(1, main[1], start[1], rest[0])
        tile1 = over(1, main[2], start[2], over(1, rest[1], start[1] + 128, tile1))
        tile2 = over(2, main[2], start[2], over(2, rest[1], start[1] + 128, main[1]))
        tile2 = over(2, main[3], start[3], over(2, rest[2], start[2] + 128, tile2))
        tile2 = jnp.where(lane < FRAME - 256, tile2, 0.0)
        for t, tile in enumerate((tile0, tile1, tile2)):
            if g < 2 * CH:
                fr[t, g // 2, 1 + 8 * (g % 2) : 9 + 8 * (g % 2)] = tile
            else:
                for i in range(8):
                    q = 8 * (g - 2 * CH) + i
                    if q < 2 * CH:
                        at = 0 if q < CH else W - 1
                        fr[t, q % CH, at : at + 1] = tile[i : i + 1]

    def spread(values, weight):
        hi, lo = halves(values)
        return jnp.dot(jnp.concatenate([hi, lo], 1), weight, preferred_element_type=F32)

    for j in range(8):
        t, off = divmod(2 * W * j, 128)
        values = fr[t].reshape(CH * PITCH, 128)
        if off:
            values = pltpu.roll(values, 128 - off, 1)
            if off + 4 * W > 128:
                after = pltpu.roll(fr[t + 1].reshape(CH * PITCH, 128), 128 - off, 1)
                values = jnp.where(lane_all < 128 - off, values, after)
        result = spread(values, wf[...])
        for b in range(3):
            up[3 * j + b] = result[:, 128 * b : 128 * b + 128].reshape(CH, PITCH, 128)
    ends = jnp.where(
        lane_all < W,
        pltpu.roll(fr[2].reshape(CH * PITCH, 128), 78, 1),
        pltpu.roll(fr[0].reshape(CH * PITCH, 128), W, 1),
    )
    upy[...] = spread(ends, wy[...]).reshape(CH, PITCH, 128)

    def both(ref_at, values):
        ref_at(0)(values)
        ref_at(1)(values)

    def ghosts(channel):
        for j in range(8):
            values = up[3 * j + 1, channel, 1 : CX + 1]
            zg[j, pl.ds(0, CX, stride=2), :] = values
            zg[j, pl.ds(1, CX, stride=2), :] = values
        values = upy[channel, 1 : CX + 1]
        uy[pl.ds(0, CX, stride=2), :] = values
        uy[pl.ds(1, CX, stride=2), :] = values

    lane32 = lanes((32, 128))
    first_z = lax.bitwise_and(lane32, 31) == 0
    ghosts(S)
    for j in range(8):
        ei[j, 40:48] = jnp.zeros((8, 128), jnp.int32)
        ei[j, 8:40] = fidx[0, :, 128 * j : 128 * j + 128] + 1
        ei[j, 7:8] = up[3 * j + 2, S, 0:1].astype(jnp.int32)
        ei[j, 40:41] = up[3 * j + 2, S, W - 1 : W].astype(jnp.int32)
    y_ghost = uy[...].astype(jnp.int32)
    before = pltpu.roll(y_ghost, 32, 1)
    for j in range(8):
        ipx[j] = ei[j, 8:48] * CLS + ei[j, 7:47]
        c = ei[j, 8:40]
        moved = pltpu.roll(c, 32, 1)
        ipy[j] = c * CLS + jnp.where(lane32 < 32, before, moved)
        before = moved
        z_ghost = zg[j].astype(jnp.int32)
        ipz[j] = c * CLS + jnp.where(first_z, z_ghost, pltpu.roll(c, 1, 1))
        ipb[j] = c * CLS + z_ghost
    ipy[8] = y_ghost * CLS + jnp.where(lane32 < 32, before, pltpu.roll(y_ghost, 32, 1))

    for c in range(CH):
        for j in range(8):
            b1[j, c, 16:24] = zero8
            b2[j, c, 0:8] = zero8
            b2[j, c, 16:24] = zero8
            if c == S:
                b1[j, c, 0:8] = zero8
                b1[j, c, 8:16] = zero8
                b2[j, c, 8:16] = zero8
        by[c, 0:8] = zero8
        by[c, 16:24] = zero8
        if c == S:
            by[c, 8:16] = zero8

    z_low = lax.bitwise_and(lane, 31) == 0
    z_top = lax.bitwise_and(lane, 31) == 31
    y_wrap = lane < 32
    y_keep = lane < 96

    def subcycle(s, src, dst, last):
        for b in range(4):
            rows = slice(8 + 8 * b, 16 + 8 * b)
            own = slice(8 * b, 8 * b + 8)
            u = [src[j, rows] for j in range(8)]
            edge = uy[own]
            moved = [pltpu.roll(a, 32, 1) for a in u]
            moved_edge = pltpu.roll(edge, 32, 1)
            gy = []
            for j in range(8):
                under = jnp.where(y_wrap, moved[j - 1] if j else moved_edge, moved[j])
                gy.append(fy[j, own] * (u[j] - under))
            gy.append(fy[8, own] * (edge - jnp.where(y_wrap, moved[7], moved_edge)))
            shifted = [pltpu.roll(a, 96, 1) for a in gy]
            reg_y = jnp.where(y_wrap, gy[0], jnp.where(y_keep, 0.0, -shifted[8]))
            yr[own] = yr[own] + reg_y if last else reg_y
            for j in range(8):
                change = jnp.where(y_keep, shifted[j], shifted[j + 1]) - gy[j]
                ghost = zg[j, own]
                gz = fz[j, own] * (u[j] - jnp.where(z_low, ghost, pltpu.roll(u[j], 1, 1)))
                gb = fb[j, own] * (ghost - u[j])
                change = change + (jnp.where(z_top, gb, pltpu.roll(gz, 127, 1)) - gz)
                reg_z = jnp.where(z_low, gz, jnp.where(z_top, -gb, 0.0))
                zr[j, own] = zr[j, own] + reg_z if last else reg_z
                low = fx[j, own] * (u[j] - src[j, 7 + 8 * b : 15 + 8 * b])
                top = fx[j, 1 + 8 * b : 9 + 8 * b] * (src[j, 9 + 8 * b : 17 + 8 * b] - u[j])
                change = change + (top - low)
                if b == 0:
                    b1[j, s, 0:1] = b1[j, s, 0:1] + low[0:1] if last else low[0:1]
                if b == 3:
                    b1[j, s, W - 1 : W] = b1[j, s, W - 1 : W] - top[7:8] if last else -top[7:8]
                value = u[j] + change
                dst[j, rows] = value
                if last:
                    fine[0, s, own, 128 * j : 128 * j + 128] = value

    def species(s, carry):
        tab = jnp.broadcast_to(ptab[pl.ds(s, 1), :], (8, 128))
        ghosts(s)
        for j in range(8):
            core = up[3 * j + 2, s]
            slope = 0.125 * (up[3 * j + 2, s, 2 : CX + 2] - up[3 * j + 2, s, 0:CX])
            middle = up[3 * j, s, 1 : CX + 1]
            ua[j, pl.ds(8, CX, stride=2), :] = middle - slope
            ua[j, pl.ds(9, CX, stride=2), :] = middle + slope
            for ref in (ua, ub):
                ref[j, 7:8] = core[0:1]
                ref[j, 40:41] = core[W - 1 : W]
            fx[j] = pick(tab, ipx[j])
            fy[j] = pick(tab, ipy[j])
            fz[j] = pick(tab, ipz[j])
            fb[j] = pick(tab, ipb[j])
        fy[8] = pick(tab, ipy[8])
        subcycle(s, ua, ub, False)
        subcycle(s, ub, ua, True)
        for j in range(8):
            b1[j, s, 1 : CX + 1] = ua[j, pl.ds(8, CX, stride=2), :] + ua[j, pl.ds(9, CX, stride=2), :]
            b2[j, s, 1 : CX + 1] = zr[j, pl.ds(0, CX, stride=2), :] + zr[j, pl.ds(1, CX, stride=2), :]
        by[s, 1 : CX + 1] = yr[pl.ds(0, CX, stride=2), :] + yr[pl.ds(1, CX, stride=2), :]
        return carry

    lax.fori_loop(0, S, species, 0)

    delta = [jnp.zeros((CH * PITCH, 128), F32) for _ in range(3)]
    for j in range(8):
        t, off = divmod(2 * W * j + W, 128)
        parts = halves(b1[j].reshape(CH * PITCH, 128)) + halves(b2[j].reshape(CH * PITCH, 128))
        sums = pltpu.roll(jnp.dot(jnp.concatenate(parts, 1), rb[...], preferred_element_type=F32), off, 1)
        if off + 2 * W > 128:
            dl[t] = (delta[t] + jnp.where(lane_all >= off, sums, 0.0)).reshape(CH, PITCH, 128)
            delta[t] = dl[t].reshape(CH * PITCH, 128)
            delta[t + 1] = delta[t + 1] + jnp.where(lane_all < off, sums, 0.0)
        else:
            delta[t] = delta[t] + sums
    sums = spread(by[...].reshape(CH * PITCH, 128), ry[...])
    delta[0] = delta[0] + jnp.where(lane_all < W, sums, 0.0)
    delta[2] = delta[2] + jnp.where(lane_all >= 50, sums, 0.0)
    for t in range(3):
        dl[t] = delta[t].reshape(CH, PITCH, 128)

    lane24 = lanes((PITCH, 128))
    row24 = lax.broadcasted_iota(jnp.int32, (PITCH, 128), 0)

    def within(a, top):
        return jnp.logical_and(a >= 1, a <= top)

    def shifted_down(tiles, by_lanes):
        moved = [pltpu.roll(a, by_lanes, 1) for a in tiles]
        return [jnp.where(lane24 < by_lanes, moved[t - 1], moved[t]) for t in range(3)]

    def shifted_up(tiles, by_lanes):
        moved = [pltpu.roll(a, 128 - by_lanes, 1) for a in tiles]
        return [jnp.where(lane24 < 128 - by_lanes, moved[t], moved[(t + 1) % 3]) for t in range(3)]

    cells = [fr[t, S].astype(jnp.int32) for t in range(3)]
    for t, (down_y, down_z) in enumerate(zip(shifted_down(cells, W), shifted_down(cells, 1))):
        ipx[t, 0:24] = cells[t] * CLS + pltpu.roll(cells[t], 1, 0)
        ipy[t, 0:24] = cells[t] * CLS + down_y
        ipz[t, 0:24] = cells[t] * CLS + down_z
        cell = lane24 + 128 * t
        y = lax.shift_right_logical(cell * 3641, 16)
        z = cell - W * y
        inside = [within(row24, CX), within(y, CX), within(z, CX)]
        both_in = lambda a, b, c: jnp.logical_and(a, jnp.logical_and(b, c))
        fx[t, 0:24] = jnp.where(both_in(within(row24, CX + 1), inside[1], inside[2]), 0.5, 0.0)
        fy[t, 0:24] = jnp.where(both_in(inside[0], within(y, CX + 1), inside[2]), 0.5, 0.0)
        fz[t, 0:24] = jnp.where(both_in(inside[0], inside[1], within(z, CX + 1)), 0.5, 0.0)
        fb[t, 0:24] = jnp.where(both_in(*inside), 1.0, 0.0)

    def coarse(s, carry):
        tab = jnp.broadcast_to(ptab[pl.ds(s, 1), :], (8, 128))
        u = [fr[t, s] for t in range(3)]
        down_y, down_z = shifted_down(u, W), shifted_down(u, 1)
        gx = [fx[t, 0:24] * pick(tab, ipx[t, 0:24]) * (u[t] - pltpu.roll(u[t], 1, 0)) for t in range(3)]
        gy = [fy[t, 0:24] * pick(tab, ipy[t, 0:24]) * (u[t] - down_y[t]) for t in range(3)]
        gz = [fz[t, 0:24] * pick(tab, ipz[t, 0:24]) * (u[t] - down_z[t]) for t in range(3)]
        up_y, up_z = shifted_up(gy, W), shifted_up(gz, 1)
        for t in range(3):
            total = (pltpu.roll(gx[t], PITCH - 1, 0) - gx[t]) + (up_y[t] - gy[t]) + (up_z[t] - gz[t])
            dl[t, s] = dl[t, s] - (fb[t, 0:24] * u[t] + total)
        return carry

    lax.fori_loop(0, S, coarse, 0)

    for t in range(3):
        hb[t, 16:24] = zero8
        for s in range(S):
            hb[t, s : s + 1] = dl[t, s, 0:1]
            hb[t, S + s : S + s + 1] = dl[t, s, W - 1 : W]

    def group_tiles(g):
        if g < 2 * S:
            return [dl[t, g // 2, 1 + 8 * (g % 2) : 9 + 8 * (g % 2)] for t in range(3)]
        return [hb[t, 8 * (g - 2 * S) : 8 * (g - 2 * S) + 8] for t in range(3)]

    main_from = ([0], [0, 1, 2], [1, 2, 3], [2, 3])
    rest_from = ([0, 1], [1, 2], [2, 3], [])
    for k in range(4):

        @pl.when(8 * k - y0 < W)
        def _(k=k):
            rest = None
            for g in range(GB):
                tiles = group_tiles(g) + [None]
                slot = 16 * (g % 8)

                def cut(number, amount, at):
                    value = zero8
                    for t in number:
                        piece = zero8 if tiles[t] is None else pltpu.roll(tiles[t], mod128(amount), 1)
                        value = jnp.where(lane >= 128 * t - at, piece, value)
                    return value

                back[owner + k, g] = cut(main_from[k], 512 - start[k], start[k])
                part = cut(rest_from[k], 512 - start[k] + slot, start[k] + 128 - slot)
                rest = part if slot == 0 else jnp.where(lane >= slot, part, rest)
                if slot == 112 or g == GB - 1:
                    back[owner + k, GB + g // 8] = rest


def add_windows(roots, arrived, acc, groups, stride):
    grp, me = lax.axis_index("grp"), lax.axis_index("dev")
    lane = lanes((8, 128))

    def clear(i, carry):
        acc[pl.ds(pl.multiple_of(8 * i, 8), 8), :] = jnp.zeros((8, 128), F32)
        return carry

    lax.fori_loop(0, stride, clear, 0)

    def one(p, carry):
        owner, y0, z0 = where_is(roots, grp * DEV + p)

        @pl.when(jnp.logical_and(me >= owner, 8 * (me - owner) - y0 < W))
        def _():
            window = jnp.logical_and(lane >= z0, lane < z0 + W)
            for number, g in enumerate(groups):
                main, rest = arrived[p, g], arrived[p, GB + g // 8]
                for y in range(8):
                    moved = pltpu.roll(main, mod128(z0 + 128 - W * y), 1)
                    if y == 7:
                        tail = pltpu.roll(rest, mod128(z0 + 2 + 128 - 16 * (g % 8)), 1)
                        moved = jnp.where(lane < z0 + 2, moved, tail)
                    rows = slice(y * stride + 8 * number, y * stride + 8 * number + 8)
                    acc[rows, :] = acc[rows, :] + jnp.where(window, moved, 0.0)

        return carry

    lax.fori_loop(0, DEV, one, 0)


def halo_kernel(roots, arrived, low, top, acc):
    add_windows(roots, arrived, acc, range(2 * S, GB), 24)
    for s in range(S):
        low[s] = acc[pl.ds(s, 8, stride=24), :]
        top[s] = acc[pl.ds(S + s, 8, stride=24), :]


def add_kernel(roots, arrived, coarse_one, out, acc):
    add_windows(roots, arrived, acc, range(2 * S), S * CX)
    for s in range(S):
        for x in range(CX):
            out[s, x] = coarse_one[s, x] + acc[pl.ds(s * CX + x, 8, stride=S * CX), :]


def call(kernel, outs, ins, scratch, name):
    return pl.pallas_call(
        kernel,
        out_shape=outs,
        in_specs=ins,
        out_specs=jax.tree.map(lambda _: VMEM, outs),
        scratch_shapes=scratch,
        compiler_params=pltpu.CompilerParams(vmem_limit_bytes=48 * 1024 * 1024),
        name=name,
    )


def shape(*dims):
    return jax.ShapeDtypeStruct(dims, F32)


def body(coarse_state, coef_index, coef_table, patch_root, fine_index):
    ends_g, ends_d = lax.axis_size("grp") - 1, lax.axis_size("dev") - 1
    up_g, down_g = [(i, i + 1) for i in range(ends_g)], [(i + 1, i) for i in range(ends_g)]
    up_d, down_d = [(i, i + 1) for i in range(ends_d)], [(i + 1, i) for i in range(ends_d)]
    known = jnp.concatenate([jnp.zeros((1, S), F32), coef_table], 0)
    pairs = (0.08 * (known[:, None] + known[None, :])).reshape(CLS * CLS, S)
    ptab = jnp.pad(pairs.T, ((0, 0), (0, 128 - CLS * CLS)))

    def plane(u, c):
        return jnp.concatenate([u, (c[None] + 1).astype(F32)], 0)

    x_lo = lax.ppermute(plane(coarse_state[:, CX - 1], coef_index[CX - 1]), "grp", up_g)
    x_hi = lax.ppermute(plane(coarse_state[:, 0], coef_index[0]), "grp", down_g)
    y_lo = lax.ppermute(plane(coarse_state[:, :, CY - 1], coef_index[:, CY - 1]), "dev", up_d)
    y_hi = lax.ppermute(plane(coarse_state[:, :, 0], coef_index[:, 0]), "dev", down_d)

    blocks = call(
        pack_kernel, shape(DEV, NF, 8, 128), [SMEM] + [VMEM] * 4, [pltpu.VMEM((8 * TR, 128), F32)], "pack"
    )(patch_root, coarse_state, coef_index, x_lo, x_hi)
    received = lax.all_to_all(blocks, "dev", split_axis=0, concat_axis=0, tiled=True)
    i32 = lambda *dims: pltpu.VMEM(dims, jnp.int32)
    f32 = lambda *dims: pltpu.VMEM(dims, F32)
    coarse_one = call(
        coarse_kernel,
        shape(S, CX, CY, 128),
        [VMEM] * 7,
        [i32(CX + 2, 8, 128), i32(CX + 1, 8, 128)] + [i32(CX, 8, 128)] * 4,
        "coarse",
    )(coarse_state, coef_index, x_lo, x_hi, y_lo, y_hi, ptab)

    tables = [jnp.asarray(w) for w in weights()]
    fine_state, corrections = call(
        patch_kernel,
        (shape(1, S, 32, 1024), shape(DEV, NB, 8, 128)),
        [SMEM] + [VMEM] * 7,
        [
            f32(3, CH, PITCH, 128), f32(24, CH, PITCH, 128), f32(CH, PITCH, 128),
            i32(8, 48, 128), i32(8, 40, 128), i32(9, 32, 128), i32(8, 32, 128), i32(8, 32, 128),
            f32(8, 48, 128), f32(8, 48, 128), f32(32, 128), f32(8, 32, 128),
            f32(8, 40, 128), f32(9, 32, 128), f32(8, 32, 128), f32(8, 32, 128),
            f32(8, 32, 128), f32(32, 128),
            f32(8, CH, PITCH, 128), f32(8, CH, PITCH, 128), f32(CH, PITCH, 128),
            f32(3, CH, PITCH, 128), f32(3, 24, 128),
        ],
        "patch",
    )(patch_root, received, fine_index, ptab, *tables)
    arrived = lax.all_to_all(corrections, "dev", split_axis=0, concat_axis=0, tiled=True)
    low, top = call(
        halo_kernel, (shape(S, CY, 128), shape(S, CY, 128)), [SMEM, VMEM], [f32(8 * 24, 128)], "halo"
    )(patch_root, arrived)
    from_above = lax.ppermute(low, "grp", down_g)
    from_below = lax.ppermute(top, "grp", up_g)
    coarse_new = call(
        add_kernel, shape(S, CX, CY, 128), [SMEM, VMEM, VMEM], [f32(8 * S * CX, 128)], "add"
    )(patch_root, arrived, coarse_one)
    coarse_new = coarse_new.at[:, CX - 1].add(from_above)
    coarse_new = coarse_new.at[:, 0].add(from_below)
    return coarse_new, fine_state


def solution(mesh):
    return jax.shard_map(
        body,
        mesh=mesh,
        in_specs=(
            P(None, "grp", "dev", None),
            P("grp", "dev", None),
            P(),
            P(),
            P(("grp", "dev"), None, None),
        ),
        out_specs=(P(None, "grp", "dev", None), P(("grp", "dev"), None, None, None)),
        check_vma=False,
    )
```

time: 1600 us -> 124 us (0.08)
  local copies, waits for them, and re-layouts: 1190 us -> 5.96 us
  other arithmetic: 257 us -> 0.84 us
  Pallas kernels: 0 us -> 33.1 us
  loops' own time: 30.6 us -> 0 us
  matrix products: 25.3 us -> 0 us
    dynamic_update_slice x16 -> x0, local copies, waits for them, and re-layouts: 495 us -> none  [put_one(): return lax.dynamic_update_slice(acc, current + windows[number], anchor)]
    scatter x8 -> x0, local copies, waits for them, and re-layouts: 316 us -> none  [the longest x1 111 us: patch_work(): dext = ghost_fill(foot_d).at[:, 1:-1, 1:-1, 1:-1].set(inner_d)]
    broadcast_in_dim x44 -> x0, local copies, waits for them, and re-layouts: 116 us -> none  [the longest x38 115 us: upsample(): return jnp.repeat(jnp.repeat(jnp.repeat(block, 2, 1), 2, 2), 2, 3)]
    unnamed x93 -> x25, local copies, waits for them, and re-layouts: 105 us -> 4.86 us
    mul x13 -> x1, other arithmetic: 94 us -> 0.08 us  [body(): pairs = (0.08 * (known[:, None] + known[None, :])).reshape(CLS * CLS, S)]
    add x28 -> x0, other arithmetic: 93.9 us -> none  [the longest x4 44.8 us: patch_work(): field = shell + pad_inner(core + lam_fine * change)]
    gather x2 -> x0, local copies, waits for them, and re-layouts: 47.8 us -> none  [cut_one(): return lax.dynamic_slice(slab, anchor, (channels, width, cells_y, width))]
    pallas_call x0 -> x5, Pallas kernels: none -> 33.1 us  [the longest x1 21.4 us: body(): call(patch_kernel, (shape(1, S, 32, 1024), shape(DEV, NB, 8, 128)), [SMEM...]
  transfers between devices with their start and end apart: 8 -> 8, of which waited for: 5 -> 4; matrix products, arithmetic and copies ran while one was open for 2% -> 1% of each run, Pallas kernels for 0% -> 7%
where the time goes in v1:
time: 124 us; the launch traced here: 123 us
  waiting for transfers between devices  54.2 us (44%)
  Pallas kernels  33.1 us (27%)
  starting transfers between devices  27.8 us (22%)
  local copies, waits for them, and re-layouts  5.96 us (5%)
    all_to_all x1, waiting for transfers between devices, body(): lax.all_to_all(blocks, 'dev', split_axis=0, concat_axis=0, tiled=True)  26.8 us
    all_to_all x1, waiting for transfers between devices, body(): lax.all_to_all(corrections, 'dev', split_axis=0, concat_axis=0, tiled=True)  24.1 us
    pallas_call x1, Pallas kernels, body(): call(patch_kernel, (shape(1, S, 32, 1024), shape(DEV, NB, 8, 128)), [SMEM...  21.4 us
    all_to_all x1, starting transfers between devices, body(): lax.all_to_all(blocks, 'dev', split_axis=0, concat_axis=0, tiled=True)  8.27 us
    unnamed x25, local copies, waits for them, and re-layouts  4.86 us
    all_to_all x1, starting transfers between devices, body(): lax.all_to_all(corrections, 'dev', split_axis=0, concat_axis=0, tiled=True)  4.06 us
    ppermute x1, starting transfers between devices, body(): lax.ppermute(plane(coarse_state[:, :, CY - 1], coef_index[:, CY - 1]), 'd...  3.83 us
    ppermute x1, starting transfers between devices, body(): x_hi = lax.ppermute(plane(coarse_state[:, 0], coef_index[0]), 'grp', down_g)  3.64 us
  transfers between devices with their start and end apart: 8, of which 4 were waited for; matrix products, arithmetic and copies ran while one was open for 1% of the time, Pallas kernels for 7%

profile of v1, /device:TPU:32, one launch (start us, length us, event | category | flops | bytes accessed | tf_op | source)
XLA Modules:
  0.0 122.8 jit_solution(27618448165989683)
XLA Ops:
  0.6 0.8 slice_bitcast_fusion
  1.4 0.7 add_convert_fusion
  2.1 1.9 %collective-permute-start = (f32[10,8,128]{2,1,0:T(8,128)S(1)}, f32[10,8,128]{2,1,0:T(8,128)S(1)}, u32[]{:S(2)}, u32[]{:S(2)}) collective-permute-start(f32[10,8,128]{2,1,0:T(8,128)S(1)} %pad_maximum_fusion.2), channel_id=1, source_target_pairs={{0,16},{16,32},{32,48},{48,64},{64,80},{80,96},{96,112},{1,17},{17... | collective-permute-start | bytes 122888 | tf_op jit(solution)/shard_map/ppermute | solution.py:522
  4.1 3.6 %collective-permute-start.1 = (f32[10,8,128]{2,1,0:T(8,128)S(1)}, f32[10,8,128]{2,1,0:T(8,128)S(1)}, u32[]{:S(2)}, u32[]{:S(2)}) collective-permute-start(f32[10,8,128]{2,1,0:T(8,128)S(1)} %pad_maximum_fusion.3), channel_id=1, source_target_pairs={{16,0},{32,16},{48,32},{64,48},{80,64},{96,80},{112,96},{17,1},{33... | collective-permute-start | bytes 122888 | tf_op jit(solution)/shard_map/ppermute | solution.py:523
  7.7 0.8 copy.21.roots
  8.5 0.0 collective-permute-done.lo
  8.5 0.9 collective-permute-done.1.hi
  9.4 0.0 copy-start
  9.4 1.1 copy-done
  10.4 0.0 copy-start.3
  10.4 0.8 copy-done.3
  11.3 3.3 %pack.1 = f32[16,26,8,128]{3,2,1,0:T(8,128)} custom-call(s32[128,3]{1,0:T(8,128)S(1)} %copy.21.roots, f32[9,16,8,128]{3,2,1,0:T(8,128)S(1)} %copy-done, s32[16,8,128]{2,1,0:T(8,128)S(1)} %copy-done.3, f32[10,8,128]{2,1,0:T(8,128)S(1)} %collective-permute-done.lo, f32[10,8,128]{2,1,0:T(8,128)S(1)} %collective-permute-done.1.hi), custom_call_target="tpu_custom_call" | custom-call | tf_op jit(solution)/shard_map/pack/pallas_call | solution.py:527
  14.6 0.0 copy-start.10
  14.6 0.0 copy-start.5
  14.6 0.0 copy-start.6
  14.6 0.0 copy-start.7
  14.6 0.0 copy-start.8
  14.6 0.0 copy-start.9
  14.6 8.3 %all-to-all-start = ((f32[16,26,8,128]{3,2,1,0:T(8,128)}), f32[16,26,8,128]{3,2,1,0:T(8,128)S(1)}, u32[]{:S(2)}, u32[]{:S(2)}) async-start(f32[16,26,8,128]{3,2,1,0:T(8,128)} %pack.1), calls=%async_computation | async-start | bytes 3407872 | tf_op jit(solution)/shard_map/all_to_all | solution.py:530
  22.9 0.0 copy-done.10
  22.9 0.1 copy.32
  23.0 0.1 concatenate.21.clone
  23.1 0.1 add_multiply_fusion
  23.2 0.1 mul.12
  23.3 26.8 %all-to-all-done.recv = f32[16,26,8,128]{3,2,1,0:T(8,128)S(1)} async-done(((f32[16,26,8,128]{3,2,1,0:T(8,128)}), f32[16,26,8,128]{3,2,1,0:T(8,128)S(1)}, u32[]{:S(2)}, u32[]{:S(2)}) %all-to-all-start) | async-done | bytes 1703968 | tf_op jit(solution)/shard_map/all_to_all | solution.py:530
  50.1 0.0 copy-done.5
  50.1 0.0 copy-done.6
  50.1 0.0 copy-done.7
  50.1 0.0 copy-done.8
  50.1 0.0 copy-done.9
  50.1 21.4 %patch.1 = (f32[1,9,32,1024]{3,2,1,0:T(8,128)}, f32[16,24,8,128]{3,2,1,0:T(8,128)S(1)}) custom-call(s32[128,3]{1,0:T(8,128)S(1)} %copy.21.roots, f32[16,26,8,128]{3,2,1,0:T(8,128)S(1)} %all-to-all-done.recv, s32[1,32,1024]{2,1,0:T(8,128)S(1)} %copy-done.6, f32[9,128]{1,0:T(8,128)S(1)} %pad.9.ptab, bf16[256,384]{1,0:T(8,128)(2,1)S(1)} %copy-done.5, ...), custom_call_target="tpu_custom_call" | custom-call | tf_op jit(solution)/shard_map/patch/pallas_call | solution.py:542
  71.5 0.0 copy-start.2
  71.5 1.2 copy-done.2
  72.7 0.0 copy-start.4
  72.7 0.0 copy-start.1
  72.7 4.1 %all-to-all-start.1 = ((f32[16,24,8,128]{3,2,1,0:T(8,128)}), f32[16,24,8,128]{3,2,1,0:T(8,128)S(1)}, u32[]{:S(2)}, u32[]{:S(2)}) async-start(f32[16,24,8,128]{3,2,1,0:T(8,128)} %copy-done.2), calls=%async_computation.1 | async-start | bytes 3145728 | tf_op jit(solution)/shard_map/all_to_all | solution.py:557
  76.8 0.0 copy-done.4
  76.8 0.0 copy-done.1
  76.8 0.1 fusion.2
  77.0 3.8 %collective-permute-start.2 = (f32[10,16,128]{2,1,0:T(8,128)S(1)}, f32[10,16,128]{2,1,0:T(8,128)S(1)}, u32[]{:S(2)}, u32[]{:S(2)}) collective-permute-start(f32[10,16,128]{2,1,0:T(8,128)S(1)} %pad_maximum_fusion), channel_id=1, source_target_pairs={{0,1},{1,2},{2,3},{3,4},{4,5},{5,6},{6,7},{7,8},{8,9},{9,10},{10,1... | collective-permute-start | bytes 245768 | tf_op jit(solution)/shard_map/ppermute | solution.py:524
  80.8 1.3 %collective-permute-start.3 = (f32[10,16,128]{2,1,0:T(8,128)S(1)}, f32[10,16,128]{2,1,0:T(8,128)S(1)}, u32[]{:S(2)}, u32[]{:S(2)}) collective-permute-start(f32[10,16,128]{2,1,0:T(8,128)S(1)} %pad_maximum_fusion.1), channel_id=1, source_target_pairs={{1,0},{2,1},{3,2},{4,3},{5,4},{6,5},{7,6},{8,7},{9,8},{10,9},{11,1... | collective-permute-start | bytes 245768 | tf_op jit(solution)/shard_map/ppermute | solution.py:525
  82.1 24.1 %all-to-all-done.1.arrived = f32[16,24,8,128]{3,2,1,0:T(8,128)S(1)} async-done(((f32[16,24,8,128]{3,2,1,0:T(8,128)}), f32[16,24,8,128]{3,2,1,0:T(8,128)S(1)}, u32[]{:S(2)}, u32[]{:S(2)}) %all-to-all-start.1) | async-done | bytes 1572896 | tf_op jit(solution)/shard_map/all_to_all | solution.py:557
  106.3 2.1 %halo.1 = (f32[9,8,128]{2,1,0:T(8,128)S(1)}, f32[9,8,128]{2,1,0:T(8,128)S(1)}) custom-call(s32[128,3]{1,0:T(8,128)S(1)} %copy.21.roots, f32[16,24,8,128]{3,2,1,0:T(8,128)S(1)} %all-to-all-done.1.arrived), custom_call_target="tpu_custom_call" | custom-call | tf_op jit(solution)/shard_map/halo/pallas_call | solution.py:558
  108.4 1.9 %collective-permute-start.4 = (f32[9,8,128]{2,1,0:T(8,128)S(1)}, f32[9,8,128]{2,1,0:T(8,128)S(1)}, u32[]{:S(2)}, u32[]{:S(2)}) collective-permute-start(f32[9,8,128]{2,1,0:T(8,128)S(1)} %get-tuple-element.31), channel_id=1, source_target_pairs={{16,0},{32,16},{48,32},{64,48},{80,64},{96,80},{112,96},{17,1},{33... | collective-permute-start | bytes 110600 | tf_op jit(solution)/shard_map/ppermute | solution.py:561
  110.3 0.0 collective-permute-done.2.ylo
  110.3 0.0 collective-permute-done.3.yhi
  110.3 3.3 %coarse.1.coarse_one = f32[9,16,8,128]{3,2,1,0:T(8,128)S(1)} custom-call(f32[9,16,8,128]{3,2,1,0:T(8,128)S(1)} %copy-done.1, s32[16,8,128]{2,1,0:T(8,128)S(1)} %copy-done.4, f32[10,8,128]{2,1,0:T(8,128)S(1)} %collective-permute-done.lo, f32[10,8,128]{2,1,0:T(8,128)S(1)} %collective-permute-done.1.hi, f32[10,16,128]{2,1,0:T(8,128)S(1)} %collective-permute-done.2.ylo, ...), custom_call_target="tpu_custom_call" | custom-call | tf_op jit(solution)/shard_map/coarse/pallas_call | solution.py:533
  113.6 3.0 %add.86 = f32[9,16,8,128]{3,2,1,0:T(8,128)S(1)} custom-call(s32[128,3]{1,0:T(8,128)S(1)} %copy.21.roots, f32[16,24,8,128]{3,2,1,0:T(8,128)S(1)} %all-to-all-done.1.arrived, f32[9,16,8,128]{3,2,1,0:T(8,128)S(1)} %coarse.1.coarse_one), custom_call_target="tpu_custom_call" | custom-call | tf_op jit(solution)/shard_map/add/pallas_call | solution.py:563
  116.7 2.9 %collective-permute-start.5 = (f32[9,8,128]{2,1,0:T(8,128)S(1)}, f32[9,8,128]{2,1,0:T(8,128)S(1)}, u32[]{:S(2)}, u32[]{:S(2)}) collective-permute-start(f32[9,8,128]{2,1,0:T(8,128)S(1)} %get-tuple-element.32), channel_id=1, source_target_pairs={{0,16},{16,32},{32,48},{48,64},{64,80},{80,96},{96,112},{1,17},{17... | collective-permute-start | bytes 110600 | tf_op jit(solution)/shard_map/ppermute | solution.py:562
  119.5 0.0 collective-permute-done.4
  119.5 2.4 %collective-permute-done.5 = f32[9,8,128]{2,1,0:T(8,128)S(1)} collective-permute-done((f32[9,8,128]{2,1,0:T(8,128)S(1)}, f32[9,8,128]{2,1,0:T(8,128)S(1)}, u32[]{:S(2)}, u32[]{:S(2)}) %collective-permute-start.5) | collective-permute-done | bytes 36896 | tf_op jit(solution)/shard_map/ppermute | solution.py:562
  121.9 0.9 copy.25
  (11 shorter events, 0.1 us)
Async XLA Ops:
  2.1 6.4 %collective-permute-start = (f32[10,8,128]{2,1,0:T(8,128)S(1)}, f32[10,8,128]{2,1,0:T(8,128)S(1)}, u32[]{:S(2)}, u32[]{:S(2)}) collective-permute-start(f32[10,8,128]{2,1,0:T(8,128)S(1)} %pad_maximum_fusion.2), channel_id=1, source_target_pairs={{0,16},{16,32},{32,48},{48,64},{64,80},{80,96},{96,112},{1,17},{17... | collective-permute-start | bytes 122888 | tf_op jit(solution)/shard_map/ppermute | solution.py:522
  4.1 5.3 %collective-permute-start.1 = (f32[10,8,128]{2,1,0:T(8,128)S(1)}, f32[10,8,128]{2,1,0:T(8,128)S(1)}, u32[]{:S(2)}, u32[]{:S(2)}) collective-permute-start(f32[10,8,128]{2,1,0:T(8,128)S(1)} %pad_maximum_fusion.3), channel_id=1, source_target_pairs={{16,0},{32,16},{48,32},{64,48},{80,64},{96,80},{112,96},{17,1},{33... | collective-permute-start | bytes 122888 | tf_op jit(solution)/shard_map/ppermute | solution.py:523
  9.4 1.1 copy-start
  10.4 0.8 copy-start.3
  14.6 8.3 %copy-start.10 = (f32[8,9]{1,0:T(8,128)S(1)}, f32[8,9]{1,0:T(8,128)}, u32[]{:S(2)}) copy-start(f32[8,9]{1,0:T(8,128)} %param.15) | copy-start | bytes 868
  14.6 35.5 %copy-start.5 = (bf16[256,384]{1,0:T(8,128)(2,1)S(1)}, bf16[256,384]{1,0:T(8,128)(2,1)}, u32[]{:S(2)}) copy-start(bf16[256,384]{1,0:T(8,128)(2,1)} %constant.72.clone.wf) | copy-start | bytes 589828
  14.6 35.5 %copy-start.6 = (s32[1,32,1024]{2,1,0:T(8,128)S(1)}, s32[1,32,1024]{2,1,0:T(8,128)}, u32[]{:S(2)}) copy-start(s32[1,32,1024]{2,1,0:T(8,128)} %fidx.1) | copy-start | bytes 393220
  14.6 35.5 %copy-start.7 = (bf16[512,128]{1,0:T(8,128)(2,1)S(1)}, bf16[512,128]{1,0:T(8,128)(2,1)}, u32[]{:S(2)}) copy-start(bf16[512,128]{1,0:T(8,128)(2,1)} %constant.74.clone.rb) | copy-start | bytes 393220
  14.6 35.5 %copy-start.8 = (bf16[256,128]{1,0:T(8,128)(2,1)S(1)}, bf16[256,128]{1,0:T(8,128)(2,1)}, u32[]{:S(2)}) copy-start(bf16[256,128]{1,0:T(8,128)(2,1)} %constant.73.clone.wy) | copy-start | bytes 196612
  14.6 35.5 %copy-start.9 = (bf16[256,128]{1,0:T(8,128)(2,1)S(1)}, bf16[256,128]{1,0:T(8,128)(2,1)}, u32[]{:S(2)}) copy-start(bf16[256,128]{1,0:T(8,128)(2,1)} %constant.75.clone.ry) | copy-start | bytes 196612
  14.6 35.4 %all-to-all-start = ((f32[16,26,8,128]{3,2,1,0:T(8,128)}), f32[16,26,8,128]{3,2,1,0:T(8,128)S(1)}, u32[]{:S(2)}, u32[]{:S(2)}) async-start(f32[16,26,8,128]{3,2,1,0:T(8,128)} %pack.1), calls=%async_computation | async-start | bytes 3407872 | tf_op jit(solution)/shard_map/all_to_all | solution.py:530
  71.5 1.2 copy-start.2
  72.7 4.1 %copy-start.4 = (s32[16,8,128]{2,1,0:T(8,128)S(1)}, s32[16,8,128]{2,1,0:T(8,128)}, u32[]{:S(2)}) copy-start(s32[16,8,128]{2,1,0:T(8,128)} %idx.3) | copy-start | bytes 196612
  72.7 4.1 %copy-start.1 = (f32[9,16,8,128]{3,2,1,0:T(8,128)S(1)}, f32[9,16,8,128]{3,2,1,0:T(8,128)}, u32[]{:S(2)}) copy-start(f32[9,16,8,128]{3,2,1,0:T(8,128)} %u.3) | copy-start | bytes 1769476
  72.7 33.6 %all-to-all-start.1 = ((f32[16,24,8,128]{3,2,1,0:T(8,128)}), f32[16,24,8,128]{3,2,1,0:T(8,128)S(1)}, u32[]{:S(2)}, u32[]{:S(2)}) async-start(f32[16,24,8,128]{3,2,1,0:T(8,128)} %copy-done.2), calls=%async_computation.1 | async-start | bytes 3145728 | tf_op jit(solution)/shard_map/all_to_all | solution.py:557
  77.0 33.3 %collective-permute-start.2 = (f32[10,16,128]{2,1,0:T(8,128)S(1)}, f32[10,16,128]{2,1,0:T(8,128)S(1)}, u32[]{:S(2)}, u32[]{:S(2)}) collective-permute-start(f32[10,16,128]{2,1,0:T(8,128)S(1)} %pad_maximum_fusion), channel_id=1, source_target_pairs={{0,1},{1,2},{2,3},{3,4},{4,5},{5,6},{6,7},{7,8},{8,9},{9,10},{10,1... | collective-permute-start | bytes 245768 | tf_op jit(solution)/shard_map/ppermute | solution.py:524
  80.8 29.5 %collective-permute-start.3 = (f32[10,16,128]{2,1,0:T(8,128)S(1)}, f32[10,16,128]{2,1,0:T(8,128)S(1)}, u32[]{:S(2)}, u32[]{:S(2)}) collective-permute-start(f32[10,16,128]{2,1,0:T(8,128)S(1)} %pad_maximum_fusion.1), channel_id=1, source_target_pairs={{1,0},{2,1},{3,2},{4,3},{5,4},{6,5},{7,6},{8,7},{9,8},{10,9},{11,1... | collective-permute-start | bytes 245768 | tf_op jit(solution)/shard_map/ppermute | solution.py:525
  108.4 11.2 %collective-permute-start.4 = (f32[9,8,128]{2,1,0:T(8,128)S(1)}, f32[9,8,128]{2,1,0:T(8,128)S(1)}, u32[]{:S(2)}, u32[]{:S(2)}) collective-permute-start(f32[9,8,128]{2,1,0:T(8,128)S(1)} %get-tuple-element.31), channel_id=1, source_target_pairs={{16,0},{32,16},{48,32},{64,48},{80,64},{96,80},{112,96},{17,1},{33... | collective-permute-start | bytes 110600 | tf_op jit(solution)/shard_map/ppermute | solution.py:561
  116.7 5.3 %collective-permute-start.5 = (f32[9,8,128]{2,1,0:T(8,128)S(1)}, f32[9,8,128]{2,1,0:T(8,128)S(1)}, u32[]{:S(2)}, u32[]{:S(2)}) collective-permute-start(f32[9,8,128]{2,1,0:T(8,128)S(1)} %get-tuple-element.32), channel_id=1, source_target_pairs={{0,16},{16,32},{32,48},{48,64},{64,80},{80,96},{96,112},{1,17},{17... | collective-permute-start | bytes 110600 | tf_op jit(solution)/shard_map/ppermute | solution.py:562

commit v2 on v1

v2 whole, which is shorter than its diff:
```python
import jax
import jax.numpy as jnp
import ml_dtypes
import numpy as np
from jax import lax
from jax.experimental import pallas as pl
from jax.experimental.pallas import tpu as pltpu
from jax.sharding import PartitionSpec as P

F32 = jnp.float32
S = 9
CH = 10
CX = 16
CY = 8
DEV = 16
W = 18
PITCH = 24
FRAME = W * W
BLK = CY * W
GF = 23
NF = GF + 3
GB = 21
NB = GB + 3
CLS = 9
VMEM = pl.BlockSpec(memory_space=pltpu.VMEM)
SMEM = pl.BlockSpec(memory_space=pltpu.SMEM)
ANY = pl.BlockSpec(memory_space=pl.ANY)


def weights():
    wf = np.zeros((128, 384), np.float32)
    rb = np.zeros((2, 128, 128), np.float32)
    for lane in range(128):
        q, fz = divmod(lane, 32)
        k, z = 1 + q // 2, fz // 2 + 1
        sy, sz = (0.125 if q % 2 else -0.125), (0.125 if fz % 2 else -0.125)
        wf[k * W + z, lane] += 1.0
        wf[(k + 1) * W + z, lane] += sy
        wf[(k - 1) * W + z, lane] -= sy
        wf[k * W + z + 1, lane] += sz
        wf[k * W + z - 1, lane] -= sz
        wf[k * W + z, 256 + lane] = 1.0
        rb[0, lane, (q // 2) * W + z] = 0.125
        if fz == 0:
            wf[k * W, 128 + lane] = 1.0
            rb[1, lane, (q // 2) * W] = 0.125
        if fz == 31:
            wf[k * W + W - 1, 128 + lane] = 1.0
            rb[1, lane, (q // 2) * W + W - 1] = 0.125
    wy = np.zeros((128, 128), np.float32)
    ry = np.zeros((128, 128), np.float32)
    for fz in range(32):
        z = fz // 2 + 1
        wy[z, 96 + fz] = 1.0
        wy[W + z, fz] = 1.0
        ry[fz, z] = 0.125
        ry[96 + fz, 50 + z] = 0.125
    wz = np.zeros((128, 256), np.float32)
    for lane in range(128):
        if lane % 32:
            wz[lane - 1, lane] = 1.0
        if lane % 32 != 31:
            wz[lane + 1, 128 + lane] = 1.0
    twice = lambda m: np.concatenate([m, m], 0).astype(ml_dtypes.bfloat16)
    return twice(np.concatenate([wf, wy, wz, ry, rb[0], rb[1]], 1))


def lanes(shape):
    return lax.broadcasted_iota(jnp.int32, shape, 1)


def mod128(x):
    return lax.bitwise_and(x, 127)


def halves(x):
    hi = x.astype(jnp.bfloat16)
    return hi, (x - hi.astype(F32)).astype(jnp.bfloat16)


def pick(tab, index):
    rows = index.shape[0]
    parts = [
        jnp.take_along_axis(tab, index[r : r + 8], axis=1, mode="promise_in_bounds") for r in range(0, rows, 8)
    ]
    return parts[0] if len(parts) == 1 else jnp.concatenate(parts, 0)


def where_is(roots, row):
    first = roots[row, 1] - 1
    owner = lax.shift_right_logical(first, 3)
    return owner, first - 8 * owner, roots[row, 2] - 1


def slab_kernel(u, idx, slab, ubuf, ibuf, sems):
    copies = [pltpu.make_async_copy(u.at[s], ubuf.at[s], sems.at[s]) for s in range(S)]
    copies.append(pltpu.make_async_copy(idx, ibuf, sems.at[S]))
    for copy in copies:
        copy.start()
    for s in range(S):
        copies[s].wait()
        for x in range(CX):
            slab[pl.ds(s * CX + x, 8, stride=CH * CX), :] = ubuf[s, x]
    copies[S].wait()
    for x in range(CX):
        slab[pl.ds(S * CX + x, 8, stride=CH * CX), :] = (ibuf[x] + 1).astype(F32)


def pack_kernel(roots, slab, lo, hi, out, halo):
    grp, me = lax.axis_index("grp"), lax.axis_index("dev")
    for c in range(CH):
        halo[pl.ds(c, 8, stride=24), :] = lo[c]
        halo[pl.ds(CH + c, 8, stride=24), :] = hi[c]
    for r in range(2 * CH, 24):
        halo[pl.ds(r, 8, stride=24), :] = jnp.zeros((8, 128), F32)
    lane = lanes((8, 128))

    def one(p, carry):
        owner, y0, z0 = where_is(roots, grp * DEV + p)

        @pl.when(jnp.logical_and(me >= owner, 8 * (me - owner) - y0 < W))
        def _():
            rest = None
            for g in range(GF):
                main = None
                for y in range(8):
                    if g < 2 * CH:
                        rows = slab[y * CH * CX + 8 * g : y * CH * CX + 8 * g + 8, :]
                    else:
                        rows = halo[y * 24 + 8 * (g - 2 * CH) : y * 24 + 8 * (g - 2 * CH) + 8, :]
                    moved = pltpu.roll(rows, mod128(W * y + 128 - z0), 1)
                    main = moved if y == 0 else jnp.where(lane >= W * y, moved, main)
                out[p, g] = main
                slot = 16 * (g % 8)
                moved = pltpu.roll(rows, mod128(126 + slot + 128 - z0), 1)
                rest = moved if slot == 0 else jnp.where(lane >= slot, moved, rest)
                if slot == 112 or g == GF - 1:
                    out[p, GF + g // 8] = rest

        return carry

    lax.fori_loop(0, DEV, one, 0)


def coarse_kernel(u, idx, lo, hi, ylo, yhi, ptab, _, out, cls, px, pyl, pyh, pzl, pzh):
    lane = lanes((8, 128))
    sub = lax.broadcasted_iota(jnp.int32, (8, 128), 0)
    cls[0] = lo[S].astype(jnp.int32)
    cls[CX + 1] = hi[S].astype(jnp.int32)
    for x in range(CX):
        cls[x + 1] = idx[x] + 1

    def below_y(a, row):
        return jnp.where(sub == 0, jnp.broadcast_to(row, (8, 128)), pltpu.roll(a, 1, 0))

    def above_y(a, row):
        return jnp.where(sub == 7, jnp.broadcast_to(row, (8, 128)), pltpu.roll(a, 7, 0))

    def below_z(a):
        return jnp.where(lane == 0, jnp.zeros_like(a), pltpu.roll(a, 1, 1))

    def above_z(a):
        return jnp.where(lane == 127, jnp.zeros_like(a), pltpu.roll(a, 127, 1))

    for x in range(CX + 1):
        px[x] = cls[x + 1] * CLS + cls[x]
    for x in range(CX):
        c = cls[x + 1]
        pyl[x] = c * CLS + below_y(c, ylo[S, x : x + 1, :].astype(jnp.int32))
        pyh[x] = c * CLS + above_y(c, yhi[S, x : x + 1, :].astype(jnp.int32))
        pzl[x] = c * CLS + below_z(c)
        pzh[x] = c * CLS + above_z(c)

    def species(s, carry):
        tab = jnp.broadcast_to(0.5 * ptab[pl.ds(s, 1), :], (8, 128))
        center = u[s, 0]
        flux = pick(tab, px[0]) * (center - lo[s])
        for x in range(CX):
            after = u[s, x + 1] if x + 1 < CX else hi[s]
            next_flux = pick(tab, px[x + 1]) * (after - center)
            total = next_flux - flux
            total = total + pick(tab, pyl[x]) * (below_y(center, ylo[s, x : x + 1, :]) - center)
            total = total + pick(tab, pyh[x]) * (above_y(center, yhi[s, x : x + 1, :]) - center)
            total = total + pick(tab, pzl[x]) * (below_z(center) - center)
            total = total + pick(tab, pzh[x]) * (above_z(center) - center)
            out[s, x] = center + total
            center, flux = after, next_flux
        return carry

    lax.fori_loop(0, S, species, 0)


def patch_kernel(
    roots, table, recv, fidx, tabs, _ylo, _yhi,
    fine, back,
    fr, fc, up, upy, da, ua, ub, uc, uy, dy, zg, dz, fx, fyl, fyh, fzl, fzh, fb, fs, gc, zr, yr, b1, b2, by, dl, mk, hb,
):
    grp, me = lax.axis_index("grp"), lax.axis_index("dev")
    owner, y0, _ = where_is(roots, grp * DEV + me)
    lane = lanes((8, 128))
    lane_all = lanes((2 * S * PITCH, 128))
    start = [BLK * k - W * y0 for k in range(4)]
    source = [jnp.minimum(owner + k, DEV - 1) for k in range(4)]
    zero8 = jnp.zeros((8, 128), F32)

    for t in range(3):
        for c in range(S):
            fr[t, c, 16:24] = zero8
        fc[t, 16:24] = zero8
    for g in range(GF):
        slot = 16 * (g % 8)
        main = [pltpu.roll(recv[source[k], g], mod128(start[k] + 256), 1) for k in range(4)]
        rest = [pltpu.roll(recv[source[k], GF + g // 8], mod128(start[k] + 384 - slot), 1) for k in range(3)]

        def over(t, piece, at, below):
            return jnp.where(lane >= at - 128 * t, piece, below)

        tile0 = over(0, main[1], start[1], over(0, rest[0], start[0] + 128, main[0]))
        tile1 = over(1, main[1], start[1], rest[0])
        tile1 = over(1, main[2], start[2], over(1, rest[1], start[1] + 128, tile1))
        tile2 = over(2, main[2], start[2], over(2, rest[1], start[1] + 128, main[1]))
        tile2 = over(2, main[3], start[3], over(2, rest[2], start[2] + 128, tile2))
        tile2 = jnp.where(lane < FRAME - 256, tile2, 0.0)
        for t, tile in enumerate((tile0, tile1, tile2)):
            if g < 2 * S:
                fr[t, g // 2, 1 + 8 * (g % 2) : 9 + 8 * (g % 2)] = tile
            elif g < 2 * CH:
                fc[t, 1 + 8 * (g % 2) : 9 + 8 * (g % 2)] = tile
            else:
                for i in range(8):
                    q = 8 * (g - 2 * CH) + i
                    if q < 2 * CH:
                        at = 0 if q < CH else W - 1
                        if q % CH < S:
                            fr[t, q % CH, at : at + 1] = tile[i : i + 1]
                        else:
                            fc[t, at : at + 1] = tile[i : i + 1]

    for t in range(3):
        for r in range(0, PITCH, 8):
            classes = fc[t, r : r + 8]
            masks = [classes == k + 1.0 for k in range(8)]
            for s in range(S):
                value = zero8
                for k in range(8):
                    value = jnp.where(masks[k], 0.08 * table[k, s], value)
                fr[t, S + s, r : r + 8] = value

    rows_all = 2 * S * PITCH

    def spread(values, weight):
        hi, lo = halves(values)
        return jnp.dot(jnp.concatenate([hi, lo], 1), weight, preferred_element_type=F32)

    for j in range(8):
        t, off = divmod(2 * W * j, 128)
        values = fr[t].reshape(rows_all, 128)
        if off:
            values = pltpu.roll(values, 128 - off, 1)
            if off + 4 * W > 128:
                after = pltpu.roll(fr[t + 1].reshape(rows_all, 128), 128 - off, 1)
                values = jnp.where(lane_all < 128 - off, values, after)
        result = spread(values, tabs[:, 0:384])
        for b in range(3):
            up[3 * j + b] = result[:, 128 * b : 128 * b + 128].reshape(2 * S, PITCH, 128)
    ends = jnp.where(
        lane_all < W,
        pltpu.roll(fr[2].reshape(rows_all, 128), 78, 1),
        pltpu.roll(fr[0].reshape(rows_all, 128), W, 1),
    )
    upy[...] = spread(ends, tabs[:, 384:512]).reshape(2 * S, PITCH, 128)

    for c in range(CH):
        for j in range(8):
            b1[j, c, 16:24] = zero8
            b2[j, c, 0:8] = zero8
            b2[j, c, 16:24] = zero8
            if c == S:
                b1[j, c, 0:8] = zero8
                b1[j, c, 8:16] = zero8
                b2[j, c, 8:16] = zero8
        by[c, 0:8] = zero8
        by[c, 16:24] = zero8
        if c == S:
            by[c, 8:16] = zero8
    for j in range(8):
        da[j, 40:48] = zero8

    lane32 = lanes((32, 128))
    z_low = lax.bitwise_and(lane32, 31) == 0
    z_top = lax.bitwise_and(lane32, 31) == 31
    inner = slice(8, 40)

    def twice(ref, at, values):
        ref[at + (pl.ds(0, CX, stride=2), slice(None))] = values
        ref[at + (pl.ds(1, CX, stride=2), slice(None))] = values

    def z_neighbours(tiles):
        result = spread(jnp.concatenate(tiles, 0), tabs[:, 512:768])
        return [(result[32 * j : 32 * j + 32, :128], result[32 * j : 32 * j + 32, 128:]) for j in range(8)]

    def y_neighbours(tiles, ghost):
        down = [pltpu.roll(a, 32, 1) for a in tiles]
        above = [pltpu.roll(a, 96, 1) for a in tiles]
        low = [jnp.where(lane32 < 32, down[j - 1] if j else ghost, down[j]) for j in range(8)]
        top = [jnp.where(lane32 < 96, above[j], above[j + 1] if j < 7 else ghost) for j in range(8)]
        return low, top

    def change(j, src, u, low, top, z):
        value = fx[j, 0:32] * src[j, 7:39] + fx[j, 1:33] * src[j, 9:41]
        value = value + (fyl[j] * low[j] + fyh[j] * top[j])
        value = value + (fzl[j] * z[j][0] + fzh[j] * z[j][1])
        return u + (value + (gc[j] - fs[j] * u))

    def species(s, carry):
        for j in range(8):
            core, dcore = up[3 * j + 2, s], up[3 * j + 2, S + s]
            slope = 0.125 * (up[3 * j + 2, s, 2 : CX + 2] - up[3 * j + 2, s, 0:CX])
            middle = up[3 * j, s, 1 : CX + 1]
            ua[j, pl.ds(8, CX, stride=2), :] = middle - slope
            ua[j, pl.ds(9, CX, stride=2), :] = middle + slope
            for ref, values in ((ua, core), (ub, core), (da, dcore)):
                ref[j, 7:8] = values[0:1]
                ref[j, 40:41] = values[W - 1 : W]
            twice(zg, (j,), up[3 * j + 1, s, 1 : CX + 1])
            twice(dz, (j,), up[3 * j + 1, S + s, 1 : CX + 1])
        twice(uy, (), upy[s, 1 : CX + 1])
        twice(dy, (), upy[S + s, 1 : CX + 1])

        known = [0.08 * table[k, s] for k in range(8)]
        diffs = []
        for j in range(8):
            index = fidx[0, :, 128 * j : 128 * j + 128]
            one, two, four = [lax.bitwise_and(index, bit) != 0 for bit in (1, 2, 4)]
            level = [jnp.where(one, known[k + 1], known[k]) for k in (0, 2, 4, 6)]
            level = [jnp.where(two, level[1], level[0]), jnp.where(two, level[3], level[2])]
            diffs.append(jnp.where(four, level[1], level[0]))
            da[j, inner] = diffs[j]
        z = z_neighbours(diffs)
        low, top = y_neighbours(diffs, dy[...])
        for j in range(8):
            d = diffs[j]
            fx[j] = da[j, 8:48] + da[j, 7:47]
            fyl[j] = d + low[j]
            fyh[j] = d + top[j]
            ghost = dz[j]
            low_z = d + jnp.where(z_low, ghost, z[j][0])
            top_z = d + jnp.where(z_top, ghost, z[j][1])
            fzl[j] = low_z
            fzh[j] = top_z
            edge = jnp.where(z_low, low_z, jnp.where(z_top, top_z, 0.0))
            fb[j] = edge
            gc[j] = edge * zg[j]
            fs[j] = ((fx[j, 0:32] + fx[j, 1:33]) + (fyl[j] + fyh[j])) + (low_z + top_z)

        first = [ua[j, inner] for j in range(8)]
        z = z_neighbours(first)
        ghost = uy[...]
        low, top = y_neighbours(first, ghost)
        for j in range(8):
            ub[j, inner] = change(j, ua, first[j], low, top, z)
        second = [ub[j, inner] for j in range(8)]
        z = z_neighbours(second)
        low, top = y_neighbours(second, ghost)
        for j in range(8):
            both = ua[j, inner] + second[j]
            value = change(j, ub, second[j], low, top, z)
            uc[j] = value
            fine[0, s, :, 128 * j : 128 * j + 128] = value
            zr[j] = fb[j] * both - 2.0 * gc[j]
            for at, row, out_row in ((0, 8, 0), (32, 39, W - 1)):
                outer = 7 if row == 8 else 40
                total = ua[j, row : row + 1] + ub[j, row : row + 1] - 2.0 * ua[j, outer : outer + 1]
                b1[j, s, out_row : out_row + 1] = fx[j, at : at + 1] * total
            if j == 0:
                yr[...] = jnp.where(lane32 < 32, fyl[0] * (both - 2.0 * ghost), 0.0)
            if j == 7:
                yr[...] = jnp.where(lane32 < 96, yr[...], fyh[7] * (both - 2.0 * ghost))
        for j in range(8):
            b1[j, s, 1 : CX + 1] = uc[j, pl.ds(0, CX, stride=2), :] + uc[j, pl.ds(1, CX, stride=2), :]
            b2[j, s, 1 : CX + 1] = zr[j, pl.ds(0, CX, stride=2), :] + zr[j, pl.ds(1, CX, stride=2), :]
        by[s, 1 : CX + 1] = yr[pl.ds(0, CX, stride=2), :] + yr[pl.ds(1, CX, stride=2), :]
        return carry

    lax.fori_loop(0, S, species, 0)

    lane_out = lanes((CH * PITCH, 128))
    delta = [jnp.zeros((CH * PITCH, 128), F32) for _ in range(3)]
    for j in range(8):
        t, off = divmod(2 * W * j + W, 128)
        sums = spread(b1[j].reshape(CH * PITCH, 128), tabs[:, 896:1024])
        sums = pltpu.roll(sums + spread(b2[j].reshape(CH * PITCH, 128), tabs[:, 1024:1152]), off, 1)
        if off + 2 * W > 128:
            delta[t] = delta[t] + jnp.where(lane_out >= off, sums, 0.0)
            delta[t + 1] = delta[t + 1] + jnp.where(lane_out < off, sums, 0.0)
        else:
            delta[t] = delta[t] + sums
    sums = spread(by[...].reshape(CH * PITCH, 128), tabs[:, 768:896])
    delta[0] = delta[0] + jnp.where(lane_out < W, sums, 0.0)
    delta[2] = delta[2] + jnp.where(lane_out >= 50, sums, 0.0)
    for t in range(3):
        dl[t] = delta[t].reshape(CH, PITCH, 128)

    rows3 = 3 * PITCH
    lane_c = lanes((rows3, 128))
    lane24 = lanes((PITCH, 128))
    row24 = lax.broadcasted_iota(jnp.int32, (PITCH, 128), 0)

    def within(a, top):
        return jnp.logical_and(a >= 1, a <= top)

    def shifted_down(tiles, by_lanes):
        moved = [pltpu.roll(a, by_lanes, 1) for a in tiles]
        return [jnp.where(lane_c < by_lanes, moved[t - 1], moved[t]) for t in range(3)]

    def shifted_up(tiles, by_lanes):
        moved = [pltpu.roll(a, 128 - by_lanes, 1) for a in tiles]
        return [jnp.where(lane_c < 128 - by_lanes, moved[t], moved[(t + 1) % 3]) for t in range(3)]

    for t in range(3):
        cell = lane24 + 128 * t
        y = lax.shift_right_logical(cell * 3641, 16)
        z = cell - W * y
        inside = [within(row24, CX), within(y, CX), within(z, CX)]
        wider = [within(row24, CX + 1), within(y, CX + 1), within(z, CX + 1)]
        every = lambda a, b, c: jnp.logical_and(a, jnp.logical_and(b, c))
        faces = [every(*(wider[n] if n == axis else inside[n] for n in range(3))) for axis in range(3)]
        for i in range(3):
            for axis in range(3):
                mk[3 * axis + t, 24 * i : 24 * i + 24] = jnp.where(faces[axis], 0.5, 0.0)
            mk[9 + t, 24 * i : 24 * i + 24] = jnp.where(every(*inside), 1.0, 0.0)

    def coarse(i, carry):
        u = [fr[t, pl.ds(3 * i, 3)].reshape(rows3, 128) for t in range(3)]
        d = [fr[t, pl.ds(S + 3 * i, 3)].reshape(rows3, 128) for t in range(3)]
        below = [[pltpu.roll(a, 1, 0) for a in v] for v in (u, d)]
        flux = [[mk[t] * (d[t] + below[1][t]) * (u[t] - below[0][t]) for t in range(3)]]
        for axis, step in ((1, W), (2, 1)):
            down = [shifted_down(v, step) for v in (u, d)]
            flux.append([mk[3 * axis + t] * (d[t] + down[1][t]) * (u[t] - down[0][t]) for t in range(3)])
        up_y, up_z = shifted_up(flux[1], W), shifted_up(flux[2], 1)
        for t in range(3):
            total = pltpu.roll(flux[0][t], rows3 - 1, 0) - flux[0][t]
            total = total + (up_y[t] - flux[1][t]) + (up_z[t] - flux[2][t])
            old = dl[t, pl.ds(3 * i, 3)].reshape(rows3, 128)
            dl[t, pl.ds(3 * i, 3)] = (old - (mk[9 + t] * u[t] + total)).reshape(3, PITCH, 128)
        return carry

    lax.fori_loop(0, S // 3, coarse, 0)

    for t in range(3):
        hb[t, 16:24] = zero8
        for s in range(S):
            hb[t, s : s + 1] = dl[t, s, 0:1]
            hb[t, S + s : S + s + 1] = dl[t, s, W - 1 : W]

    def group_tiles(g):
        if g < 2 * S:
            return [dl[t, g // 2, 1 + 8 * (g % 2) : 9 + 8 * (g % 2)] for t in range(3)]
        return [hb[t, 8 * (g - 2 * S) : 8 * (g - 2 * S) + 8] for t in range(3)]

    main_from = ([0], [0, 1, 2], [1, 2, 3], [2, 3])
    rest_from = ([0, 1], [1, 2], [2, 3], [])
    for k in range(4):

        @pl.when(8 * k - y0 < W)
        def _(k=k):
            rest = None
            for g in range(GB):
                tiles = group_tiles(g) + [None]
                slot = 16 * (g % 8)

                def cut(number, amount, at):
                    value = zero8
                    for t in number:
                        piece = zero8 if tiles[t] is None else pltpu.roll(tiles[t], mod128(amount), 1)
                        value = jnp.where(lane >= 128 * t - at, piece, value)
                    return value

                back[owner + k, g] = cut(main_from[k], 512 - start[k], start[k])
                part = cut(rest_from[k], 512 - start[k] + slot, start[k] + 128 - slot)
                rest = part if slot == 0 else jnp.where(lane >= slot, part, rest)
                if slot == 112 or g == GB - 1:
                    back[owner + k, GB + g // 8] = rest


def add_windows(roots, arrived, acc, groups, stride):
    grp, me = lax.axis_index("grp"), lax.axis_index("dev")
    lane = lanes((8, 128))

    def clear(i, carry):
        acc[pl.ds(pl.multiple_of(8 * i, 8), 8), :] = jnp.zeros((8, 128), F32)
        return carry

    lax.fori_loop(0, stride, clear, 0)

    def one(p, carry):
        owner, y0, z0 = where_is(roots, grp * DEV + p)

        @pl.when(jnp.logical_and(me >= owner, 8 * (me - owner) - y0 < W))
        def _():
            window = jnp.logical_and(lane >= z0, lane < z0 + W)
            for number, g in enumerate(groups):
                main, rest = arrived[p, g], arrived[p, GB + g // 8]
                for y in range(8):
                    moved = pltpu.roll(main, mod128(z0 + 128 - W * y), 1)
                    if y == 7:
                        tail = pltpu.roll(rest, mod128(z0 + 2 + 128 - 16 * (g % 8)), 1)
                        moved = jnp.where(lane < z0 + 2, moved, tail)
                    rows = slice(y * stride + 8 * number, y * stride + 8 * number + 8)
                    acc[rows, :] = acc[rows, :] + jnp.where(window, moved, 0.0)

        return carry

    lax.fori_loop(0, DEV, one, 0)


def halo_kernel(roots, arrived, _, low, top, acc):
    add_windows(roots, arrived, acc, range(2 * S, GB), 24)
    for s in range(S):
        low[s] = acc[pl.ds(s, 8, stride=24), :]
        top[s] = acc[pl.ds(S + s, 8, stride=24), :]


def add_kernel(roots, arrived, coarse_one, below, above, out, acc):
    add_windows(roots, arrived, acc, range(2 * S), S * CX)
    for s in range(S):
        for x in range(CX):
            value = coarse_one[s, x] + acc[pl.ds(s * CX + x, 8, stride=S * CX), :]
            if x == 0:
                value = value + below[s]
            if x == CX - 1:
                value = value + above[s]
            out[s, x] = value


def call(kernel, outs, ins, scratch, name, mib):
    return pl.pallas_call(
        kernel,
        out_shape=outs,
        in_specs=ins,
        out_specs=jax.tree.map(lambda _: VMEM, outs),
        scratch_shapes=scratch,
        compiler_params=pltpu.CompilerParams(vmem_limit_bytes=mib * 1024 * 1024),
        name=name,
    )


def shape(*dims):
    return jax.ShapeDtypeStruct(dims, F32)


def body(coarse_state, coef_index, coef_table, patch_root, fine_index):
    ends_g, ends_d = lax.axis_size("grp") - 1, lax.axis_size("dev") - 1
    up_g, down_g = [(i, i + 1) for i in range(ends_g)], [(i + 1, i) for i in range(ends_g)]
    up_d, down_d = [(i, i + 1) for i in range(ends_d)], [(i + 1, i) for i in range(ends_d)]
    known = jnp.concatenate([jnp.zeros((1, S), F32), coef_table], 0)
    pairs = (0.08 * (known[:, None] + known[None, :])).reshape(CLS * CLS, S)
    ptab = jnp.pad(pairs.T, ((0, 0), (0, 128 - CLS * CLS)))

    def plane(u, c):
        return jnp.concatenate([u, (c[None] + 1).astype(F32)], 0)

    x_lo = lax.ppermute(plane(coarse_state[:, CX - 1], coef_index[CX - 1]), "grp", up_g)
    x_hi = lax.ppermute(plane(coarse_state[:, 0], coef_index[0]), "grp", down_g)
    y_lo = lax.ppermute(plane(coarse_state[:, :, CY - 1], coef_index[:, CY - 1]), "dev", up_d)
    y_hi = lax.ppermute(plane(coarse_state[:, :, 0], coef_index[:, 0]), "dev", down_d)

    slab = call(
        slab_kernel,
        shape(CY * CH * CX, 128),
        [ANY] * 2,
        [
            pltpu.VMEM((S, CX, CY, 128), F32),
            pltpu.VMEM((CX, CY, 128), jnp.int32),
            pltpu.SemaphoreType.DMA((CH,)),
        ],
        "slab",
        8,
    )(coarse_state, coef_index)
    blocks = call(
        pack_kernel, shape(DEV, NF, 8, 128), [SMEM] + [VMEM] * 3, [pltpu.VMEM((8 * 24, 128), F32)], "pack", 8
    )(patch_root, slab, x_lo, x_hi)
    received = lax.all_to_all(blocks, "dev", split_axis=0, concat_axis=0, tiled=True)
    i32 = lambda *dims: pltpu.VMEM(dims, jnp.int32)
    f32 = lambda *dims: pltpu.VMEM(dims, F32)
    fine_state, corrections = call(
        patch_kernel,
        (shape(1, S, 32, 1024), shape(DEV, NB, 8, 128)),
        [SMEM, SMEM] + [VMEM] * 3 + [ANY] * 2,
        [
            f32(3, 2 * S, PITCH, 128), f32(3, PITCH, 128), f32(24, 2 * S, PITCH, 128), f32(2 * S, PITCH, 128),
            f32(8, 48, 128), f32(8, 48, 128), f32(8, 48, 128), f32(8, 32, 128),
            f32(32, 128), f32(32, 128), f32(8, 32, 128), f32(8, 32, 128),
            f32(8, 40, 128), f32(8, 32, 128), f32(8, 32, 128), f32(8, 32, 128), f32(8, 32, 128),
            f32(8, 32, 128), f32(8, 32, 128), f32(8, 32, 128), f32(8, 32, 128), f32(32, 128),
            f32(8, CH, PITCH, 128), f32(8, CH, PITCH, 128), f32(CH, PITCH, 128),
            f32(3, CH, PITCH, 128), f32(12, 3 * PITCH, 128), f32(3, 24, 128),
        ],
        "patch",
        32,
    )(patch_root, coef_table, received, fine_index, jnp.asarray(weights()), y_lo, y_hi)
    arrived = lax.all_to_all(corrections, "dev", split_axis=0, concat_axis=0, tiled=True)
    coarse_one = call(
        coarse_kernel,
        shape(S, CX, CY, 128),
        [VMEM] * 7 + [ANY],
        [i32(CX + 2, 8, 128), i32(CX + 1, 8, 128)] + [i32(CX, 8, 128)] * 4,
        "coarse",
        8,
    )(coarse_state, coef_index, x_lo, x_hi, y_lo, y_hi, ptab, corrections)
    low, top = call(
        halo_kernel, (shape(S, CY, 128), shape(S, CY, 128)), [SMEM, VMEM, ANY], [f32(8 * 24, 128)], "halo", 8
    )(patch_root, arrived, coarse_one)
    from_above = lax.ppermute(low, "grp", down_g)
    from_below = lax.ppermute(top, "grp", up_g)
    coarse_new = call(
        add_kernel, shape(S, CX, CY, 128), [SMEM] + [VMEM] * 4, [f32(8 * S * CX, 128)], "add", 8
    )(patch_root, arrived, coarse_one, from_below, from_above)
    return coarse_new, fine_state


def solution(mesh):
    return jax.shard_map(
        body,
        mesh=mesh,
        in_specs=(
            P(None, "grp", "dev", None),
            P("grp", "dev", None),
            P(),
            P(),
            P(("grp", "dev"), None, None),
        ),
        out_specs=(P(None, "grp", "dev", None), P(("grp", "dev"), None, None, None)),
        check_vma=False,
    )
```

time: 124 us -> 112 us (0.903)
  the two profiles are of different devices: /device:TPU:32 before, /device:TPU:1 now
where the time goes in v2:
time: 112 us; the launch traced here: 111 us
  waiting for transfers between devices  42.8 us (38%)
  starting transfers between devices  36.6 us (33%)
  Pallas kernels  26.1 us (23%)
  local copies, waits for them, and re-layouts  4.09 us (4%)
    all_to_all x1, waiting for transfers between devices, body(): lax.all_to_all(corrections, 'dev', split_axis=0, concat_axis=0, tiled=True)  19.3 us
    ppermute x1, waiting for transfers between devices, body(): lax.ppermute(plane(coarse_state[:, :, CY - 1], coef_index[:, CY - 1]), 'd...  14.3 us
    pallas_call x1, Pallas kernels, body(): call(patch_kernel, (shape(1, S, 32, 1024), shape(DEV, NB, 8, 128)), [SMEM...  11.9 us
    ppermute x1, starting transfers between devices, body(): from_below = lax.ppermute(top, 'grp', up_g)  11.3 us
    all_to_all x1, starting transfers between devices, body(): lax.all_to_all(blocks, 'dev', split_axis=0, concat_axis=0, tiled=True)  7.72 us
    ppermute x1, starting transfers between devices, body(): lax.ppermute(plane(coarse_state[:, CX - 1], coef_index[CX - 1]), 'grp', u...  4.92 us
    all_to_all x1, starting transfers between devices, body(): lax.all_to_all(corrections, 'dev', split_axis=0, concat_axis=0, tiled=True)  4.21 us
    pallas_call x1, Pallas kernels, body(): call(add_kernel, shape(S, CX, CY, 128), [SMEM] + [VMEM] * 4, [f32(8 * S *...  4 us
  transfers between devices with their start and end apart: 8, of which 5 were waited for; matrix products, arithmetic and copies ran while one was open for 1% of the time, Pallas kernels for 4%

profile of v2, /device:TPU:1, one launch (start us, length us, event | category | flops | bytes accessed | tf_op | source)
XLA Modules:
  0.0 111.3 jit_solution(12946830830930640067)
XLA Ops:
  0.6 0.0 copy-start.13
  0.6 0.8 slice_bitcast_fusion
  1.4 0.7 add_convert_fusion
  2.2 4.9 %collective-permute-start = (f32[10,8,128]{2,1,0:T(8,128)S(1)}, f32[10,8,128]{2,1,0:T(8,128)S(1)}, u32[]{:S(2)}, u32[]{:S(2)}) collective-permute-start(f32[10,8,128]{2,1,0:T(8,128)S(1)} %pad_maximum_fusion.2), channel_id=1, source_target_pairs={{0,16},{16,32},{32,48},{48,64},{64,80},{80,96},{96,112},{1,17},{17... | collective-permute-start | bytes 122888 | tf_op jit(solution)/shard_map/ppermute | solution.py:564
  7.1 1.9 %collective-permute-start.1 = (f32[10,8,128]{2,1,0:T(8,128)S(1)}, f32[10,8,128]{2,1,0:T(8,128)S(1)}, u32[]{:S(2)}, u32[]{:S(2)}) collective-permute-start(f32[10,8,128]{2,1,0:T(8,128)S(1)} %pad_maximum_fusion.3), channel_id=1, source_target_pairs={{16,0},{32,16},{48,32},{64,48},{80,64},{96,80},{112,96},{17,1},{33... | collective-permute-start | bytes 122888 | tf_op jit(solution)/shard_map/ppermute | solution.py:565
  9.0 0.0 copy-start
  9.0 1.1 copy-done
  10.1 0.0 copy-start.3
  10.1 0.8 copy-done.3
  10.9 1.3 %slab.1 = f32[1280,128]{1,0:T(8,128)S(1)} custom-call(f32[9,16,8,128]{3,2,1,0:T(8,128)S(1)} %copy-done, s32[16,8,128]{2,1,0:T(8,128)S(1)} %copy-done.3), custom_call_target="tpu_custom_call" | custom-call | tf_op jit(solution)/shard_map/slab/pallas_call | solution.py:569
  12.3 0.0 copy-done.13
  12.3 0.1 copy.19.roots
  12.4 0.0 collective-permute-done.lo
  12.4 0.0 copy-start.7
  12.4 0.0 collective-permute-done.1.hi
  12.4 0.0 copy-start.9
  12.4 3.4 %pack.1 = f32[16,26,8,128]{3,2,1,0:T(8,128)} custom-call(s32[128,3]{1,0:T(8,128)S(1)} %copy.19.roots, f32[1280,128]{1,0:T(8,128)S(1)} %slab.1, f32[10,8,128]{2,1,0:T(8,128)S(1)} %collective-permute-done.lo, f32[10,8,128]{2,1,0:T(8,128)S(1)} %collective-permute-done.1.hi), custom_call_target="tpu_custom_call" | custom-call | tf_op jit(solution)/shard_map/pack/pallas_call | solution.py:581
  15.9 0.0 copy-start.4
  15.9 0.0 copy-start.1
  15.9 0.0 copy-start.2
  15.9 0.0 copy-start.11
  15.9 0.0 copy-start.12
  15.9 0.0 copy-done.7
  15.9 0.0 copy-done.9
  15.9 7.7 %all-to-all-start = ((f32[16,26,8,128]{3,2,1,0:T(8,128)}), f32[16,26,8,128]{3,2,1,0:T(8,128)S(1)}, u32[]{:S(2)}, u32[]{:S(2)}) async-start(f32[16,26,8,128]{3,2,1,0:T(8,128)} %pack.1), calls=%async_computation | async-start | bytes 3407872 | tf_op jit(solution)/shard_map/all_to_all | solution.py:584
  23.6 0.0 copy-done.4
  23.7 0.0 copy-done.1
  23.7 0.1 fusion
  23.8 3.3 %collective-permute-start.2 = (f32[10,16,128]{2,1,0:T(8,128)S(1)}, f32[10,16,128]{2,1,0:T(8,128)S(1)}, u32[]{:S(2)}, u32[]{:S(2)}) collective-permute-start(f32[10,16,128]{2,1,0:T(8,128)S(1)} %pad_maximum_fusion), channel_id=1, source_target_pairs={{0,1},{1,2},{2,3},{3,4},{4,5},{5,6},{6,7},{7,8},{8,9},{9,10},{10,1... | collective-permute-start | bytes 245768 | tf_op jit(solution)/shard_map/ppermute | solution.py:566
  27.1 1.3 %collective-permute-start.3 = (f32[10,16,128]{2,1,0:T(8,128)S(1)}, f32[10,16,128]{2,1,0:T(8,128)S(1)}, u32[]{:S(2)}, u32[]{:S(2)}) collective-permute-start(f32[10,16,128]{2,1,0:T(8,128)S(1)} %pad_maximum_fusion.1), channel_id=1, source_target_pairs={{1,0},{2,1},{3,2},{4,3},{5,4},{6,5},{7,6},{8,7},{9,8},{10,9},{11,1... | collective-permute-start | bytes 245768 | tf_op jit(solution)/shard_map/ppermute | solution.py:567
  28.4 14.3 %collective-permute-done.2._ylo.ylo = f32[10,16,128]{2,1,0:T(8,128)S(1)} collective-permute-done((f32[10,16,128]{2,1,0:T(8,128)S(1)}, f32[10,16,128]{2,1,0:T(8,128)S(1)}, u32[]{:S(2)}, u32[]{:S(2)}) %collective-permute-start.2) | collective-permute-done | bytes 81952 | tf_op jit(solution)/shard_map/ppermute | solution.py:566
  42.7 2.4 %collective-permute-done.3._yhi.yhi = f32[10,16,128]{2,1,0:T(8,128)S(1)} collective-permute-done((f32[10,16,128]{2,1,0:T(8,128)S(1)}, f32[10,16,128]{2,1,0:T(8,128)S(1)}, u32[]{:S(2)}, u32[]{:S(2)}) %collective-permute-start.3) | collective-permute-done | bytes 81952 | tf_op jit(solution)/shard_map/ppermute | solution.py:567
  45.1 0.0 copy-start.5
  45.1 3.5 %all-to-all-done.recv = f32[16,26,8,128]{3,2,1,0:T(8,128)S(1)} async-done(((f32[16,26,8,128]{3,2,1,0:T(8,128)}), f32[16,26,8,128]{3,2,1,0:T(8,128)S(1)}, u32[]{:S(2)}, u32[]{:S(2)}) %all-to-all-start) | async-done | bytes 1703968 | tf_op jit(solution)/shard_map/all_to_all | solution.py:584
  48.6 0.0 copy-done.2
  48.6 0.0 copy-done.11
  48.6 0.0 copy-done.12
  48.6 11.9 %patch.1 = (f32[1,9,32,1024]{3,2,1,0:T(8,128)}, f32[16,24,8,128]{3,2,1,0:T(8,128)}) custom-call(s32[128,3]{1,0:T(8,128)S(1)} %copy.19.roots, f32[8,9]{1,0:T(8,128)S(1)} %copy-done.12, f32[16,26,8,128]{3,2,1,0:T(8,128)S(1)} %all-to-all-done.recv, s32[1,32,1024]{2,1,0:T(8,128)S(1)} %copy-done.11, bf16[256,1152]{1,0:T(8,128)(2,1)S(1)} %copy-done.2, ...), custom_call_target="tpu_custom_call" | custom-call | tf_op jit(solution)/shard_map/patch/pallas_call | solution.py:587
  60.4 0.0 copy-start.8
  60.4 0.0 copy-start.10
  60.4 0.0 copy-done.5
  60.4 4.2 %all-to-all-start.1 = ((f32[16,24,8,128]{3,2,1,0:T(8,128)}), f32[16,24,8,128]{3,2,1,0:T(8,128)S(1)}, u32[]{:S(2)}, u32[]{:S(2)}) async-start(f32[16,24,8,128]{3,2,1,0:T(8,128)} %get-tuple-element.6._), calls=%async_computation.1 | async-start | bytes 3145728 | tf_op jit(solution)/shard_map/all_to_all | solution.py:603
  64.7 0.1 copy.26
  64.7 0.1 concatenate.19.clone
  64.8 0.1 add_multiply_fusion
  64.9 0.1 mul.12
  65.0 0.0 copy-done.8
  65.0 0.0 copy-done.10
  65.0 0.0 copy-start.6
  65.0 0.9 copy-done.6
  65.9 3.3 %coarse.1._.coarse_one = f32[9,16,8,128]{3,2,1,0:T(8,128)S(1)} custom-call(f32[9,16,8,128]{3,2,1,0:T(8,128)S(1)} %copy-done.1, s32[16,8,128]{2,1,0:T(8,128)S(1)} %copy-done.4, f32[10,8,128]{2,1,0:T(8,128)S(1)} %copy-done.8, f32[10,8,128]{2,1,0:T(8,128)S(1)} %copy-done.10, f32[10,16,128]{2,1,0:T(8,128)S(1)} %collective-permute-done.2._ylo.ylo, ...), custom_call_target="tpu_custom_call" | custom-call | tf_op jit(solution)/shard_map/coarse/pallas_call | solution.py:604
  69.3 19.3 %all-to-all-done.1.arrived = f32[16,24,8,128]{3,2,1,0:T(8,128)S(1)} async-done(((f32[16,24,8,128]{3,2,1,0:T(8,128)}), f32[16,24,8,128]{3,2,1,0:T(8,128)S(1)}, u32[]{:S(2)}, u32[]{:S(2)}) %all-to-all-start.1) | async-done | bytes 1572896 | tf_op jit(solution)/shard_map/all_to_all | solution.py:603
  88.5 2.2 %halo.1 = (f32[9,8,128]{2,1,0:T(8,128)S(1)}, f32[9,8,128]{2,1,0:T(8,128)S(1)}) custom-call(s32[128,3]{1,0:T(8,128)S(1)} %copy.19.roots, f32[16,24,8,128]{3,2,1,0:T(8,128)S(1)} %all-to-all-done.1.arrived, f32[9,16,8,128]{3,2,1,0:T(8,128)S(1)} %coarse.1._.coarse_one), custom_call_target="tpu_custom_call" | custom-call | tf_op jit(solution)/shard_map/halo/pallas_call | solution.py:612
  90.7 11.3 %collective-permute-start.4 = (f32[9,8,128]{2,1,0:T(8,128)S(1)}, f32[9,8,128]{2,1,0:T(8,128)S(1)}, u32[]{:S(2)}, u32[]{:S(2)}) collective-permute-start(f32[9,8,128]{2,1,0:T(8,128)S(1)} %get-tuple-element.7), channel_id=1, source_target_pairs={{0,16},{16,32},{32,48},{48,64},{64,80},{80,96},{96,112},{1,17},{17... | collective-permute-start | bytes 110600 | tf_op jit(solution)/shard_map/ppermute | solution.py:616
  102.1 1.9 %collective-permute-start.5 = (f32[9,8,128]{2,1,0:T(8,128)S(1)}, f32[9,8,128]{2,1,0:T(8,128)S(1)}, u32[]{:S(2)}, u32[]{:S(2)}) collective-permute-start(f32[9,8,128]{2,1,0:T(8,128)S(1)} %get-tuple-element.8), channel_id=1, source_target_pairs={{16,0},{32,16},{48,32},{64,48},{80,64},{96,80},{112,96},{17,1},{33... | collective-permute-start | bytes 110600 | tf_op jit(solution)/shard_map/ppermute | solution.py:615
  104.0 0.0 collective-permute-done.4.below
  104.0 3.3 %collective-permute-done.5.above = f32[9,8,128]{2,1,0:T(8,128)S(1)} collective-permute-done((f32[9,8,128]{2,1,0:T(8,128)S(1)}, f32[9,8,128]{2,1,0:T(8,128)S(1)}, u32[]{:S(2)}, u32[]{:S(2)}) %collective-permute-start.5) | collective-permute-done | bytes 36896 | tf_op jit(solution)/shard_map/ppermute | solution.py:615
  107.3 4.0 %add.64 = f32[9,16,8,128]{3,2,1,0:T(8,128)} custom-call(s32[128,3]{1,0:T(8,128)S(1)} %copy.19.roots, f32[16,24,8,128]{3,2,1,0:T(8,128)S(1)} %all-to-all-done.1.arrived, f32[9,16,8,128]{3,2,1,0:T(8,128)S(1)} %coarse.1._.coarse_one, f32[9,8,128]{2,1,0:T(8,128)S(1)} %collective-permute-done.4.below, f32[9,8,128]{2,1,0:T(8,128)S(1)} %collective-permute-done.5.above), custom_call_target="tpu_custom_call" | custom-call | tf_op jit(solution)/shard_map/add/pallas_call | solution.py:617
  (8 shorter events, 0.1 us)
Async XLA Ops:
  0.6 11.6 %copy-start.13 = (s32[128,3]{0,1:T(4,128)S(1)}, s32[128,3]{0,1:T(4,128)}, u32[]{:S(2)}) copy-start(s32[128,3]{0,1:T(4,128)} %param.9) | copy-start | bytes 4612
  2.2 10.2 %collective-permute-start = (f32[10,8,128]{2,1,0:T(8,128)S(1)}, f32[10,8,128]{2,1,0:T(8,128)S(1)}, u32[]{:S(2)}, u32[]{:S(2)}) collective-permute-start(f32[10,8,128]{2,1,0:T(8,128)S(1)} %pad_maximum_fusion.2), channel_id=1, source_target_pairs={{0,16},{16,32},{32,48},{48,64},{64,80},{80,96},{96,112},{1,17},{17... | collective-permute-start | bytes 122888 | tf_op jit(solution)/shard_map/ppermute | solution.py:564
  7.1 5.3 %collective-permute-start.1 = (f32[10,8,128]{2,1,0:T(8,128)S(1)}, f32[10,8,128]{2,1,0:T(8,128)S(1)}, u32[]{:S(2)}, u32[]{:S(2)}) collective-permute-start(f32[10,8,128]{2,1,0:T(8,128)S(1)} %pad_maximum_fusion.3), channel_id=1, source_target_pairs={{16,0},{32,16},{48,32},{64,48},{80,64},{96,80},{112,96},{17,1},{33... | collective-permute-start | bytes 122888 | tf_op jit(solution)/shard_map/ppermute | solution.py:565
  9.0 1.1 copy-start
  10.1 0.8 copy-start.3
  12.4 3.5 %copy-start.7 = (f32[10,8,128]{2,1,0:T(8,128)}, f32[10,8,128]{2,1,0:T(8,128)S(1)}, u32[]{:S(2)}) copy-start(f32[10,8,128]{2,1,0:T(8,128)S(1)} %collective-permute-done.lo) | copy-start | bytes 122884
  12.4 3.5 %copy-start.9 = (f32[10,8,128]{2,1,0:T(8,128)}, f32[10,8,128]{2,1,0:T(8,128)S(1)}, u32[]{:S(2)}) copy-start(f32[10,8,128]{2,1,0:T(8,128)S(1)} %collective-permute-done.1.hi) | copy-start | bytes 122884
  15.9 7.8 %copy-start.4 = (s32[16,8,128]{2,1,0:T(8,128)S(1)}, s32[16,8,128]{2,1,0:T(8,128)}, u32[]{:S(2)}) copy-start(s32[16,8,128]{2,1,0:T(8,128)} %idx.3) | copy-start | bytes 196612
  15.9 7.8 %copy-start.1 = (f32[9,16,8,128]{3,2,1,0:T(8,128)S(1)}, f32[9,16,8,128]{3,2,1,0:T(8,128)}, u32[]{:S(2)}) copy-start(f32[9,16,8,128]{3,2,1,0:T(8,128)} %u.3) | copy-start | bytes 1769476
  15.9 32.7 %copy-start.2 = (bf16[256,1152]{1,0:T(8,128)(2,1)S(1)}, bf16[256,1152]{1,0:T(8,128)(2,1)}, u32[]{:S(2)}) copy-start(bf16[256,1152]{1,0:T(8,128)(2,1)} %constant.3.clone.tabs) | copy-start | bytes 1769476
  15.9 32.7 %copy-start.11 = (s32[1,32,1024]{2,1,0:T(8,128)S(1)}, s32[1,32,1024]{2,1,0:T(8,128)}, u32[]{:S(2)}) copy-start(s32[1,32,1024]{2,1,0:T(8,128)} %fidx.1) | copy-start | bytes 393220
  15.9 32.7 %copy-start.12 = (f32[8,9]{1,0:T(8,128)S(1)}, f32[8,9]{1,0:T(8,128)}, u32[]{:S(2)}) copy-start(f32[8,9]{1,0:T(8,128)} %table.1) | copy-start | bytes 868
  15.9 32.6 %all-to-all-start = ((f32[16,26,8,128]{3,2,1,0:T(8,128)}), f32[16,26,8,128]{3,2,1,0:T(8,128)S(1)}, u32[]{:S(2)}, u32[]{:S(2)}) async-start(f32[16,26,8,128]{3,2,1,0:T(8,128)} %pack.1), calls=%async_computation | async-start | bytes 3407872 | tf_op jit(solution)/shard_map/all_to_all | solution.py:584
  23.8 18.9 %collective-permute-start.2 = (f32[10,16,128]{2,1,0:T(8,128)S(1)}, f32[10,16,128]{2,1,0:T(8,128)S(1)}, u32[]{:S(2)}, u32[]{:S(2)}) collective-permute-start(f32[10,16,128]{2,1,0:T(8,128)S(1)} %pad_maximum_fusion), channel_id=1, source_target_pairs={{0,1},{1,2},{2,3},{3,4},{4,5},{5,6},{6,7},{7,8},{8,9},{9,10},{10,1... | collective-permute-start | bytes 245768 | tf_op jit(solution)/shard_map/ppermute | solution.py:566
  27.1 18.0 %collective-permute-start.3 = (f32[10,16,128]{2,1,0:T(8,128)S(1)}, f32[10,16,128]{2,1,0:T(8,128)S(1)}, u32[]{:S(2)}, u32[]{:S(2)}) collective-permute-start(f32[10,16,128]{2,1,0:T(8,128)S(1)} %pad_maximum_fusion.1), channel_id=1, source_target_pairs={{1,0},{2,1},{3,2},{4,3},{5,4},{6,5},{7,6},{8,7},{9,8},{10,9},{11,1... | collective-permute-start | bytes 245768 | tf_op jit(solution)/shard_map/ppermute | solution.py:567
  45.1 15.4 %copy-start.5 = (f32[10,16,128]{2,1,0:T(8,128)}, f32[10,16,128]{2,1,0:T(8,128)S(1)}, u32[]{:S(2)}) copy-start(f32[10,16,128]{2,1,0:T(8,128)S(1)} %collective-permute-done.3._yhi.yhi) | copy-start | bytes 245764
  60.4 4.6 %copy-start.8 = (f32[10,8,128]{2,1,0:T(8,128)S(1)}, f32[10,8,128]{2,1,0:T(8,128)}, u32[]{:S(2)}) copy-start(f32[10,8,128]{2,1,0:T(8,128)} %copy-done.7) | copy-start | bytes 122884
  60.4 4.6 %copy-start.10 = (f32[10,8,128]{2,1,0:T(8,128)S(1)}, f32[10,8,128]{2,1,0:T(8,128)}, u32[]{:S(2)}) copy-start(f32[10,8,128]{2,1,0:T(8,128)} %copy-done.9) | copy-start | bytes 122884
  60.4 28.1 %all-to-all-start.1 = ((f32[16,24,8,128]{3,2,1,0:T(8,128)}), f32[16,24,8,128]{3,2,1,0:T(8,128)S(1)}, u32[]{:S(2)}, u32[]{:S(2)}) async-start(f32[16,24,8,128]{3,2,1,0:T(8,128)} %get-tuple-element.6._), calls=%async_computation.1 | async-start | bytes 3145728 | tf_op jit(solution)/shard_map/all_to_all | solution.py:603
  65.0 0.9 copy-start.6
  90.7 13.3 %collective-permute-start.4 = (f32[9,8,128]{2,1,0:T(8,128)S(1)}, f32[9,8,128]{2,1,0:T(8,128)S(1)}, u32[]{:S(2)}, u32[]{:S(2)}) collective-permute-start(f32[9,8,128]{2,1,0:T(8,128)S(1)} %get-tuple-element.7), channel_id=1, source_target_pairs={{0,16},{16,32},{32,48},{48,64},{64,80},{80,96},{96,112},{1,17},{17... | collective-permute-start | bytes 110600 | tf_op jit(solution)/shard_map/ppermute | solution.py:616
  102.1 5.3 %collective-permute-start.5 = (f32[9,8,128]{2,1,0:T(8,128)S(1)}, f32[9,8,128]{2,1,0:T(8,128)S(1)}, u32[]{:S(2)}, u32[]{:S(2)}) collective-permute-start(f32[9,8,128]{2,1,0:T(8,128)S(1)} %get-tuple-element.8), channel_id=1, source_target_pairs={{16,0},{32,16},{48,32},{64,48},{80,64},{96,80},{112,96},{17,1},{33... | collective-permute-start | bytes 110600 | tf_op jit(solution)/shard_map/ppermute | solution.py:615

commit v3 on v2

--- a/solution.py
+++ b/solution.py
@@ -142,7 +142,7 @@
     lax.fori_loop(0, DEV, one, 0)
 
 
-def coarse_kernel(u, idx, lo, hi, ylo, yhi, ptab, _, out, cls, px, pyl, pyh, pzl, pzh):
+def coarse_kernel(u, idx, lo, hi, ptab, _, out, cls, px, pyl, pyh, pzl, pzh):
     lane = lanes((8, 128))
     sub = lax.broadcasted_iota(jnp.int32, (8, 128), 0)
     cls[0] = lo[S].astype(jnp.int32)
@@ -150,12 +150,6 @@
     for x in range(CX):
         cls[x + 1] = idx[x] + 1
 
-    def below_y(a, row):
-        return jnp.where(sub == 0, jnp.broadcast_to(row, (8, 128)), pltpu.roll(a, 1, 0))
-
-    def above_y(a, row):
-        return jnp.where(sub == 7, jnp.broadcast_to(row, (8, 128)), pltpu.roll(a, 7, 0))
-
     def below_z(a):
         return jnp.where(lane == 0, jnp.zeros_like(a), pltpu.roll(a, 1, 1))
 
@@ -166,8 +160,8 @@
         px[x] = cls[x + 1] * CLS + cls[x]
     for x in range(CX):
         c = cls[x + 1]
-        pyl[x] = c * CLS + below_y(c, ylo[S, x : x + 1, :].astype(jnp.int32))
-        pyh[x] = c * CLS + above_y(c, yhi[S, x : x + 1, :].astype(jnp.int32))
+        pyl[x] = jnp.where(sub == 0, 127, c * CLS + pltpu.roll(c, 1, 0))
+        pyh[x] = jnp.where(sub == 7, 127, c * CLS + pltpu.roll(c, 7, 0))
         pzl[x] = c * CLS + below_z(c)
         pzh[x] = c * CLS + above_z(c)
 
@@ -179,8 +173,8 @@
             after = u[s, x + 1] if x + 1 < CX else hi[s]
             next_flux = pick(tab, px[x + 1]) * (after - center)
             total = next_flux - flux
-            total = total + pick(tab, pyl[x]) * (below_y(center, ylo[s, x : x + 1, :]) - center)
-            total = total + pick(tab, pyh[x]) * (above_y(center, yhi[s, x : x + 1, :]) - center)
+            total = total + pick(tab, pyl[x]) * (pltpu.roll(center, 1, 0) - center)
+            total = total + pick(tab, pyh[x]) * (pltpu.roll(center, 7, 0) - center)
             total = total + pick(tab, pzl[x]) * (below_z(center) - center)
             total = total + pick(tab, pzh[x]) * (above_z(center) - center)
             out[s, x] = center + total
@@ -191,9 +185,9 @@
 
 
 def patch_kernel(
-    roots, table, recv, fidx, tabs, _ylo, _yhi,
+    roots, table, recv, fidx, tabs,
     fine, back,
-    fr, fc, up, upy, da, ua, ub, uc, uy, dy, zg, dz, fx, fyl, fyh, fzl, fzh, fb, fs, gc, zr, yr, b1, b2, by, dl, mk, hb,
+    fr, fc, up, upy, da, ua, ub, uc, uy, dy, zg, dz, fx, fyl, fyh, fzl, fzh, fb, fs, gc, zr, yr, b1, b2, by, dl, mk, hb, fbuf, bbuf, fsem, bsem,
 ):
     grp, me = lax.axis_index("grp"), lax.axis_index("dev")
     owner, y0, _ = where_is(roots, grp * DEV + me)
@@ -311,6 +305,10 @@
         value = value + (fyl[j] * low[j] + fyh[j] * top[j])
         value = value + (fzl[j] * z[j][0] + fzh[j] * z[j][1])
         return u + (value + (gc[j] - fs[j] * u))
+
+    def leave(s):
+        half = lax.bitwise_and(s, 1)
+        return pltpu.make_async_copy(fbuf.at[half], fine.at[0, s], fsem.at[half])
 
     def species(s, carry):
         for j in range(8):
@@ -360,13 +358,19 @@
         for j in range(8):
             ub[j, inner] = change(j, ua, first[j], low, top, z)
         second = [ub[j, inner] for j in range(8)]
+        half = lax.bitwise_and(s, 1)
+
+        @pl.when(s >= 2)
+        def _():
+            leave(s - 2).wait()
+
         z = z_neighbours(second)
         low, top = y_neighbours(second, ghost)
         for j in range(8):
             both = ua[j, inner] + second[j]
             value = change(j, ub, second[j], low, top, z)
             uc[j] = value
-            fine[0, s, :, 128 * j : 128 * j + 128] = value
+            fbuf[half, :, 128 * j : 128 * j + 128] = value
             zr[j] = fb[j] * both - 2.0 * gc[j]
             for at, row, out_row in ((0, 8, 0), (32, 39, W - 1)):
                 outer = 7 if row == 8 else 40
@@ -380,6 +384,7 @@
             b1[j, s, 1 : CX + 1] = uc[j, pl.ds(0, CX, stride=2), :] + uc[j, pl.ds(1, CX, stride=2), :]
             b2[j, s, 1 : CX + 1] = zr[j, pl.ds(0, CX, stride=2), :] + zr[j, pl.ds(1, CX, stride=2), :]
         by[s, 1 : CX + 1] = yr[pl.ds(0, CX, stride=2), :] + yr[pl.ds(1, CX, stride=2), :]
+        leave(s).start()
         return carry
 
     lax.fori_loop(0, S, species, 0)
@@ -461,6 +466,10 @@
 
     main_from = ([0], [0, 1, 2], [1, 2, 3], [2, 3])
     rest_from = ([0, 1], [1, 2], [2, 3], [])
+
+    def send(k):
+        return pltpu.make_async_copy(bbuf.at[k], back.at[owner + k], bsem.at[k])
+
     for k in range(4):
 
         @pl.when(8 * k - y0 < W)
@@ -477,14 +486,25 @@
                         value = jnp.where(lane >= 128 * t - at, piece, value)
                     return value
 
-                back[owner + k, g] = cut(main_from[k], 512 - start[k], start[k])
+                bbuf[k, g] = cut(main_from[k], 512 - start[k], start[k])
                 part = cut(rest_from[k], 512 - start[k] + slot, start[k] + 128 - slot)
                 rest = part if slot == 0 else jnp.where(lane >= slot, part, rest)
                 if slot == 112 or g == GB - 1:
-                    back[owner + k, GB + g // 8] = rest
-
-
-def add_windows(roots, arrived, acc, groups, stride):
+                    bbuf[k, GB + g // 8] = rest
+            send(k).start()
+
+
+    for k in range(4):
+
+        @pl.when(8 * k - y0 < W)
+        def _(k=k):
+            send(k).wait()
+
+    for s in (S - 2, S - 1):
+        leave(jnp.int32(s)).wait()
+
+
+def add_windows(roots, arrived, acc, groups, stride, first=None):
     grp, me = lax.axis_index("grp"), lax.axis_index("dev")
     lane = lanes((8, 128))
 
@@ -493,6 +513,8 @@
         return carry
 
     lax.fori_loop(0, stride, clear, 0)
+    if first is not None:
+        first()
 
     def one(p, carry):
         owner, y0, z0 = where_is(roots, grp * DEV + p)
@@ -522,8 +544,15 @@
         top[s] = acc[pl.ds(S + s, 8, stride=24), :]
 
 
-def add_kernel(roots, arrived, coarse_one, below, above, out, acc):
-    add_windows(roots, arrived, acc, range(2 * S), S * CX)
+def add_kernel(roots, arrived, coarse_one, below, above, own_lo, own_hi, ylo, yhi, ptab, out, acc):
+    def faces():
+        for at, own, other in ((0, own_lo, ylo), (7 * S * CX, own_hi, yhi)):
+            pair = own[S].astype(jnp.int32) * CLS + other[S].astype(jnp.int32)
+            for s in range(S):
+                tab = jnp.broadcast_to(0.5 * ptab[s : s + 1, :], (8, 128))
+                acc[at + s * CX : at + s * CX + CX, :] = pick(tab, pair) * (other[s] - own[s])
+
+    add_windows(roots, arrived, acc, range(2 * S), S * CX, faces)
     for s in range(S):
         for x in range(CX):
             value = coarse_one[s, x] + acc[pl.ds(s * CX + x, 8, stride=S * CX), :]
@@ -534,12 +563,12 @@
             out[s, x] = value
 
 
-def call(kernel, outs, ins, scratch, name, mib):
+def call(kernel, outs, ins, scratch, name, mib, to=VMEM):
     return pl.pallas_call(
         kernel,
         out_shape=outs,
         in_specs=ins,
-        out_specs=jax.tree.map(lambda _: VMEM, outs),
+        out_specs=jax.tree.map(lambda _: to, outs),
         scratch_shapes=scratch,
         compiler_params=pltpu.CompilerParams(vmem_limit_bytes=mib * 1024 * 1024),
         name=name,
@@ -563,8 +592,10 @@
 
     x_lo = lax.ppermute(plane(coarse_state[:, CX - 1], coef_index[CX - 1]), "grp", up_g)
     x_hi = lax.ppermute(plane(coarse_state[:, 0], coef_index[0]), "grp", down_g)
-    y_lo = lax.ppermute(plane(coarse_state[:, :, CY - 1], coef_index[:, CY - 1]), "dev", up_d)
-    y_hi = lax.ppermute(plane(coarse_state[:, :, 0], coef_index[:, 0]), "dev", down_d)
+    own_lo = plane(coarse_state[:, :, 0], coef_index[:, 0])
+    own_hi = plane(coarse_state[:, :, CY - 1], coef_index[:, CY - 1])
+    y_lo = lax.ppermute(own_hi, "dev", up_d)
+    y_hi = lax.ppermute(own_lo, "dev", down_d)
 
     slab = call(
         slab_kernel,
@@ -587,7 +618,7 @@
     fine_state, corrections = call(
         patch_kernel,
         (shape(1, S, 32, 1024), shape(DEV, NB, 8, 128)),
-        [SMEM, SMEM] + [VMEM] * 3 + [ANY] * 2,
+        [SMEM, SMEM] + [VMEM] * 3,
         [
             f32(3, 2 * S, PITCH, 128), f32(3, PITCH, 128), f32(24, 2 * S, PITCH, 128), f32(2 * S, PITCH, 128),
             f32(8, 48, 128), f32(8, 48, 128), f32(8, 48, 128), f32(8, 32, 128),
@@ -596,27 +627,29 @@
             f32(8, 32, 128), f32(8, 32, 128), f32(8, 32, 128), f32(8, 32, 128), f32(32, 128),
             f32(8, CH, PITCH, 128), f32(8, CH, PITCH, 128), f32(CH, PITCH, 128),
             f32(3, CH, PITCH, 128), f32(12, 3 * PITCH, 128), f32(3, 24, 128),
+            f32(2, 32, 1024), f32(4, NB, 8, 128), pltpu.SemaphoreType.DMA((2,)), pltpu.SemaphoreType.DMA((4,)),
         ],
         "patch",
         32,
-    )(patch_root, coef_table, received, fine_index, jnp.asarray(weights()), y_lo, y_hi)
+        ANY,
+    )(patch_root, coef_table, received, fine_index, jnp.asarray(weights()))
     arrived = lax.all_to_all(corrections, "dev", split_axis=0, concat_axis=0, tiled=True)
     coarse_one = call(
         coarse_kernel,
         shape(S, CX, CY, 128),
-        [VMEM] * 7 + [ANY],
+        [VMEM] * 5 + [ANY],
         [i32(CX + 2, 8, 128), i32(CX + 1, 8, 128)] + [i32(CX, 8, 128)] * 4,
         "coarse",
         8,
-    )(coarse_state, coef_index, x_lo, x_hi, y_lo, y_hi, ptab, corrections)
+    )(coarse_state, coef_index, x_lo, x_hi, ptab, corrections)
     low, top = call(
         halo_kernel, (shape(S, CY, 128), shape(S, CY, 128)), [SMEM, VMEM, ANY], [f32(8 * 24, 128)], "halo", 8
     )(patch_root, arrived, coarse_one)
     from_above = lax.ppermute(low, "grp", down_g)
     from_below = lax.ppermute(top, "grp", up_g)
     coarse_new = call(
-        add_kernel, shape(S, CX, CY, 128), [SMEM] + [VMEM] * 4, [f32(8 * S * CX, 128)], "add", 8
-    )(patch_root, arrived, coarse_one, from_below, from_above)
+        add_kernel, shape(S, CX, CY, 128), [SMEM] + [VMEM] * 9, [f32(8 * S * CX, 128)], "add", 8
+    )(patch_root, arrived, coarse_one, from_below, from_above, own_lo, own_hi, y_lo, y_hi, ptab)
     return coarse_new, fine_state
 
 

time: 112 us -> 102 us (0.911)
  the two profiles are of different devices: /device:TPU:1 before, /device:TPU:33 now
where the time goes in v3:
time: 102 us
  blocking collectives  30.2 us (30%)
  starting transfers between devices  26.3 us (26%)
  Pallas kernels  24.6 us (24%)
  waiting for transfers between devices  15.6 us (15%)
  local copies, waits for them, and re-layouts  3.2 us (3%)
    all_to_all x1, blocking collectives, body(): lax.all_to_all(blocks, 'dev', split_axis=0, concat_axis=0, tiled=True)  30.2 us
    all_to_all x1, waiting for transfers between devices, body(): lax.all_to_all(corrections, 'dev', split_axis=0, concat_axis=0, tiled=True)  12.2 us
    pallas_call x1, Pallas kernels, body(): call(patch_kernel, (shape(1, S, 32, 1024), shape(DEV, NB, 8, 128)), [SMEM...  11.4 us
    ppermute x1, starting transfers between devices, body(): from_below = lax.ppermute(top, 'grp', up_g)  9.91 us
    pallas_call x1, Pallas kernels, body(): call(add_kernel, shape(S, CX, CY, 128), [SMEM] + [VMEM] * 9, [f32(8 * S *...  4.12 us
    ppermute x1, starting transfers between devices, body(): lax.ppermute(plane(coarse_state[:, CX - 1], coef_index[CX - 1]), 'grp', u...  4.09 us
    all_to_all x1, starting transfers between devices, body(): lax.all_to_all(corrections, 'dev', split_axis=0, concat_axis=0, tiled=True)  3.9 us
    pallas_call x1, Pallas kernels, body(): call(coarse_kernel, shape(S, CX, CY, 128), [VMEM] * 5 + [ANY], [i32(CX +...  3.32 us
  transfers between devices with their start and end apart: 7, of which 2 were waited for; matrix products, arithmetic and copies ran while one was open for 1% of the time, Pallas kernels for 7%

profile of v3, /device:TPU:33, one launch (start us, length us, event | category | flops | bytes accessed | tf_op | source)
XLA Modules:
  0.0 101.6 jit_solution(3836016929211084940)
XLA Ops:
  0.6 0.0 copy-start.7
  0.6 0.8 slice_bitcast_fusion
  1.4 0.7 add_convert_fusion
  2.2 4.1 %collective-permute-start = (f32[10,8,128]{2,1,0:T(8,128)S(1)}, f32[10,8,128]{2,1,0:T(8,128)S(1)}, u32[]{:S(2)}, u32[]{:S(2)}) collective-permute-start(f32[10,8,128]{2,1,0:T(8,128)S(1)} %pad_maximum_fusion.2), channel_id=1, source_target_pairs={{0,16},{16,32},{32,48},{48,64},{64,80},{80,96},{96,112},{1,17},{17... | collective-permute-start | bytes 122888 | tf_op jit(solution)/shard_map/ppermute | solution.py:593
  6.3 1.9 %collective-permute-start.1 = (f32[10,8,128]{2,1,0:T(8,128)S(1)}, f32[10,8,128]{2,1,0:T(8,128)S(1)}, u32[]{:S(2)}, u32[]{:S(2)}) collective-permute-start(f32[10,8,128]{2,1,0:T(8,128)S(1)} %pad_maximum_fusion.3), channel_id=1, source_target_pairs={{16,0},{32,16},{48,32},{64,48},{80,64},{96,80},{112,96},{17,1},{33... | collective-permute-start | bytes 122888 | tf_op jit(solution)/shard_map/ppermute | solution.py:594
  8.2 0.0 copy-start
  8.2 1.1 %copy-done = f32[9,16,8,128]{3,2,1,0:T(8,128)S(1)} copy-done((f32[9,16,8,128]{3,2,1,0:T(8,128)S(1)}, f32[9,16,8,128]{3,2,1,0:T(8,128)}, u32[]{:S(2)}) %copy-start) | copy-done | bytes 589848
  9.3 0.0 copy-start.3
  9.3 0.8 copy-done.3
  10.1 1.3 %slab.1 = f32[1280,128]{1,0:T(8,128)S(1)} custom-call(f32[9,16,8,128]{3,2,1,0:T(8,128)S(1)} %copy-done, s32[16,8,128]{2,1,0:T(8,128)S(1)} %copy-done.3), custom_call_target="tpu_custom_call" | custom-call | tf_op jit(solution)/shard_map/slab/pallas_call | solution.py:600
  11.4 0.0 copy-done.7
  11.4 0.1 copy.19.roots
  11.5 0.0 collective-permute-done.lo
  11.6 0.0 collective-permute-done.1.hi
  11.6 2.2 %pack.1 = f32[16,26,8,128]{3,2,1,0:T(8,128)S(1)} custom-call(s32[128,3]{1,0:T(8,128)S(1)} %copy.19.roots, f32[1280,128]{1,0:T(8,128)S(1)} %slab.1, f32[10,8,128]{2,1,0:T(8,128)S(1)} %collective-permute-done.lo, f32[10,8,128]{2,1,0:T(8,128)S(1)} %collective-permute-done.1.hi), custom_call_target="tpu_custom_call" | custom-call | tf_op jit(solution)/shard_map/pack/pallas_call | solution.py:612
  13.8 0.0 copy-start.2
  13.8 0.0 copy-start.5
  13.8 0.0 copy-start.6
  13.8 30.2 %all_to_all.10.recv = f32[16,26,8,128]{3,2,1,0:T(8,128)S(1)} all-to-all(f32[16,26,8,128]{3,2,1,0:T(8,128)S(1)} %pack.1), channel_id=1, replica_groups=mesh['grp'=8,'dev'=16] {'dev'}, dimensions={0} | all-to-all | bytes 3407872 | tf_op jit(solution)/shard_map/all_to_all | solution.py:615
  44.1 0.0 copy-done.2
  44.1 0.0 copy-done.5
  44.1 0.0 copy-done.6
  44.1 11.4 %patch.1 = (f32[1,9,32,1024]{3,2,1,0:T(8,128)}, f32[16,24,8,128]{3,2,1,0:T(8,128)}) custom-call(s32[128,3]{1,0:T(8,128)S(1)} %copy.19.roots, f32[8,9]{1,0:T(8,128)S(1)} %copy-done.6, f32[16,26,8,128]{3,2,1,0:T(8,128)S(1)} %all_to_all.10.recv, s32[1,32,1024]{2,1,0:T(8,128)S(1)} %copy-done.5, bf16[256,1152]{1,0:T(8,128)(2,1)S(1)} %copy-done.2), custom_call_target="tpu_custom_call" | custom-call | tf_op jit(solution)/shard_map/patch/pallas_call | solution.py:618
  55.5 0.0 copy-start.4
  55.5 0.0 copy-start.1
  55.5 3.9 %all-to-all-start.1 = ((f32[16,24,8,128]{3,2,1,0:T(8,128)}), f32[16,24,8,128]{3,2,1,0:T(8,128)S(1)}, u32[]{:S(2)}, u32[]{:S(2)}) async-start(f32[16,24,8,128]{3,2,1,0:T(8,128)} %get-tuple-element.6._), calls=%async_computation.1 | async-start | bytes 3145728 | tf_op jit(solution)/shard_map/all_to_all | solution.py:636
  59.4 0.0 copy-done.4
  59.5 0.0 copy-done.1
  59.5 0.1 fusion
  59.6 3.3 %collective-permute-start.4 = (f32[10,16,128]{2,1,0:T(8,128)S(1)}, f32[10,16,128]{2,1,0:T(8,128)S(1)}, u32[]{:S(2)}, u32[]{:S(2)}) collective-permute-start(f32[10,16,128]{2,1,0:T(8,128)S(1)} %pad_maximum_fusion.1.own_hi), channel_id=1, source_target_pairs={{0,1},{1,2},{2,3},{3,4},{4,5},{5,6},{6,7},{7,8},{8,9},{9,10},{10,1... | collective-permute-start | bytes 245768 | tf_op jit(solution)/shard_map/ppermute | solution.py:597
  62.9 1.3 %collective-permute-start.5 = (f32[10,16,128]{2,1,0:T(8,128)S(1)}, f32[10,16,128]{2,1,0:T(8,128)S(1)}, u32[]{:S(2)}, u32[]{:S(2)}) collective-permute-start(f32[10,16,128]{2,1,0:T(8,128)S(1)} %pad_maximum_fusion.own_lo), channel_id=1, source_target_pairs={{1,0},{2,1},{3,2},{4,3},{5,4},{6,5},{7,6},{8,7},{9,8},{10,9},{11,1... | collective-permute-start | bytes 245768 | tf_op jit(solution)/shard_map/ppermute | solution.py:598
  64.2 0.1 copy.26
  64.3 0.1 concatenate.17.clone
  64.4 0.1 add_multiply_fusion
  64.5 0.1 mul.12
  64.6 3.3 %coarse.1._.coarse_one = f32[9,16,8,128]{3,2,1,0:T(8,128)S(1)} custom-call(f32[9,16,8,128]{3,2,1,0:T(8,128)S(1)} %copy-done.1, s32[16,8,128]{2,1,0:T(8,128)S(1)} %copy-done.4, f32[10,8,128]{2,1,0:T(8,128)S(1)} %collective-permute-done.lo, f32[10,8,128]{2,1,0:T(8,128)S(1)} %collective-permute-done.1.hi, f32[9,128]{1,0:T(8,128)S(1)} %pad.5.ptab, ...), custom_call_target="tpu_custom_call" | custom-call | tf_op jit(solution)/shard_map/coarse/pallas_call | solution.py:637
  67.9 12.2 %all-to-all-done.1.arrived = f32[16,24,8,128]{3,2,1,0:T(8,128)S(1)} async-done(((f32[16,24,8,128]{3,2,1,0:T(8,128)}), f32[16,24,8,128]{3,2,1,0:T(8,128)S(1)}, u32[]{:S(2)}, u32[]{:S(2)}) %all-to-all-start.1) | async-done | bytes 1572896 | tf_op jit(solution)/shard_map/all_to_all | solution.py:636
  80.1 2.2 %halo.1 = (f32[9,8,128]{2,1,0:T(8,128)S(1)}, f32[9,8,128]{2,1,0:T(8,128)S(1)}) custom-call(s32[128,3]{1,0:T(8,128)S(1)} %copy.19.roots, f32[16,24,8,128]{3,2,1,0:T(8,128)S(1)} %all-to-all-done.1.arrived, f32[9,16,8,128]{3,2,1,0:T(8,128)S(1)} %coarse.1._.coarse_one), custom_call_target="tpu_custom_call" | custom-call | tf_op jit(solution)/shard_map/halo/pallas_call | solution.py:645
  82.3 9.9 %collective-permute-start.2 = (f32[9,8,128]{2,1,0:T(8,128)S(1)}, f32[9,8,128]{2,1,0:T(8,128)S(1)}, u32[]{:S(2)}, u32[]{:S(2)}) collective-permute-start(f32[9,8,128]{2,1,0:T(8,128)S(1)} %get-tuple-element.7), channel_id=1, source_target_pairs={{0,16},{16,32},{32,48},{48,64},{64,80},{80,96},{96,112},{1,17},{17... | collective-permute-start | bytes 110600 | tf_op jit(solution)/shard_map/ppermute | solution.py:649
  92.2 1.9 %collective-permute-start.3 = (f32[9,8,128]{2,1,0:T(8,128)S(1)}, f32[9,8,128]{2,1,0:T(8,128)S(1)}, u32[]{:S(2)}, u32[]{:S(2)}) collective-permute-start(f32[9,8,128]{2,1,0:T(8,128)S(1)} %get-tuple-element.8), channel_id=1, source_target_pairs={{16,0},{32,16},{48,32},{64,48},{80,64},{96,80},{112,96},{17,1},{33... | collective-permute-start | bytes 110600 | tf_op jit(solution)/shard_map/ppermute | solution.py:648
  94.1 0.0 collective-permute-done.4.ylo
  94.2 0.0 collective-permute-done.5.yhi
  94.2 0.0 collective-permute-done.2.below
  94.2 3.3 %collective-permute-done.3.above = f32[9,8,128]{2,1,0:T(8,128)S(1)} collective-permute-done((f32[9,8,128]{2,1,0:T(8,128)S(1)}, f32[9,8,128]{2,1,0:T(8,128)S(1)}, u32[]{:S(2)}, u32[]{:S(2)}) %collective-permute-start.3) | collective-permute-done | bytes 36896 | tf_op jit(solution)/shard_map/ppermute | solution.py:648
  97.5 4.1 %add.64 = f32[9,16,8,128]{3,2,1,0:T(8,128)} custom-call(s32[128,3]{1,0:T(8,128)S(1)} %copy.19.roots, f32[16,24,8,128]{3,2,1,0:T(8,128)S(1)} %all-to-all-done.1.arrived, f32[9,16,8,128]{3,2,1,0:T(8,128)S(1)} %coarse.1._.coarse_one, f32[9,8,128]{2,1,0:T(8,128)S(1)} %collective-permute-done.2.below, f32[9,8,128]{2,1,0:T(8,128)S(1)} %collective-permute-done.3.above, ...), custom_call_target="tpu_custom_call" | custom-call | tf_op jit(solution)/shard_map/add/pallas_call | solution.py:650
  (8 shorter events, 0.1 us)
Async XLA Ops:
  0.6 10.8 %copy-start.7 = (s32[128,3]{0,1:T(4,128)S(1)}, s32[128,3]{0,1:T(4,128)}, u32[]{:S(2)}) copy-start(s32[128,3]{0,1:T(4,128)} %param.9) | copy-start | bytes 4612
  2.2 9.4 %collective-permute-start = (f32[10,8,128]{2,1,0:T(8,128)S(1)}, f32[10,8,128]{2,1,0:T(8,128)S(1)}, u32[]{:S(2)}, u32[]{:S(2)}) collective-permute-start(f32[10,8,128]{2,1,0:T(8,128)S(1)} %pad_maximum_fusion.2), channel_id=1, source_target_pairs={{0,16},{16,32},{32,48},{48,64},{64,80},{80,96},{96,112},{1,17},{17... | collective-permute-start | bytes 122888 | tf_op jit(solution)/shard_map/ppermute | solution.py:593
  6.3 5.3 %collective-permute-start.1 = (f32[10,8,128]{2,1,0:T(8,128)S(1)}, f32[10,8,128]{2,1,0:T(8,128)S(1)}, u32[]{:S(2)}, u32[]{:S(2)}) collective-permute-start(f32[10,8,128]{2,1,0:T(8,128)S(1)} %pad_maximum_fusion.3), channel_id=1, source_target_pairs={{16,0},{32,16},{48,32},{64,48},{80,64},{96,80},{112,96},{17,1},{33... | collective-permute-start | bytes 122888 | tf_op jit(solution)/shard_map/ppermute | solution.py:594
  8.2 1.1 %copy-start = (f32[9,16,8,128]{3,2,1,0:T(8,128)S(1)}, f32[9,16,8,128]{3,2,1,0:T(8,128)}, u32[]{:S(2)}) copy-start(f32[9,16,8,128]{3,2,1,0:T(8,128)} %u.3) | copy-start | bytes 1769476
  9.3 0.8 copy-start.3
  13.8 30.3 %copy-start.2 = (bf16[256,1152]{1,0:T(8,128)(2,1)S(1)}, bf16[256,1152]{1,0:T(8,128)(2,1)}, u32[]{:S(2)}) copy-start(bf16[256,1152]{1,0:T(8,128)(2,1)} %constant.3.clone.tabs) | copy-start | bytes 1769476
  13.8 30.3 %copy-start.5 = (s32[1,32,1024]{2,1,0:T(8,128)S(1)}, s32[1,32,1024]{2,1,0:T(8,128)}, u32[]{:S(2)}) copy-start(s32[1,32,1024]{2,1,0:T(8,128)} %fidx.1) | copy-start | bytes 393220
  13.8 30.2 %copy-start.6 = (f32[8,9]{1,0:T(8,128)S(1)}, f32[8,9]{1,0:T(8,128)}, u32[]{:S(2)}) copy-start(f32[8,9]{1,0:T(8,128)} %table.1) | copy-start | bytes 868
  55.5 3.9 %copy-start.4 = (s32[16,8,128]{2,1,0:T(8,128)S(1)}, s32[16,8,128]{2,1,0:T(8,128)}, u32[]{:S(2)}) copy-start(s32[16,8,128]{2,1,0:T(8,128)} %idx.3) | copy-start | bytes 196612
  55.5 4.0 %copy-start.1 = (f32[9,16,8,128]{3,2,1,0:T(8,128)S(1)}, f32[9,16,8,128]{3,2,1,0:T(8,128)}, u32[]{:S(2)}) copy-start(f32[9,16,8,128]{3,2,1,0:T(8,128)} %u.3) | copy-start | bytes 1769476
  55.5 24.6 %all-to-all-start.1 = ((f32[16,24,8,128]{3,2,1,0:T(8,128)}), f32[16,24,8,128]{3,2,1,0:T(8,128)S(1)}, u32[]{:S(2)}, u32[]{:S(2)}) async-start(f32[16,24,8,128]{3,2,1,0:T(8,128)} %get-tuple-element.6._), calls=%async_computation.1 | async-start | bytes 3145728 | tf_op jit(solution)/shard_map/all_to_all | solution.py:636
  59.6 34.5 %collective-permute-start.4 = (f32[10,16,128]{2,1,0:T(8,128)S(1)}, f32[10,16,128]{2,1,0:T(8,128)S(1)}, u32[]{:S(2)}, u32[]{:S(2)}) collective-permute-start(f32[10,16,128]{2,1,0:T(8,128)S(1)} %pad_maximum_fusion.1.own_hi), channel_id=1, source_target_pairs={{0,1},{1,2},{2,3},{3,4},{4,5},{5,6},{6,7},{7,8},{8,9},{9,10},{10,1... | collective-permute-start | bytes 245768 | tf_op jit(solution)/shard_map/ppermute | solution.py:597
  62.9 31.2 %collective-permute-start.5 = (f32[10,16,128]{2,1,0:T(8,128)S(1)}, f32[10,16,128]{2,1,0:T(8,128)S(1)}, u32[]{:S(2)}, u32[]{:S(2)}) collective-permute-start(f32[10,16,128]{2,1,0:T(8,128)S(1)} %pad_maximum_fusion.own_lo), channel_id=1, source_target_pairs={{1,0},{2,1},{3,2},{4,3},{5,4},{6,5},{7,6},{8,7},{9,8},{10,9},{11,1... | collective-permute-start | bytes 245768 | tf_op jit(solution)/shard_map/ppermute | solution.py:598
  82.3 11.9 %collective-permute-start.2 = (f32[9,8,128]{2,1,0:T(8,128)S(1)}, f32[9,8,128]{2,1,0:T(8,128)S(1)}, u32[]{:S(2)}, u32[]{:S(2)}) collective-permute-start(f32[9,8,128]{2,1,0:T(8,128)S(1)} %get-tuple-element.7), channel_id=1, source_target_pairs={{0,16},{16,32},{32,48},{48,64},{64,80},{80,96},{96,112},{1,17},{17... | collective-permute-start | bytes 110600 | tf_op jit(solution)/shard_map/ppermute | solution.py:649
  92.2 5.3 %collective-permute-start.3 = (f32[9,8,128]{2,1,0:T(8,128)S(1)}, f32[9,8,128]{2,1,0:T(8,128)S(1)}, u32[]{:S(2)}, u32[]{:S(2)}) collective-permute-start(f32[9,8,128]{2,1,0:T(8,128)S(1)} %get-tuple-element.8), channel_id=1, source_target_pairs={{16,0},{32,16},{48,32},{64,48},{80,64},{96,80},{112,96},{17,1},{33... | collective-permute-start | bytes 110600 | tf_op jit(solution)/shard_map/ppermute | solution.py:648

commit v4 on v3

--- a/solution.py
+++ b/solution.py
@@ -106,7 +106,16 @@
         slab[pl.ds(S * CX + x, 8, stride=CH * CX), :] = (ibuf[x] + 1).astype(F32)
 
 
-def pack_kernel(roots, slab, lo, hi, out, halo):
+def listed(roots, slab, me, into, row):
+    count = jnp.int32(0)
+    for p in range(DEV):
+        owner, y0, _ = where_is(roots, slab * DEV + p)
+        into[row, count] = p
+        count = count + touches(owner, y0, me).astype(jnp.int32)
+    return count
+
+
+def pack_kernel(roots, slab, lo, hi, out, halo, mine):
     grp, me = lax.axis_index("grp"), lax.axis_index("dev")
     for c in range(CH):
         halo[pl.ds(c, 8, stride=24), :] = lo[c]
@@ -115,31 +124,28 @@
         halo[pl.ds(r, 8, stride=24), :] = jnp.zeros((8, 128), F32)
     lane = lanes((8, 128))
 
-    def one(p, carry):
-        owner, y0, z0 = where_is(roots, grp * DEV + p)
-
-        @pl.when(jnp.logical_and(me >= owner, 8 * (me - owner) - y0 < W))
-        def _():
-            rest = None
-            for g in range(GF):
-                main = None
-                for y in range(8):
-                    if g < 2 * CH:
-                        rows = slab[y * CH * CX + 8 * g : y * CH * CX + 8 * g + 8, :]
-                    else:
-                        rows = halo[y * 24 + 8 * (g - 2 * CH) : y * 24 + 8 * (g - 2 * CH) + 8, :]
-                    moved = pltpu.roll(rows, mod128(W * y + 128 - z0), 1)
-                    main = moved if y == 0 else jnp.where(lane >= W * y, moved, main)
-                out[p, g] = main
-                slot = 16 * (g % 8)
-                moved = pltpu.roll(rows, mod128(126 + slot + 128 - z0), 1)
-                rest = moved if slot == 0 else jnp.where(lane >= slot, moved, rest)
-                if slot == 112 or g == GF - 1:
-                    out[p, GF + g // 8] = rest
-
+    def one(i, carry):
+        p = mine[0, i]
+        z0 = where_is(roots, grp * DEV + p)[2]
+        rest = None
+        for g in range(GF):
+            main = None
+            for y in range(8):
+                if g < 2 * CH:
+                    rows = slab[y * CH * CX + 8 * g : y * CH * CX + 8 * g + 8, :]
+                else:
+                    rows = halo[y * 24 + 8 * (g - 2 * CH) : y * 24 + 8 * (g - 2 * CH) + 8, :]
+                moved = pltpu.roll(rows, mod128(W * y + 128 - z0), 1)
+                main = moved if y == 0 else jnp.where(lane >= W * y, moved, main)
+            out[p, g] = main
+            slot = 16 * (g % 8)
+            moved = pltpu.roll(rows, mod128(126 + slot + 128 - z0), 1)
+            rest = moved if slot == 0 else jnp.where(lane >= slot, moved, rest)
+            if slot == 112 or g == GF - 1:
+                out[p, GF + g // 8] = rest
         return carry
 
-    lax.fori_loop(0, DEV, one, 0)
+    lax.fori_loop(0, listed(roots, grp, me, mine, 0), one, 0)
 
 
 def coarse_kernel(u, idx, lo, hi, ptab, _, out, cls, px, pyl, pyh, pzl, pzh):
@@ -186,8 +192,8 @@
 
 def patch_kernel(
     roots, table, recv, fidx, tabs,
-    fine, back,
-    fr, fc, up, upy, da, ua, ub, uc, uy, dy, zg, dz, fx, fyl, fyh, fzl, fzh, fb, fs, gc, zr, yr, b1, b2, by, dl, mk, hb, fbuf, bbuf, fsem, bsem,
+    fine, dl, flo, fhi,
+    fr, fc, up, upy, da, ua, ub, uc, uy, dy, zg, dz, fx, fyl, fyh, fzl, fzh, fb, fs, gc, zr, yr, b1, b2, by, mk, fbuf, fsem,
 ):
     grp, me = lax.axis_index("grp"), lax.axis_index("dev")
     owner, y0, _ = where_is(roots, grp * DEV + me)
@@ -454,113 +460,162 @@
     lax.fori_loop(0, S // 3, coarse, 0)
 
     for t in range(3):
-        hb[t, 16:24] = zero8
-        for s in range(S):
-            hb[t, s : s + 1] = dl[t, s, 0:1]
-            hb[t, S + s : S + s + 1] = dl[t, s, W - 1 : W]
-
-    def group_tiles(g):
-        if g < 2 * S:
-            return [dl[t, g // 2, 1 + 8 * (g % 2) : 9 + 8 * (g % 2)] for t in range(3)]
-        return [hb[t, 8 * (g - 2 * S) : 8 * (g - 2 * S) + 8] for t in range(3)]
-
+        for ref, row, last in ((flo, 0, 8), (fhi, W - 1, 9)):
+            ref[t, 8:16] = zero8
+            for s in range(S):
+                at = s if s < 8 else last
+                ref[t, at : at + 1] = dl[t, s, row : row + 1]
+    for s in (S - 2, S - 1):
+        leave(jnp.int32(s)).wait()
+
+
+def beside(grp, step):
+    last = lax.axis_size("grp") - 1
+    return (grp < last, jnp.minimum(grp + 1, last)) if step > 0 else (grp > 0, jnp.maximum(grp - 1, 0))
+
+
+def touches(owner, y0, dev):
+    return jnp.logical_and(dev >= owner, 8 * (dev - owner) - y0 < W)
+
+
+def cut_kernel(roots, dl, above, below, back, buf, sems):
+    grp, me = lax.axis_index("grp"), lax.axis_index("dev")
+    lane = lanes((8, 128))
+    sub = lax.broadcasted_iota(jnp.int32, (8, 128), 0)
+    zero8 = jnp.zeros((8, 128), F32)
     main_from = ([0], [0, 1, 2], [1, 2, 3], [2, 3])
     rest_from = ([0, 1], [1, 2], [2, 3], [])
 
-    def send(k):
-        return pltpu.make_async_copy(bbuf.at[k], back.at[owner + k], bsem.at[k])
+    def cut(tiles, number, amount, at):
+        value = zero8
+        for t in number:
+            piece = zero8 if t == 3 else pltpu.roll(tiles[t], mod128(amount), 1)
+            value = jnp.where(lane >= 128 * t - at, piece, value)
+        return value
+
+    def parts(tiles, k, y0, slot):
+        start = BLK * k - W * y0
+        main = cut(tiles, main_from[k], 512 - start, start)
+        return main, cut(tiles, rest_from[k], 512 - start + slot, start + 128 - slot)
+
+    def always_or(k, offset):
+        return (lambda f: f()) if k < 3 else pl.when(8 * k - offset < W)
+
+    owner, y0, _ = where_is(roots, grp * DEV + me)
+
+    def own_rows(k):
+        return [
+            pltpu.make_async_copy(
+                buf.at[owner + k, first : first + size], back.at[owner + k, first : first + size], sems.at[2 * k + n]
+            )
+            for n, (first, size) in enumerate(((0, 2 * S), (GB, 2)))
+        ]
 
     for k in range(4):
 
-        @pl.when(8 * k - y0 < W)
+        @always_or(k, y0)
         def _(k=k):
-            rest = None
-            for g in range(GB):
-                tiles = group_tiles(g) + [None]
+            to = owner + k
+            for g in range(2 * S):
                 slot = 16 * (g % 8)
-
-                def cut(number, amount, at):
-                    value = zero8
-                    for t in number:
-                        piece = zero8 if tiles[t] is None else pltpu.roll(tiles[t], mod128(amount), 1)
-                        value = jnp.where(lane >= 128 * t - at, piece, value)
-                    return value
-
-                bbuf[k, g] = cut(main_from[k], 512 - start[k], start[k])
-                part = cut(rest_from[k], 512 - start[k] + slot, start[k] + 128 - slot)
+                tiles = [dl[t, g // 2, 1 + 8 * (g % 2) : 9 + 8 * (g % 2)] for t in range(3)]
+                buf[to, g], part = parts(tiles, k, y0, slot)
                 rest = part if slot == 0 else jnp.where(lane >= slot, part, rest)
-                if slot == 112 or g == GB - 1:
-                    bbuf[k, GB + g // 8] = rest
-            send(k).start()
-
-
+                if slot == 112:
+                    buf[to, GB + g // 8] = rest
+            buf[to, GB + 2] = jnp.where(lane < 32, rest, buf[to, GB + 2])
+            for copy in own_rows(k):
+                copy.start()
+
+    for step, faces, group, row in ((1, above, 18, 0), (-1, below, 19, 1)):
+        near, y_near, _ = where_is(roots, beside(grp, step)[1] * DEV + me)
+        for k in range(4):
+
+            @always_or(k, y_near)
+            def _(k=k, faces=faces, group=group, row=row, near=near, y_near=y_near):
+                to = near + k
+                slot = 16 * (group - 16)
+                buf[to, group], rest = parts([faces[t, 0:8] for t in range(3)], k, y_near, slot)
+                main, last = parts([faces[t, 8:16] for t in range(3)], k, y_near, 64)
+                buf[to, 20] = jnp.where(sub == row, main, buf[to, 20])
+                own_lanes = jnp.logical_and(lane >= slot, lane < slot + 16)
+                last_lanes = jnp.logical_and(jnp.logical_and(lane >= 64, lane < 80), sub == row)
+                old = buf[to, GB + 2]
+                buf[to, GB + 2] = jnp.where(own_lanes, rest, jnp.where(last_lanes, last, old))
+
+    shared = [
+        pltpu.make_async_copy(
+            buf.at[:, first : first + size], back.at[:, first : first + size], sems.at[8 + n]
+        )
+        for n, (first, size) in enumerate(((2 * S, 3), (GB + 2, 1)))
+    ]
+    for copy in shared:
+        copy.start()
     for k in range(4):
 
-        @pl.when(8 * k - y0 < W)
+        @always_or(k, y0)
         def _(k=k):
-            send(k).wait()
-
-    for s in (S - 2, S - 1):
-        leave(jnp.int32(s)).wait()
-
-
-def add_windows(roots, arrived, acc, groups, stride, first=None):
+            for copy in own_rows(k):
+                copy.wait()
+
+    for copy in shared:
+        copy.wait()
+
+
+def add_kernel(roots, arrived, coarse_one, own_lo, own_hi, ylo, yhi, ptab, result, out, acc, acc2, mine, sems):
+    def faces():
+        for at, own, other in ((0, own_lo, ylo), (7 * S * CX, own_hi, yhi)):
+            pair = own[S].astype(jnp.int32) * CLS + other[S].astype(jnp.int32)
+            for s in range(S):
+                tab = jnp.broadcast_to(0.5 * ptab[s : s + 1, :], (8, 128))
+                acc[at + s * CX : at + s * CX + CX, :] = pick(tab, pair) * (other[s] - own[s])
+
     grp, me = lax.axis_index("grp"), lax.axis_index("dev")
     lane = lanes((8, 128))
+    zero8 = jnp.zeros((8, 128), F32)
 
     def clear(i, carry):
-        acc[pl.ds(pl.multiple_of(8 * i, 8), 8), :] = jnp.zeros((8, 128), F32)
+        acc[pl.ds(pl.multiple_of(8 * i, 8), 8), :] = zero8
         return carry
 
-    lax.fori_loop(0, stride, clear, 0)
-    if first is not None:
-        first()
-
-    def one(p, carry):
-        owner, y0, z0 = where_is(roots, grp * DEV + p)
-
-        @pl.when(jnp.logical_and(me >= owner, 8 * (me - owner) - y0 < W))
-        def _():
+    lax.fori_loop(0, S * CX, clear, 0)
+    for i in range(32):
+        acc2[8 * i : 8 * i + 8, :] = zero8
+    faces()
+    jobs = [(jnp.bool_(True), grp, range(2 * S), acc, S * CX, 0)]
+    jobs.append(beside(grp, 1) + ((18, 20), acc2, 32, 0))
+    jobs.append(beside(grp, -1) + ((19, 20), acc2, 32, 16))
+
+    for number, (there, slab, groups, into, stride, base) in enumerate(jobs):
+
+        def one(i, carry, number=number, slab=slab, groups=groups, into=into, stride=stride, base=base):
+            p = mine[number, i]
+            z0 = where_is(roots, slab * DEV + p)[2]
             window = jnp.logical_and(lane >= z0, lane < z0 + W)
-            for number, g in enumerate(groups):
+            for at_group, g in enumerate(groups):
                 main, rest = arrived[p, g], arrived[p, GB + g // 8]
                 for y in range(8):
                     moved = pltpu.roll(main, mod128(z0 + 128 - W * y), 1)
                     if y == 7:
                         tail = pltpu.roll(rest, mod128(z0 + 2 + 128 - 16 * (g % 8)), 1)
                         moved = jnp.where(lane < z0 + 2, moved, tail)
-                    rows = slice(y * stride + 8 * number, y * stride + 8 * number + 8)
-                    acc[rows, :] = acc[rows, :] + jnp.where(window, moved, 0.0)
-
-        return carry
-
-    lax.fori_loop(0, DEV, one, 0)
-
-
-def halo_kernel(roots, arrived, _, low, top, acc):
-    add_windows(roots, arrived, acc, range(2 * S, GB), 24)
-    for s in range(S):
-        low[s] = acc[pl.ds(s, 8, stride=24), :]
-        top[s] = acc[pl.ds(S + s, 8, stride=24), :]
-
-
-def add_kernel(roots, arrived, coarse_one, below, above, own_lo, own_hi, ylo, yhi, ptab, out, acc):
-    def faces():
-        for at, own, other in ((0, own_lo, ylo), (7 * S * CX, own_hi, yhi)):
-            pair = own[S].astype(jnp.int32) * CLS + other[S].astype(jnp.int32)
-            for s in range(S):
-                tab = jnp.broadcast_to(0.5 * ptab[s : s + 1, :], (8, 128))
-                acc[at + s * CX : at + s * CX + CX, :] = pick(tab, pair) * (other[s] - own[s])
-
-    add_windows(roots, arrived, acc, range(2 * S), S * CX, faces)
+                    at = y * stride + base + 8 * at_group
+                    into[at : at + 8, :] = into[at : at + 8, :] + jnp.where(window, moved, 0.0)
+            return carry
+
+        lax.fori_loop(0, jnp.where(there, listed(roots, slab, me, mine, number), 0), one, 0)
+    copies = [pltpu.make_async_copy(out.at[s], result.at[s], sems.at[s]) for s in range(S)]
     for s in range(S):
         for x in range(CX):
             value = coarse_one[s, x] + acc[pl.ds(s * CX + x, 8, stride=S * CX), :]
+            if x == CX - 1:
+                value = value + acc2[pl.ds(s, 8, stride=32), :]
             if x == 0:
-                value = value + below[s]
-            if x == CX - 1:
-                value = value + above[s]
+                value = value + acc2[pl.ds(16 + s if s < 8 else 25, 8, stride=32), :]
             out[s, x] = value
+        copies[s].start()
+    for copy in copies:
+        copy.wait()
 
 
 def call(kernel, outs, ins, scratch, name, mib, to=VMEM):
@@ -568,7 +623,7 @@
         kernel,
         out_shape=outs,
         in_specs=ins,
-        out_specs=jax.tree.map(lambda _: to, outs),
+        out_specs=to,
         scratch_shapes=scratch,
         compiler_params=pltpu.CompilerParams(vmem_limit_bytes=mib * 1024 * 1024),
         name=name,
@@ -610,14 +665,14 @@
         8,
     )(coarse_state, coef_index)
     blocks = call(
-        pack_kernel, shape(DEV, NF, 8, 128), [SMEM] + [VMEM] * 3, [pltpu.VMEM((8 * 24, 128), F32)], "pack", 8
+        pack_kernel, shape(DEV, NF, 8, 128), [SMEM] + [VMEM] * 3, [pltpu.VMEM((8 * 24, 128), F32), pltpu.SMEM((1, DEV + 1), jnp.int32)], "pack", 8
     )(patch_root, slab, x_lo, x_hi)
     received = lax.all_to_all(blocks, "dev", split_axis=0, concat_axis=0, tiled=True)
     i32 = lambda *dims: pltpu.VMEM(dims, jnp.int32)
     f32 = lambda *dims: pltpu.VMEM(dims, F32)
-    fine_state, corrections = call(
+    fine_state, delta, face_lo, face_hi = call(
         patch_kernel,
-        (shape(1, S, 32, 1024), shape(DEV, NB, 8, 128)),
+        (shape(1, S, 32, 1024), shape(3, CH, PITCH, 128), shape(3, 16, 128), shape(3, 16, 128)),
         [SMEM, SMEM] + [VMEM] * 3,
         [
             f32(3, 2 * S, PITCH, 128), f32(3, PITCH, 128), f32(24, 2 * S, PITCH, 128), f32(2 * S, PITCH, 128),
@@ -626,13 +681,23 @@
             f32(8, 40, 128), f32(8, 32, 128), f32(8, 32, 128), f32(8, 32, 128), f32(8, 32, 128),
             f32(8, 32, 128), f32(8, 32, 128), f32(8, 32, 128), f32(8, 32, 128), f32(32, 128),
             f32(8, CH, PITCH, 128), f32(8, CH, PITCH, 128), f32(CH, PITCH, 128),
-            f32(3, CH, PITCH, 128), f32(12, 3 * PITCH, 128), f32(3, 24, 128),
-            f32(2, 32, 1024), f32(4, NB, 8, 128), pltpu.SemaphoreType.DMA((2,)), pltpu.SemaphoreType.DMA((4,)),
+            f32(12, 3 * PITCH, 128), f32(2, 32, 1024), pltpu.SemaphoreType.DMA((2,)),
         ],
         "patch",
         32,
+        (ANY, VMEM, VMEM, VMEM),
+    )(patch_root, coef_table, received, fine_index, jnp.asarray(weights()))
+    from_above = lax.ppermute(face_lo, "grp", down_g)
+    from_below = lax.ppermute(face_hi, "grp", up_g)
+    corrections = call(
+        cut_kernel,
+        shape(DEV, NB, 8, 128),
+        [SMEM] + [VMEM] * 3,
+        [f32(DEV, NB, 8, 128), pltpu.SemaphoreType.DMA((10,))],
+        "cut",
+        12,
         ANY,
-    )(patch_root, coef_table, received, fine_index, jnp.asarray(weights()))
+    )(patch_root, delta, from_above, from_below)
     arrived = lax.all_to_all(corrections, "dev", split_axis=0, concat_axis=0, tiled=True)
     coarse_one = call(
         coarse_kernel,
@@ -642,14 +707,21 @@
         "coarse",
         8,
     )(coarse_state, coef_index, x_lo, x_hi, ptab, corrections)
-    low, top = call(
-        halo_kernel, (shape(S, CY, 128), shape(S, CY, 128)), [SMEM, VMEM, ANY], [f32(8 * 24, 128)], "halo", 8
-    )(patch_root, arrived, coarse_one)
-    from_above = lax.ppermute(low, "grp", down_g)
-    from_below = lax.ppermute(top, "grp", up_g)
     coarse_new = call(
-        add_kernel, shape(S, CX, CY, 128), [SMEM] + [VMEM] * 9, [f32(8 * S * CX, 128)], "add", 8
-    )(patch_root, arrived, coarse_one, from_below, from_above, own_lo, own_hi, y_lo, y_hi, ptab)
+        add_kernel,
+        shape(S, CX, CY, 128),
+        [SMEM] + [VMEM] * 7,
+        [
+            f32(S, CX, CY, 128),
+            f32(8 * S * CX, 128),
+            f32(8 * 32, 128),
+            pltpu.SMEM((3, DEV + 1), jnp.int32),
+            pltpu.SemaphoreType.DMA((S,)),
+        ],
+        "add",
+        8,
+        ANY,
+    )(patch_root, arrived, coarse_one, own_lo, own_hi, y_lo, y_hi, ptab)
     return coarse_new, fine_state
 
 

time: 102 us -> 99.7 us (0.977)
  the two profiles are of different devices: /device:TPU:33 before, /device:TPU:32 now
where the time goes in v4:
time: 99.7 us; the launch traced here: 98.2 us
  blocking collectives  32.5 us (33%)
  Pallas kernels  24.1 us (24%)
  starting transfers between devices  18.7 us (19%)
  waiting for transfers between devices  17.9 us (18%)
  local copies, waits for them, and re-layouts  3.2 us (3%)
    all_to_all x1, blocking collectives, body(): lax.all_to_all(blocks, 'dev', split_axis=0, concat_axis=0, tiled=True)  32.5 us
    ppermute x1, waiting for transfers between devices, body(): y_lo = lax.ppermute(own_hi, 'dev', up_d)  10.3 us
    pallas_call x1, Pallas kernels, body(): call(patch_kernel, (shape(1, S, 32, 1024), shape(3, CH, PITCH, 128), shap...  10.3 us
    pallas_call x1, Pallas kernels, body(): call(add_kernel, shape(S, CX, CY, 128), [SMEM] + [VMEM] * 7, [f32(S, CX,...  4.26 us
    all_to_all x1, starting transfers between devices, body(): lax.all_to_all(corrections, 'dev', split_axis=0, concat_axis=0, tiled=True)  3.85 us
    ppermute x1, starting transfers between devices, body(): y_lo = lax.ppermute(own_hi, 'dev', up_d)  3.71 us
    ppermute x1, starting transfers between devices, body(): x_hi = lax.ppermute(plane(coarse_state[:, 0], coef_index[0]), 'grp', down_g)  3.64 us
    all_to_all x1, waiting for transfers between devices, body(): lax.all_to_all(corrections, 'dev', split_axis=0, concat_axis=0, tiled=True)  3.6 us
  transfers between devices with their start and end apart: 7, of which 4 were waited for; matrix products, arithmetic and copies ran while one was open for 1% of the time, Pallas kernels for 5%

profile of v4, /device:TPU:32, one launch (start us, length us, event | category | flops | bytes accessed | tf_op | source)
XLA Modules:
  0.0 98.2 jit_solution(2345106381592723510)
XLA Ops:
  0.6 0.0 copy-start.7
  0.6 0.8 slice_bitcast_fusion
  1.4 0.7 add_convert_fusion
  2.2 1.9 %collective-permute-start = (f32[10,8,128]{2,1,0:T(8,128)S(1)}, f32[10,8,128]{2,1,0:T(8,128)S(1)}, u32[]{:S(2)}, u32[]{:S(2)}) collective-permute-start(f32[10,8,128]{2,1,0:T(8,128)S(1)} %pad_maximum_fusion.2), channel_id=1, source_target_pairs={{0,16},{16,32},{32,48},{48,64},{64,80},{80,96},{96,112},{1,17},{17... | collective-permute-start | bytes 122888 | tf_op jit(solution)/shard_map/ppermute | solution.py:648
  4.1 3.6 %collective-permute-start.1 = (f32[10,8,128]{2,1,0:T(8,128)S(1)}, f32[10,8,128]{2,1,0:T(8,128)S(1)}, u32[]{:S(2)}, u32[]{:S(2)}) collective-permute-start(f32[10,8,128]{2,1,0:T(8,128)S(1)} %pad_maximum_fusion.3), channel_id=1, source_target_pairs={{16,0},{32,16},{48,32},{64,48},{80,64},{96,80},{112,96},{17,1},{33... | collective-permute-start | bytes 122888 | tf_op jit(solution)/shard_map/ppermute | solution.py:649
  7.7 0.0 copy-start
  7.7 1.1 %copy-done = f32[9,16,8,128]{3,2,1,0:T(8,128)S(1)} copy-done((f32[9,16,8,128]{3,2,1,0:T(8,128)S(1)}, f32[9,16,8,128]{3,2,1,0:T(8,128)}, u32[]{:S(2)}) %copy-start) | copy-done | bytes 589848
  8.8 0.0 copy-start.3
  8.8 0.8 copy-done.3
  9.6 1.3 %slab.1 = f32[1280,128]{1,0:T(8,128)S(1)} custom-call(f32[9,16,8,128]{3,2,1,0:T(8,128)S(1)} %copy-done, s32[16,8,128]{2,1,0:T(8,128)S(1)} %copy-done.3), custom_call_target="tpu_custom_call" | custom-call | tf_op jit(solution)/shard_map/slab/pallas_call | solution.py:655
  11.0 0.0 copy-done.7
  11.0 0.1 copy.19.roots
  11.1 0.0 collective-permute-done.lo
  11.1 0.0 collective-permute-done.1.hi
  11.1 2.0 %pack.1 = f32[16,26,8,128]{3,2,1,0:T(8,128)S(1)} custom-call(s32[128,3]{1,0:T(8,128)S(1)} %copy.19.roots, f32[1280,128]{1,0:T(8,128)S(1)} %slab.1, f32[10,8,128]{2,1,0:T(8,128)S(1)} %collective-permute-done.lo, f32[10,8,128]{2,1,0:T(8,128)S(1)} %collective-permute-done.1.hi), custom_call_target="tpu_custom_call" | custom-call | tf_op jit(solution)/shard_map/pack/pallas_call | solution.py:667
  13.1 0.0 copy-start.2
  13.1 0.0 copy-start.5
  13.1 0.0 copy-start.6
  13.1 32.5 %all_to_all.10.recv = f32[16,26,8,128]{3,2,1,0:T(8,128)S(1)} all-to-all(f32[16,26,8,128]{3,2,1,0:T(8,128)S(1)} %pack.1), channel_id=1, replica_groups=mesh['grp'=8,'dev'=16] {'dev'}, dimensions={0} | all-to-all | bytes 3407872 | tf_op jit(solution)/shard_map/all_to_all | solution.py:670
  45.6 0.0 copy-done.2
  45.7 0.0 copy-done.5
  45.7 0.0 copy-done.6
  45.7 10.3 %patch.1 = (f32[1,9,32,1024]{3,2,1,0:T(8,128)}, f32[3,10,24,128]{3,2,1,0:T(8,128)S(1)}, f32[3,16,128]{2,1,0:T(8,128)S(1)}, f32[3,16,128]{2,1,0:T(8,128)S(1)}) custom-call(s32[128,3]{1,0:T(8,128)S(1)} %copy.19.roots, f32[8,9]{1,0:T(8,128)S(1)} %copy-done.6, f32[16,26,8,128]{3,2,1,0:T(8,128)S(1)} %all_to_all.10.recv, s32[1,32,1024]{2,1,0:T(8,128)S(1)} %copy-done.5, ...), custom_call_target="tpu_custom_call" | custom-call | tf_op jit(solution)/shard_map/patch/pallas_call | solution.py:673
  56.0 1.9 %collective-permute-start.2 = (f32[3,16,128]{2,1,0:T(8,128)S(1)}, f32[3,16,128]{2,1,0:T(8,128)S(1)}, u32[]{:S(2)}, u32[]{:S(2)}) collective-permute-start(f32[3,16,128]{2,1,0:T(8,128)S(1)} %get-tuple-element.7), channel_id=1, source_target_pairs={{16,0},{32,16},{48,32},{64,48},{80,64},{96,80},{112,96},{17,1},{33... | collective-permute-start | bytes 73736 | tf_op jit(solution)/shard_map/ppermute | solution.py:690
  57.9 2.4 %collective-permute-start.3 = (f32[3,16,128]{2,1,0:T(8,128)S(1)}, f32[3,16,128]{2,1,0:T(8,128)S(1)}, u32[]{:S(2)}, u32[]{:S(2)}) collective-permute-start(f32[3,16,128]{2,1,0:T(8,128)S(1)} %get-tuple-element.8), channel_id=1, source_target_pairs={{0,16},{16,32},{32,48},{48,64},{64,80},{80,96},{96,112},{1,17},{17... | collective-permute-start | bytes 73736 | tf_op jit(solution)/shard_map/ppermute | solution.py:691
  60.3 0.0 collective-permute-done.2.above
  60.3 2.7 %collective-permute-done.3.below = f32[3,16,128]{2,1,0:T(8,128)S(1)} collective-permute-done((f32[3,16,128]{2,1,0:T(8,128)S(1)}, f32[3,16,128]{2,1,0:T(8,128)S(1)}, u32[]{:S(2)}, u32[]{:S(2)}) %collective-permute-start.3) | collective-permute-done | bytes 24608 | tf_op jit(solution)/shard_map/ppermute | solution.py:691
  63.0 3.0 %cut.1._ = f32[16,24,8,128]{3,2,1,0:T(8,128)} custom-call(s32[128,3]{1,0:T(8,128)S(1)} %copy.19.roots, f32[3,10,24,128]{3,2,1,0:T(8,128)S(1)} %get-tuple-element.6.dl, f32[3,16,128]{2,1,0:T(8,128)S(1)} %collective-permute-done.2.above, f32[3,16,128]{2,1,0:T(8,128)S(1)} %collective-permute-done.3.below), custom_call_target="tpu_custom_call" | custom-call | tf_op jit(solution)/shard_map/cut/pallas_call | solution.py:692
  66.0 0.0 copy-start.4
  66.0 0.0 copy-start.1
  66.0 3.9 %all-to-all-start.1 = ((f32[16,24,8,128]{3,2,1,0:T(8,128)}), f32[16,24,8,128]{3,2,1,0:T(8,128)S(1)}, u32[]{:S(2)}, u32[]{:S(2)}) async-start(f32[16,24,8,128]{3,2,1,0:T(8,128)} %cut.1._), calls=%async_computation.1 | async-start | bytes 3145728 | tf_op jit(solution)/shard_map/all_to_all | solution.py:701
  69.9 0.0 copy-done.4
  69.9 0.0 copy-done.1
  70.0 0.1 fusion
  70.1 3.7 %collective-permute-start.4 = (f32[10,16,128]{2,1,0:T(8,128)S(1)}, f32[10,16,128]{2,1,0:T(8,128)S(1)}, u32[]{:S(2)}, u32[]{:S(2)}) collective-permute-start(f32[10,16,128]{2,1,0:T(8,128)S(1)} %pad_maximum_fusion.1.own_hi), channel_id=1, source_target_pairs={{0,1},{1,2},{2,3},{3,4},{4,5},{5,6},{6,7},{7,8},{8,9},{9,10},{10,1... | collective-permute-start | bytes 245768 | tf_op jit(solution)/shard_map/ppermute | solution.py:652
  73.8 1.3 %collective-permute-start.5 = (f32[10,16,128]{2,1,0:T(8,128)S(1)}, f32[10,16,128]{2,1,0:T(8,128)S(1)}, u32[]{:S(2)}, u32[]{:S(2)}) collective-permute-start(f32[10,16,128]{2,1,0:T(8,128)S(1)} %pad_maximum_fusion.own_lo), channel_id=1, source_target_pairs={{1,0},{2,1},{3,2},{4,3},{5,4},{6,5},{7,6},{8,7},{9,8},{10,9},{11,1... | collective-permute-start | bytes 245768 | tf_op jit(solution)/shard_map/ppermute | solution.py:653
  75.1 0.1 copy.26
  75.2 0.1 concatenate.17.clone
  75.3 0.1 add_multiply_fusion
  75.4 0.1 mul.12
  75.5 3.3 %coarse.1.coarse_one = f32[9,16,8,128]{3,2,1,0:T(8,128)S(1)} custom-call(f32[9,16,8,128]{3,2,1,0:T(8,128)S(1)} %copy-done.1, s32[16,8,128]{2,1,0:T(8,128)S(1)} %copy-done.4, f32[10,8,128]{2,1,0:T(8,128)S(1)} %collective-permute-done.lo, f32[10,8,128]{2,1,0:T(8,128)S(1)} %collective-permute-done.1.hi, f32[9,128]{1,0:T(8,128)S(1)} %pad.5.ptab, ...), custom_call_target="tpu_custom_call" | custom-call | tf_op jit(solution)/shard_map/coarse/pallas_call | solution.py:702
  78.8 10.3 %collective-permute-done.4.ylo = f32[10,16,128]{2,1,0:T(8,128)S(1)} collective-permute-done((f32[10,16,128]{2,1,0:T(8,128)S(1)}, f32[10,16,128]{2,1,0:T(8,128)S(1)}, u32[]{:S(2)}, u32[]{:S(2)}) %collective-permute-start.4) | collective-permute-done | bytes 81952 | tf_op jit(solution)/shard_map/ppermute | solution.py:652
  89.1 1.2 %collective-permute-done.5.yhi = f32[10,16,128]{2,1,0:T(8,128)S(1)} collective-permute-done((f32[10,16,128]{2,1,0:T(8,128)S(1)}, f32[10,16,128]{2,1,0:T(8,128)S(1)}, u32[]{:S(2)}, u32[]{:S(2)}) %collective-permute-start.5) | collective-permute-done | bytes 81952 | tf_op jit(solution)/shard_map/ppermute | solution.py:653
  90.4 3.6 %all-to-all-done.1.arrived = f32[16,24,8,128]{3,2,1,0:T(8,128)S(1)} async-done(((f32[16,24,8,128]{3,2,1,0:T(8,128)}), f32[16,24,8,128]{3,2,1,0:T(8,128)S(1)}, u32[]{:S(2)}, u32[]{:S(2)}) %all-to-all-start.1) | async-done | bytes 1572896 | tf_op jit(solution)/shard_map/all_to_all | solution.py:701
  94.0 4.3 %add.64 = f32[9,16,8,128]{3,2,1,0:T(8,128)} custom-call(s32[128,3]{1,0:T(8,128)S(1)} %copy.19.roots, f32[16,24,8,128]{3,2,1,0:T(8,128)S(1)} %all-to-all-done.1.arrived, f32[9,16,8,128]{3,2,1,0:T(8,128)S(1)} %coarse.1.coarse_one, f32[10,16,128]{2,1,0:T(8,128)S(1)} %pad_maximum_fusion.own_lo, f32[10,16,128]{2,1,0:T(8,128)S(1)} %pad_maximum_fusion.1.own_hi, ...), custom_call_target="tpu_custom_call" | custom-call | tf_op jit(solution)/shard_map/add/pallas_call | solution.py:710
  (8 shorter events, 0.1 us)
Async XLA Ops:
  0.6 10.3 %copy-start.7 = (s32[128,3]{0,1:T(4,128)S(1)}, s32[128,3]{0,1:T(4,128)}, u32[]{:S(2)}) copy-start(s32[128,3]{0,1:T(4,128)} %param.9) | copy-start | bytes 4612
  2.2 8.9 %collective-permute-start = (f32[10,8,128]{2,1,0:T(8,128)S(1)}, f32[10,8,128]{2,1,0:T(8,128)S(1)}, u32[]{:S(2)}, u32[]{:S(2)}) collective-permute-start(f32[10,8,128]{2,1,0:T(8,128)S(1)} %pad_maximum_fusion.2), channel_id=1, source_target_pairs={{0,16},{16,32},{32,48},{48,64},{64,80},{80,96},{96,112},{1,17},{17... | collective-permute-start | bytes 122888 | tf_op jit(solution)/shard_map/ppermute | solution.py:648
  4.1 7.0 %collective-permute-start.1 = (f32[10,8,128]{2,1,0:T(8,128)S(1)}, f32[10,8,128]{2,1,0:T(8,128)S(1)}, u32[]{:S(2)}, u32[]{:S(2)}) collective-permute-start(f32[10,8,128]{2,1,0:T(8,128)S(1)} %pad_maximum_fusion.3), channel_id=1, source_target_pairs={{16,0},{32,16},{48,32},{64,48},{80,64},{96,80},{112,96},{17,1},{33... | collective-permute-start | bytes 122888 | tf_op jit(solution)/shard_map/ppermute | solution.py:649
  7.7 1.1 %copy-start = (f32[9,16,8,128]{3,2,1,0:T(8,128)S(1)}, f32[9,16,8,128]{3,2,1,0:T(8,128)}, u32[]{:S(2)}) copy-start(f32[9,16,8,128]{3,2,1,0:T(8,128)} %u.3) | copy-start | bytes 1769476
  8.8 0.8 copy-start.3
  13.1 32.6 %copy-start.2 = (bf16[256,1152]{1,0:T(8,128)(2,1)S(1)}, bf16[256,1152]{1,0:T(8,128)(2,1)}, u32[]{:S(2)}) copy-start(bf16[256,1152]{1,0:T(8,128)(2,1)} %constant.3.clone.tabs) | copy-start | bytes 1769476
  13.1 32.5 %copy-start.5 = (s32[1,32,1024]{2,1,0:T(8,128)S(1)}, s32[1,32,1024]{2,1,0:T(8,128)}, u32[]{:S(2)}) copy-start(s32[1,32,1024]{2,1,0:T(8,128)} %fidx.1) | copy-start | bytes 393220
  13.1 32.5 %copy-start.6 = (f32[8,9]{1,0:T(8,128)S(1)}, f32[8,9]{1,0:T(8,128)}, u32[]{:S(2)}) copy-start(f32[8,9]{1,0:T(8,128)} %table.1) | copy-start | bytes 868
  56.0 4.3 %collective-permute-start.2 = (f32[3,16,128]{2,1,0:T(8,128)S(1)}, f32[3,16,128]{2,1,0:T(8,128)S(1)}, u32[]{:S(2)}, u32[]{:S(2)}) collective-permute-start(f32[3,16,128]{2,1,0:T(8,128)S(1)} %get-tuple-element.7), channel_id=1, source_target_pairs={{16,0},{32,16},{48,32},{64,48},{80,64},{96,80},{112,96},{17,1},{33... | collective-permute-start | bytes 73736 | tf_op jit(solution)/shard_map/ppermute | solution.py:690
  57.9 5.1 %collective-permute-start.3 = (f32[3,16,128]{2,1,0:T(8,128)S(1)}, f32[3,16,128]{2,1,0:T(8,128)S(1)}, u32[]{:S(2)}, u32[]{:S(2)}) collective-permute-start(f32[3,16,128]{2,1,0:T(8,128)S(1)} %get-tuple-element.8), channel_id=1, source_target_pairs={{0,16},{16,32},{32,48},{48,64},{64,80},{80,96},{96,112},{1,17},{17... | collective-permute-start | bytes 73736 | tf_op jit(solution)/shard_map/ppermute | solution.py:691
  66.0 3.9 %copy-start.4 = (s32[16,8,128]{2,1,0:T(8,128)S(1)}, s32[16,8,128]{2,1,0:T(8,128)}, u32[]{:S(2)}) copy-start(s32[16,8,128]{2,1,0:T(8,128)} %idx.3) | copy-start | bytes 196612
  66.0 3.9 %copy-start.1 = (f32[9,16,8,128]{3,2,1,0:T(8,128)S(1)}, f32[9,16,8,128]{3,2,1,0:T(8,128)}, u32[]{:S(2)}) copy-start(f32[9,16,8,128]{3,2,1,0:T(8,128)} %u.3) | copy-start | bytes 1769476
  66.0 27.9 %all-to-all-start.1 = ((f32[16,24,8,128]{3,2,1,0:T(8,128)}), f32[16,24,8,128]{3,2,1,0:T(8,128)S(1)}, u32[]{:S(2)}, u32[]{:S(2)}) async-start(f32[16,24,8,128]{3,2,1,0:T(8,128)} %cut.1._), calls=%async_computation.1 | async-start | bytes 3145728 | tf_op jit(solution)/shard_map/all_to_all | solution.py:701
  70.1 19.1 %collective-permute-start.4 = (f32[10,16,128]{2,1,0:T(8,128)S(1)}, f32[10,16,128]{2,1,0:T(8,128)S(1)}, u32[]{:S(2)}, u32[]{:S(2)}) collective-permute-start(f32[10,16,128]{2,1,0:T(8,128)S(1)} %pad_maximum_fusion.1.own_hi), channel_id=1, source_target_pairs={{0,1},{1,2},{2,3},{3,4},{4,5},{5,6},{6,7},{7,8},{8,9},{9,10},{10,1... | collective-permute-start | bytes 245768 | tf_op jit(solution)/shard_map/ppermute | solution.py:652
  73.8 16.6 %collective-permute-start.5 = (f32[10,16,128]{2,1,0:T(8,128)S(1)}, f32[10,16,128]{2,1,0:T(8,128)S(1)}, u32[]{:S(2)}, u32[]{:S(2)}) collective-permute-start(f32[10,16,128]{2,1,0:T(8,128)S(1)} %pad_maximum_fusion.own_lo), channel_id=1, source_target_pairs={{1,0},{2,1},{3,2},{4,3},{5,4},{6,5},{7,6},{8,7},{9,8},{10,9},{11,1... | collective-permute-start | bytes 245768 | tf_op jit(solution)/shard_map/ppermute | solution.py:653

commit v5 on v4

--- a/solution.py
+++ b/solution.py
@@ -92,18 +92,11 @@
     return owner, first - 8 * owner, roots[row, 2] - 1
 
 
-def slab_kernel(u, idx, slab, ubuf, ibuf, sems):
-    copies = [pltpu.make_async_copy(u.at[s], ubuf.at[s], sems.at[s]) for s in range(S)]
-    copies.append(pltpu.make_async_copy(idx, ibuf, sems.at[S]))
-    for copy in copies:
-        copy.start()
-    for s in range(S):
-        copies[s].wait()
-        for x in range(CX):
-            slab[pl.ds(s * CX + x, 8, stride=CH * CX), :] = ubuf[s, x]
-    copies[S].wait()
+def slab_kernel(u, idx, slab):
     for x in range(CX):
-        slab[pl.ds(S * CX + x, 8, stride=CH * CX), :] = (ibuf[x] + 1).astype(F32)
+        for s in range(S):
+            slab[pl.ds(s * CX + x, 8, stride=CH * CX), :] = u[s, x]
+        slab[pl.ds(S * CX + x, 8, stride=CH * CX), :] = (idx[x] + 1).astype(F32)
 
 
 def listed(roots, slab, me, into, row):
@@ -412,8 +405,8 @@
     for t in range(3):
         dl[t] = delta[t].reshape(CH, PITCH, 128)
 
-    rows3 = 3 * PITCH
-    lane_c = lanes((rows3, 128))
+    rows9 = S * PITCH
+    lane_c = lanes((rows9, 128))
     lane24 = lanes((PITCH, 128))
     row24 = lax.broadcasted_iota(jnp.int32, (PITCH, 128), 0)
 
@@ -436,28 +429,26 @@
         wider = [within(row24, CX + 1), within(y, CX + 1), within(z, CX + 1)]
         every = lambda a, b, c: jnp.logical_and(a, jnp.logical_and(b, c))
         faces = [every(*(wider[n] if n == axis else inside[n] for n in range(3))) for axis in range(3)]
-        for i in range(3):
-            for axis in range(3):
-                mk[3 * axis + t, 24 * i : 24 * i + 24] = jnp.where(faces[axis], 0.5, 0.0)
-            mk[9 + t, 24 * i : 24 * i + 24] = jnp.where(every(*inside), 1.0, 0.0)
-
-    def coarse(i, carry):
-        u = [fr[t, pl.ds(3 * i, 3)].reshape(rows3, 128) for t in range(3)]
-        d = [fr[t, pl.ds(S + 3 * i, 3)].reshape(rows3, 128) for t in range(3)]
-        below = [[pltpu.roll(a, 1, 0) for a in v] for v in (u, d)]
-        flux = [[mk[t] * (d[t] + below[1][t]) * (u[t] - below[0][t]) for t in range(3)]]
-        for axis, step in ((1, W), (2, 1)):
-            down = [shifted_down(v, step) for v in (u, d)]
-            flux.append([mk[3 * axis + t] * (d[t] + down[1][t]) * (u[t] - down[0][t]) for t in range(3)])
-        up_y, up_z = shifted_up(flux[1], W), shifted_up(flux[2], 1)
-        for t in range(3):
-            total = pltpu.roll(flux[0][t], rows3 - 1, 0) - flux[0][t]
-            total = total + (up_y[t] - flux[1][t]) + (up_z[t] - flux[2][t])
-            old = dl[t, pl.ds(3 * i, 3)].reshape(rows3, 128)
-            dl[t, pl.ds(3 * i, 3)] = (old - (mk[9 + t] * u[t] + total)).reshape(3, PITCH, 128)
-        return carry
-
-    lax.fori_loop(0, S // 3, coarse, 0)
+        for axis in range(3):
+            mk[3 * axis + t] = jnp.where(faces[axis], 0.5, 0.0)
+        mk[9 + t] = jnp.where(every(*inside), 1.0, 0.0)
+
+    def masks_of(n):
+        return jnp.broadcast_to(mk[n][None], (S, PITCH, 128)).reshape(rows9, 128)
+
+    u = [fr[t, 0:S].reshape(rows9, 128) for t in range(3)]
+    d = [fr[t, S : 2 * S].reshape(rows9, 128) for t in range(3)]
+    below = [[pltpu.roll(a, 1, 0) for a in v] for v in (u, d)]
+    flux = [[masks_of(t) * (d[t] + below[1][t]) * (u[t] - below[0][t]) for t in range(3)]]
+    for axis, step in ((1, W), (2, 1)):
+        down = [shifted_down(v, step) for v in (u, d)]
+        flux.append([masks_of(3 * axis + t) * (d[t] + down[1][t]) * (u[t] - down[0][t]) for t in range(3)])
+    up_y, up_z = shifted_up(flux[1], W), shifted_up(flux[2], 1)
+    for t in range(3):
+        total = pltpu.roll(flux[0][t], rows9 - 1, 0) - flux[0][t]
+        total = total + (up_y[t] - flux[1][t]) + (up_z[t] - flux[2][t])
+        value = dl[t, 0:S].reshape(rows9, 128) - (masks_of(9 + t) * u[t] + total)
+        dl[t, 0:S] = value.reshape(S, PITCH, 128)
 
     for t in range(3):
         for ref, row, last in ((flo, 0, 8), (fhi, W - 1, 9)):
@@ -652,18 +643,7 @@
     y_lo = lax.ppermute(own_hi, "dev", up_d)
     y_hi = lax.ppermute(own_lo, "dev", down_d)
 
-    slab = call(
-        slab_kernel,
-        shape(CY * CH * CX, 128),
-        [ANY] * 2,
-        [
-            pltpu.VMEM((S, CX, CY, 128), F32),
-            pltpu.VMEM((CX, CY, 128), jnp.int32),
-            pltpu.SemaphoreType.DMA((CH,)),
-        ],
-        "slab",
-        8,
-    )(coarse_state, coef_index)
+    slab = call(slab_kernel, shape(CY * CH * CX, 128), [VMEM] * 2, [], "slab", 8)(coarse_state, coef_index)
     blocks = call(
         pack_kernel, shape(DEV, NF, 8, 128), [SMEM] + [VMEM] * 3, [pltpu.VMEM((8 * 24, 128), F32), pltpu.SMEM((1, DEV + 1), jnp.int32)], "pack", 8
     )(patch_root, slab, x_lo, x_hi)
@@ -681,7 +661,7 @@
             f32(8, 40, 128), f32(8, 32, 128), f32(8, 32, 128), f32(8, 32, 128), f32(8, 32, 128),
             f32(8, 32, 128), f32(8, 32, 128), f32(8, 32, 128), f32(8, 32, 128), f32(32, 128),
             f32(8, CH, PITCH, 128), f32(8, CH, PITCH, 128), f32(CH, PITCH, 128),
-            f32(12, 3 * PITCH, 128), f32(2, 32, 1024), pltpu.SemaphoreType.DMA((2,)),
+            f32(12, PITCH, 128), f32(2, 32, 1024), pltpu.SemaphoreType.DMA((2,)),
         ],
         "patch",
         32,

time: 99.7 us -> 98.6 us (0.989)
  transfers between devices with their start and end apart: 7 -> 7, of which waited for: 4 -> 4; matrix products, arithmetic and copies ran while one was open for 1% -> 1% of each run, Pallas kernels for 5% -> 4%
where the time goes in v5:
time: 98.6 us; the launch traced here: 97.3 us
  blocking collectives  32.6 us (33%)
  Pallas kernels  23.9 us (24%)
  starting transfers between devices  18.7 us (19%)
  waiting for transfers between devices  17.1 us (17%)
  local copies, waits for them, and re-layouts  3.2 us (3%)
    all_to_all x1, blocking collectives, body(): lax.all_to_all(blocks, 'dev', split_axis=0, concat_axis=0, tiled=True)  32.6 us
    pallas_call x1, Pallas kernels, body(): call(patch_kernel, (shape(1, S, 32, 1024), shape(3, CH, PITCH, 128), shap...  9.76 us
    ppermute x1, waiting for transfers between devices, body(): y_lo = lax.ppermute(own_hi, 'dev', up_d)  9.41 us
    pallas_call x1, Pallas kernels, body(): call(add_kernel, shape(S, CX, CY, 128), [SMEM] + [VMEM] * 7, [f32(S, CX,...  4.93 us
    all_to_all x1, starting transfers between devices, body(): lax.all_to_all(corrections, 'dev', split_axis=0, concat_axis=0, tiled=True)  3.85 us
    ppermute x1, starting transfers between devices, body(): y_lo = lax.ppermute(own_hi, 'dev', up_d)  3.71 us
    ppermute x1, starting transfers between devices, body(): x_hi = lax.ppermute(plane(coarse_state[:, 0], coef_index[0]), 'grp', down_g)  3.64 us
    pallas_call x1, Pallas kernels, body(): call(coarse_kernel, shape(S, CX, CY, 128), [VMEM] * 5 + [ANY], [i32(CX +...  3.32 us
  transfers between devices with their start and end apart: 7, of which 4 were waited for; matrix products, arithmetic and copies ran while one was open for 1% of the time, Pallas kernels for 4%

profile of v5, /device:TPU:32, one launch (start us, length us, event | category | flops | bytes accessed | tf_op | source)
XLA Modules:
  0.0 97.3 jit_solution(4608325006789547158)
XLA Ops:
  0.6 0.0 copy-start.7
  0.6 0.8 slice_bitcast_fusion
  1.4 0.7 add_convert_fusion
  2.2 1.9 %collective-permute-start = (f32[10,8,128]{2,1,0:T(8,128)S(1)}, f32[10,8,128]{2,1,0:T(8,128)S(1)}, u32[]{:S(2)}, u32[]{:S(2)}) collective-permute-start(f32[10,8,128]{2,1,0:T(8,128)S(1)} %pad_maximum_fusion.2), channel_id=1, source_target_pairs={{0,16},{16,32},{32,48},{48,64},{64,80},{80,96},{96,112},{1,17},{17... | collective-permute-start | bytes 122888 | tf_op jit(solution)/shard_map/ppermute | solution.py:639
  4.1 3.6 %collective-permute-start.1 = (f32[10,8,128]{2,1,0:T(8,128)S(1)}, f32[10,8,128]{2,1,0:T(8,128)S(1)}, u32[]{:S(2)}, u32[]{:S(2)}) collective-permute-start(f32[10,8,128]{2,1,0:T(8,128)S(1)} %pad_maximum_fusion.3), channel_id=1, source_target_pairs={{16,0},{32,16},{48,32},{64,48},{80,64},{96,80},{112,96},{17,1},{33... | collective-permute-start | bytes 122888 | tf_op jit(solution)/shard_map/ppermute | solution.py:640
  7.7 0.0 copy-start
  7.7 1.1 %copy-done = f32[9,16,8,128]{3,2,1,0:T(8,128)S(1)} copy-done((f32[9,16,8,128]{3,2,1,0:T(8,128)S(1)}, f32[9,16,8,128]{3,2,1,0:T(8,128)}, u32[]{:S(2)}) %copy-start) | copy-done | bytes 589848
  8.8 0.0 copy-start.3
  8.8 0.8 copy-done.3
  9.6 0.4 slab.1
  10.1 0.0 copy-done.7
  10.1 0.1 copy.19.roots
  10.2 0.0 collective-permute-done.lo
  10.2 0.0 collective-permute-done.1.hi
  10.2 2.6 %pack.1 = f32[16,26,8,128]{3,2,1,0:T(8,128)S(1)} custom-call(s32[128,3]{1,0:T(8,128)S(1)} %copy.19.roots, f32[1280,128]{1,0:T(8,128)S(1)} %slab.1, f32[10,8,128]{2,1,0:T(8,128)S(1)} %collective-permute-done.lo, f32[10,8,128]{2,1,0:T(8,128)S(1)} %collective-permute-done.1.hi), custom_call_target="tpu_custom_call" | custom-call | tf_op jit(solution)/shard_map/pack/pallas_call | solution.py:647
  12.8 0.0 copy-start.2
  12.8 0.0 copy-start.5
  12.8 0.0 copy-start.6
  12.8 32.6 %all_to_all.10.recv = f32[16,26,8,128]{3,2,1,0:T(8,128)S(1)} all-to-all(f32[16,26,8,128]{3,2,1,0:T(8,128)S(1)} %pack.1), channel_id=1, replica_groups=mesh['grp'=8,'dev'=16] {'dev'}, dimensions={0} | all-to-all | bytes 3407872 | tf_op jit(solution)/shard_map/all_to_all | solution.py:650
  45.4 0.0 copy-done.2
  45.4 0.0 copy-done.5
  45.4 0.0 copy-done.6
  45.4 9.8 %patch.1 = (f32[1,9,32,1024]{3,2,1,0:T(8,128)}, f32[3,10,24,128]{3,2,1,0:T(8,128)S(1)}, f32[3,16,128]{2,1,0:T(8,128)S(1)}, f32[3,16,128]{2,1,0:T(8,128)S(1)}) custom-call(s32[128,3]{1,0:T(8,128)S(1)} %copy.19.roots, f32[8,9]{1,0:T(8,128)S(1)} %copy-done.6, f32[16,26,8,128]{3,2,1,0:T(8,128)S(1)} %all_to_all.10.recv, s32[1,32,1024]{2,1,0:T(8,128)S(1)} %copy-done.5, ...), custom_call_target="tpu_custom_call" | custom-call | tf_op jit(solution)/shard_map/patch/pallas_call | solution.py:653
  55.2 1.9 %collective-permute-start.2 = (f32[3,16,128]{2,1,0:T(8,128)S(1)}, f32[3,16,128]{2,1,0:T(8,128)S(1)}, u32[]{:S(2)}, u32[]{:S(2)}) collective-permute-start(f32[3,16,128]{2,1,0:T(8,128)S(1)} %get-tuple-element.7), channel_id=1, source_target_pairs={{16,0},{32,16},{48,32},{64,48},{80,64},{96,80},{112,96},{17,1},{33... | collective-permute-start | bytes 73736 | tf_op jit(solution)/shard_map/ppermute | solution.py:670
  57.1 2.4 %collective-permute-start.3 = (f32[3,16,128]{2,1,0:T(8,128)S(1)}, f32[3,16,128]{2,1,0:T(8,128)S(1)}, u32[]{:S(2)}, u32[]{:S(2)}) collective-permute-start(f32[3,16,128]{2,1,0:T(8,128)S(1)} %get-tuple-element.8), channel_id=1, source_target_pairs={{0,16},{16,32},{32,48},{48,64},{64,80},{80,96},{96,112},{1,17},{17... | collective-permute-start | bytes 73736 | tf_op jit(solution)/shard_map/ppermute | solution.py:671
  59.5 0.0 collective-permute-done.2.above
  59.6 2.7 %collective-permute-done.3.below = f32[3,16,128]{2,1,0:T(8,128)S(1)} collective-permute-done((f32[3,16,128]{2,1,0:T(8,128)S(1)}, f32[3,16,128]{2,1,0:T(8,128)S(1)}, u32[]{:S(2)}, u32[]{:S(2)}) %collective-permute-start.3) | collective-permute-done | bytes 24608 | tf_op jit(solution)/shard_map/ppermute | solution.py:671
  62.3 2.9 %cut.1._ = f32[16,24,8,128]{3,2,1,0:T(8,128)} custom-call(s32[128,3]{1,0:T(8,128)S(1)} %copy.19.roots, f32[3,10,24,128]{3,2,1,0:T(8,128)S(1)} %get-tuple-element.6.dl, f32[3,16,128]{2,1,0:T(8,128)S(1)} %collective-permute-done.2.above, f32[3,16,128]{2,1,0:T(8,128)S(1)} %collective-permute-done.3.below), custom_call_target="tpu_custom_call" | custom-call | tf_op jit(solution)/shard_map/cut/pallas_call | solution.py:672
  65.2 0.0 copy-start.4
  65.2 0.0 copy-start.1
  65.2 3.9 %all-to-all-start.1 = ((f32[16,24,8,128]{3,2,1,0:T(8,128)}), f32[16,24,8,128]{3,2,1,0:T(8,128)S(1)}, u32[]{:S(2)}, u32[]{:S(2)}) async-start(f32[16,24,8,128]{3,2,1,0:T(8,128)} %cut.1._), calls=%async_computation.1 | async-start | bytes 3145728 | tf_op jit(solution)/shard_map/all_to_all | solution.py:681
  69.1 0.0 copy-done.4
  69.1 0.0 copy-done.1
  69.1 0.1 fusion
  69.2 3.7 %collective-permute-start.4 = (f32[10,16,128]{2,1,0:T(8,128)S(1)}, f32[10,16,128]{2,1,0:T(8,128)S(1)}, u32[]{:S(2)}, u32[]{:S(2)}) collective-permute-start(f32[10,16,128]{2,1,0:T(8,128)S(1)} %pad_maximum_fusion.1.own_hi), channel_id=1, source_target_pairs={{0,1},{1,2},{2,3},{3,4},{4,5},{5,6},{6,7},{7,8},{8,9},{9,10},{10,1... | collective-permute-start | bytes 245768 | tf_op jit(solution)/shard_map/ppermute | solution.py:643
  73.0 1.3 %collective-permute-start.5 = (f32[10,16,128]{2,1,0:T(8,128)S(1)}, f32[10,16,128]{2,1,0:T(8,128)S(1)}, u32[]{:S(2)}, u32[]{:S(2)}) collective-permute-start(f32[10,16,128]{2,1,0:T(8,128)S(1)} %pad_maximum_fusion.own_lo), channel_id=1, source_target_pairs={{1,0},{2,1},{3,2},{4,3},{5,4},{6,5},{7,6},{8,7},{9,8},{10,9},{11,1... | collective-permute-start | bytes 245768 | tf_op jit(solution)/shard_map/ppermute | solution.py:644
  74.3 0.1 copy.26
  74.4 0.1 concatenate.17.clone
  74.4 0.1 add_multiply_fusion
  74.5 0.1 mul.12
  74.6 3.3 %coarse.1.coarse_one = f32[9,16,8,128]{3,2,1,0:T(8,128)S(1)} custom-call(f32[9,16,8,128]{3,2,1,0:T(8,128)S(1)} %copy-done.1, s32[16,8,128]{2,1,0:T(8,128)S(1)} %copy-done.4, f32[10,8,128]{2,1,0:T(8,128)S(1)} %collective-permute-done.lo, f32[10,8,128]{2,1,0:T(8,128)S(1)} %collective-permute-done.1.hi, f32[9,128]{1,0:T(8,128)S(1)} %pad.5.ptab, ...), custom_call_target="tpu_custom_call" | custom-call | tf_op jit(solution)/shard_map/coarse/pallas_call | solution.py:682
  78.0 9.4 %collective-permute-done.4.ylo = f32[10,16,128]{2,1,0:T(8,128)S(1)} collective-permute-done((f32[10,16,128]{2,1,0:T(8,128)S(1)}, f32[10,16,128]{2,1,0:T(8,128)S(1)}, u32[]{:S(2)}, u32[]{:S(2)}) %collective-permute-start.4) | collective-permute-done | bytes 81952 | tf_op jit(solution)/shard_map/ppermute | solution.py:643
  87.4 2.1 %collective-permute-done.5.yhi = f32[10,16,128]{2,1,0:T(8,128)S(1)} collective-permute-done((f32[10,16,128]{2,1,0:T(8,128)S(1)}, f32[10,16,128]{2,1,0:T(8,128)S(1)}, u32[]{:S(2)}, u32[]{:S(2)}) %collective-permute-start.5) | collective-permute-done | bytes 81952 | tf_op jit(solution)/shard_map/ppermute | solution.py:644
  89.5 2.8 %all-to-all-done.1.arrived = f32[16,24,8,128]{3,2,1,0:T(8,128)S(1)} async-done(((f32[16,24,8,128]{3,2,1,0:T(8,128)}), f32[16,24,8,128]{3,2,1,0:T(8,128)S(1)}, u32[]{:S(2)}, u32[]{:S(2)}) %all-to-all-start.1) | async-done | bytes 1572896 | tf_op jit(solution)/shard_map/all_to_all | solution.py:681
  92.3 4.9 %add.64 = f32[9,16,8,128]{3,2,1,0:T(8,128)} custom-call(s32[128,3]{1,0:T(8,128)S(1)} %copy.19.roots, f32[16,24,8,128]{3,2,1,0:T(8,128)S(1)} %all-to-all-done.1.arrived, f32[9,16,8,128]{3,2,1,0:T(8,128)S(1)} %coarse.1.coarse_one, f32[10,16,128]{2,1,0:T(8,128)S(1)} %pad_maximum_fusion.own_lo, f32[10,16,128]{2,1,0:T(8,128)S(1)} %pad_maximum_fusion.1.own_hi, ...), custom_call_target="tpu_custom_call" | custom-call | tf_op jit(solution)/shard_map/add/pallas_call | solution.py:690
  (8 shorter events, 0.1 us)
Async XLA Ops:
  0.6 9.5 %copy-start.7 = (s32[128,3]{0,1:T(4,128)S(1)}, s32[128,3]{0,1:T(4,128)}, u32[]{:S(2)}) copy-start(s32[128,3]{0,1:T(4,128)} %param.9) | copy-start | bytes 4612
  2.2 8.1 %collective-permute-start = (f32[10,8,128]{2,1,0:T(8,128)S(1)}, f32[10,8,128]{2,1,0:T(8,128)S(1)}, u32[]{:S(2)}, u32[]{:S(2)}) collective-permute-start(f32[10,8,128]{2,1,0:T(8,128)S(1)} %pad_maximum_fusion.2), channel_id=1, source_target_pairs={{0,16},{16,32},{32,48},{48,64},{64,80},{80,96},{96,112},{1,17},{17... | collective-permute-start | bytes 122888 | tf_op jit(solution)/shard_map/ppermute | solution.py:639
  4.1 6.1 %collective-permute-start.1 = (f32[10,8,128]{2,1,0:T(8,128)S(1)}, f32[10,8,128]{2,1,0:T(8,128)S(1)}, u32[]{:S(2)}, u32[]{:S(2)}) collective-permute-start(f32[10,8,128]{2,1,0:T(8,128)S(1)} %pad_maximum_fusion.3), channel_id=1, source_target_pairs={{16,0},{32,16},{48,32},{64,48},{80,64},{96,80},{112,96},{17,1},{33... | collective-permute-start | bytes 122888 | tf_op jit(solution)/shard_map/ppermute | solution.py:640
  7.7 1.1 %copy-start = (f32[9,16,8,128]{3,2,1,0:T(8,128)S(1)}, f32[9,16,8,128]{3,2,1,0:T(8,128)}, u32[]{:S(2)}) copy-start(f32[9,16,8,128]{3,2,1,0:T(8,128)} %u.3) | copy-start | bytes 1769476
  8.8 0.8 copy-start.3
  12.8 32.6 %copy-start.2 = (bf16[256,1152]{1,0:T(8,128)(2,1)S(1)}, bf16[256,1152]{1,0:T(8,128)(2,1)}, u32[]{:S(2)}) copy-start(bf16[256,1152]{1,0:T(8,128)(2,1)} %constant.3.clone.tabs) | copy-start | bytes 1769476
  12.8 32.6 %copy-start.5 = (s32[1,32,1024]{2,1,0:T(8,128)S(1)}, s32[1,32,1024]{2,1,0:T(8,128)}, u32[]{:S(2)}) copy-start(s32[1,32,1024]{2,1,0:T(8,128)} %fidx.1) | copy-start | bytes 393220
  12.8 32.6 %copy-start.6 = (f32[8,9]{1,0:T(8,128)S(1)}, f32[8,9]{1,0:T(8,128)}, u32[]{:S(2)}) copy-start(f32[8,9]{1,0:T(8,128)} %table.1) | copy-start | bytes 868
  55.2 4.3 %collective-permute-start.2 = (f32[3,16,128]{2,1,0:T(8,128)S(1)}, f32[3,16,128]{2,1,0:T(8,128)S(1)}, u32[]{:S(2)}, u32[]{:S(2)}) collective-permute-start(f32[3,16,128]{2,1,0:T(8,128)S(1)} %get-tuple-element.7), channel_id=1, source_target_pairs={{16,0},{32,16},{48,32},{64,48},{80,64},{96,80},{112,96},{17,1},{33... | collective-permute-start | bytes 73736 | tf_op jit(solution)/shard_map/ppermute | solution.py:670
  57.1 5.1 %collective-permute-start.3 = (f32[3,16,128]{2,1,0:T(8,128)S(1)}, f32[3,16,128]{2,1,0:T(8,128)S(1)}, u32[]{:S(2)}, u32[]{:S(2)}) collective-permute-start(f32[3,16,128]{2,1,0:T(8,128)S(1)} %get-tuple-element.8), channel_id=1, source_target_pairs={{0,16},{16,32},{32,48},{48,64},{64,80},{80,96},{96,112},{1,17},{17... | collective-permute-start | bytes 73736 | tf_op jit(solution)/shard_map/ppermute | solution.py:671
  65.2 3.9 %copy-start.4 = (s32[16,8,128]{2,1,0:T(8,128)S(1)}, s32[16,8,128]{2,1,0:T(8,128)}, u32[]{:S(2)}) copy-start(s32[16,8,128]{2,1,0:T(8,128)} %idx.3) | copy-start | bytes 196612
  65.2 3.9 %copy-start.1 = (f32[9,16,8,128]{3,2,1,0:T(8,128)S(1)}, f32[9,16,8,128]{3,2,1,0:T(8,128)}, u32[]{:S(2)}) copy-start(f32[9,16,8,128]{3,2,1,0:T(8,128)} %u.3) | copy-start | bytes 1769476
  65.2 27.1 %all-to-all-start.1 = ((f32[16,24,8,128]{3,2,1,0:T(8,128)}), f32[16,24,8,128]{3,2,1,0:T(8,128)S(1)}, u32[]{:S(2)}, u32[]{:S(2)}) async-start(f32[16,24,8,128]{3,2,1,0:T(8,128)} %cut.1._), calls=%async_computation.1 | async-start | bytes 3145728 | tf_op jit(solution)/shard_map/all_to_all | solution.py:681
  69.2 18.1 %collective-permute-start.4 = (f32[10,16,128]{2,1,0:T(8,128)S(1)}, f32[10,16,128]{2,1,0:T(8,128)S(1)}, u32[]{:S(2)}, u32[]{:S(2)}) collective-permute-start(f32[10,16,128]{2,1,0:T(8,128)S(1)} %pad_maximum_fusion.1.own_hi), channel_id=1, source_target_pairs={{0,1},{1,2},{2,3},{3,4},{4,5},{5,6},{6,7},{7,8},{8,9},{9,10},{10,1... | collective-permute-start | bytes 245768 | tf_op jit(solution)/shard_map/ppermute | solution.py:643
  73.0 16.5 %collective-permute-start.5 = (f32[10,16,128]{2,1,0:T(8,128)S(1)}, f32[10,16,128]{2,1,0:T(8,128)S(1)}, u32[]{:S(2)}, u32[]{:S(2)}) collective-permute-start(f32[10,16,128]{2,1,0:T(8,128)S(1)} %pad_maximum_fusion.own_lo), channel_id=1, source_target_pairs={{1,0},{2,1},{3,2},{4,3},{5,4},{6,5},{7,6},{8,7},{9,8},{10,9},{11,1... | collective-permute-start | bytes 245768 | tf_op jit(solution)/shard_map/ppermute | solution.py:644
